TPU v7x, 128 devices: a whole 4x4x4 slice. The times are simulated.
128 devices in a mesh: row: 8 (over x_hi, z), col: 16 (over y, x_lo, core).
Axes of the slice: x: 4 (x_hi: 2, x_lo: 2; x = x_hi * 2 + x_lo), y: 4, z: 4, core: 2. Of those that a mesh axis runs over, the one named last changes fastest.
Arguments:
- root_front: float32 [8192, 8192], P('row', 'col'), may hold values from -0.03314563 to 10.033146, as said below
- contrib: float32 [16384, 4096], P('row', 'col'), may hold values from -0.046875 to 0.046875, as said below
- index_map: int32 [4, 4096], replicated, may hold values from 0 to 8191, as said below
Outputs:
- factored: float32 [8192, 8192], P('row', 'col')
Inputs may be any that keep to these rules, and one draw needn't show every extreme that they name: `index_map`: each child's list is strictly increasing, and exactly 256 of its entries lie in each range [j * 512, (j + 1) * 512). `root_front`: Symmetric, and positive definite after the children's blocks are added. `contrib`: each child's update matrix is symmetric.
All inputs are finite; a program needn't handle non-finite values.
Results may differ from a plain program's by a relative error of at most 0.0001.
Values sent between devices are 32-bit elements; how exact they have to be, the bound alone decides.
No kernel may reach another device: no remote copies, remote signals or barrier semaphores. Data moves between devices by JAX's collectives and lax.ppermute only.
A program may use at most 128 MiB of HBM per device.

v0:
```python
import jax
import jax.numpy as jnp
from jax import lax
from jax.sharding import PartitionSpec as P

CB = 4096
NKIDS = 4
BLOCK = 512
PANELS = 3


def from_root(block, axis, owner):
    block = jnp.where(lax.axis_index(axis) == owner, block, jnp.zeros_like(block))
    return lax.psum(block, axis)


def body(root_front, contrib, index_map):
    row_count = lax.axis_size("row")
    col_count = lax.axis_size("col")
    my_row = lax.axis_index("row")
    my_col = lax.axis_index("col")
    rows_loc, cols_loc = root_front.shape
    kid_group = row_count // NKIDS
    per_owner = CB // row_count
    kid_cols = contrib.shape[1]
    cyc_rows = contrib.shape[0] // row_count
    col_map = (
        lax.dynamic_slice(index_map, (0, my_col * kid_cols), (NKIDS, kid_cols)) - my_col * cols_loc
    )
    row_map = (
        lax.dynamic_slice(index_map, (0, my_row * per_owner), (NKIDS, per_owner))
        - my_row * rows_loc
    )
    row_index = row_map.reshape(row_count, cyc_rows)
    outgoing = contrib.reshape(row_count, cyc_rows, kid_cols)
    own_cols = lax.dynamic_index_in_dim(col_map, my_row // kid_group, 0, keepdims=False)
    widened = (
        jnp.zeros((row_count, cyc_rows, cols_loc), jnp.float32).at[:, :, own_cols].set(outgoing)
    )
    arrived = lax.all_to_all(widened, "row", split_axis=0, concat_axis=0, tiled=True)
    assembled = root_front.at[row_index.reshape(-1)].add(
        arrived.reshape(row_count * cyc_rows, cols_loc)
    )
    global_rows = my_row * rows_loc + jnp.arange(rows_loc)
    global_cols = my_col * cols_loc + jnp.arange(cols_loc)
    col_ratio = col_count // row_count
    for panel_step in range(PANELS):
        col_start = panel_step * BLOCK
        own_col = col_start // cols_loc
        own_row = col_start // rows_loc
        col_off = col_start % cols_loc
        row_off = col_start % rows_loc
        local_cols = assembled
        panel_rows = from_root(local_cols, "col", own_col)
        pivot_part = lax.slice_in_dim(panel_rows, row_off, row_off + BLOCK, axis=0)
        pivot_block = from_root(pivot_part, "row", own_row)
        pivot_factor = jnp.linalg.cholesky(pivot_block)
        solved = lax.linalg.triangular_solve(
            pivot_factor, panel_rows, left_side=False, lower=True, transpose_a=True
        )
        is_below = (global_rows >= col_start + BLOCK)[:, None]
        trailing = jnp.where(is_below, solved, 0.0)
        with_pivot = lax.dynamic_update_slice(trailing, pivot_factor, (row_off, 0))
        factor_cols = jnp.where(my_row == own_row, with_pivot, trailing)
        own_share = lax.dynamic_slice_in_dim(trailing, my_col % col_ratio * cols_loc, cols_loc, 0)
        partner_rows = from_root(own_share, "row", my_col // col_ratio)
        assembled = assembled - jnp.dot(
            trailing,
            partner_rows.T,
            precision=lax.Precision.HIGHEST,
            preferred_element_type=jnp.float32,
        )
        current = assembled
        assembled = jnp.where(my_col == own_col, factor_cols, current)
        pivot_rows = lax.slice_in_dim(assembled, row_off, row_off + BLOCK, axis=0)
        to_clear = (my_row == own_row) & (global_cols >= col_start + BLOCK)[None, :]
        assembled = lax.dynamic_update_slice(
            assembled, jnp.where(to_clear, 0.0, pivot_rows), (row_off, 0)
        )
    return assembled


def solution(mesh):
    placed = (P("row", "col"), P("row", "col"), P())
    return jax.shard_map(
        body, mesh=mesh, in_specs=placed, out_specs=P("row", "col"), check_vma=False
    )
```

profile of v0, /device:TPU:7, one launch (start us, length us, event | category | flops | bytes accessed | tf_op | source)
XLA Modules:
  0.0 1531.8 jit_solution(2470952183670806186)
XLA Ops:
  11.7 26.5 %scatter_fusion = f32[8,256,512]{1,0,2:T(8,128)} fusion(f32[8,256,512]{1,0,2:T(8,128)} %broadcast_in_dim.59, s32[256]{0:T(256)S(1)} %bitcast.175, f32[256,8,256]{2,1,0:T(8,128)S(1)} %bitcast.171), kind=kCustom, calls=%fused_computation | custom fusion | bytes 6292480 | tf_op jit(solution)/shard_map/scatter | solution.py:38
  38.2 5.5 copy.119
  43.7 7.7 all-to-all-start
  52.2 47.7 %all-to-all-done = f32[8,256,512]{1,2,0:T(8,128)} async-done(((f32[8,256,512]{1,2,0:T(8,128)}), f32[8,256,512]{1,2,0:T(8,128)}, u32[]{:S(2)}, u32[]{:S(2)}) %all-to-all-start) | async-done | bytes 4194336 | tf_op jit(solution)/shard_map/all_to_all | solution.py:40
  99.9 5.5 copy.120
  105.4 14.0 scatter_fusion.1
  122.8 121.3 %all-reduce.11.cloned.1.call-done = f32[1024,512]{0,1:T(8,128)} async-done(((f32[1024,512]{0,1:T(8,128)}), f32[1024,512]{0,1:T(8,128)}) %all-reduce.11.cloned.1.call-update) | async-done | bytes 2097168 | tf_op jit(solution)/shard_map/psum | solution.py:14
  247.0 84.5 %all-reduce.13.cloned.1.call-done = f32[512,512]{0,1:T(8,128)} async-done(((f32[512,512]{0,1:T(8,128)}), f32[512,512]{0,1:T(8,128)}) %all-reduce.13.cloned.1.call-update) | async-done | bytes 1048592 | tf_op jit(solution)/shard_map/psum | solution.py:14
  333.4 11.7 cholesky.374
  345.2 9.8 custom-call.31
  355.7 11.7 cholesky.393
  367.7 10.0 custom-call.32
  378.8 11.7 cholesky.414
  390.7 9.8 custom-call.33
  401.3 12.1 cholesky.431
  419.0 11.5 while.6
  431.3 40.1 %custom-call.34 = f32[4,128,128]{1,2,0:T(8,128)S(1)} custom-call(f32[4,128,128]{2,1,0:T(8,128)} %copy-done.14), custom_call_target="InvertDiagBlocksLowerTriangular" | custom-call | tf_op jit(solution)/shard_map/triangular_solve/custom-call.3 | solution.py:58
  481.4 3.3 dynamic-slice_select_fusion.2
  484.8 85.9 %all-reduce.15.cloned.1.call-done = f32[512,512]{0,1:T(8,128)} async-done(((f32[512,512]{0,1:T(8,128)}), f32[512,512]{0,1:T(8,128)}) %all-reduce.15.cloned.1.call-update) | async-done | bytes 1048592 | tf_op jit(solution)/shard_map/psum | solution.py:14
  570.7 6.1 subtract_select_fusion.2
  578.6 126.3 %all-reduce.17.cloned.1.call-done = f32[1024,512]{0,1:T(8,128)} async-done(((f32[1024,512]{0,1:T(8,128)}), f32[1024,512]{0,1:T(8,128)}) %all-reduce.17.cloned.1.call-update) | async-done | bytes 2097168 | tf_op jit(solution)/shard_map/psum | solution.py:14
  707.5 84.8 %all-reduce.19.cloned.1.call-done = f32[512,512]{0,1:T(8,128)} async-done(((f32[512,512]{0,1:T(8,128)}), f32[512,512]{0,1:T(8,128)}) %all-reduce.19.cloned.1.call-update) | async-done | bytes 1048592 | tf_op jit(solution)/shard_map/psum | solution.py:14
  797.3 11.7 cholesky.446
  809.1 9.8 custom-call.35
  821.4 11.7 cholesky.465
  834.7 10.8 custom-call.36
  850.0 11.7 cholesky.486
  861.9 9.8 custom-call.37
  873.3 11.9 cholesky.503
  891.6 11.8 while.7
  904.1 40.1 %custom-call.38 = f32[4,128,128]{1,2,0:T(8,128)S(1)} custom-call(f32[4,128,128]{2,1,0:T(8,128)} %copy-done.15), custom_call_target="InvertDiagBlocksLowerTriangular" | custom-call | tf_op jit(solution)/shard_map/triangular_solve/custom-call.3 | solution.py:58
  955.1 3.3 dynamic-slice_select_fusion.1
  958.5 85.9 %all-reduce.21.cloned.1.call-done = f32[512,512]{0,1:T(8,128)} async-done(((f32[512,512]{0,1:T(8,128)}), f32[512,512]{0,1:T(8,128)}) %all-reduce.21.cloned.1.call-update) | async-done | bytes 1048592 | tf_op jit(solution)/shard_map/psum | solution.py:14
  1044.4 5.5 subtract_select_fusion.1
  1053.1 126.3 %all-reduce.23.cloned.1.call-done = f32[1024,512]{0,1:T(8,128)} async-done(((f32[1024,512]{0,1:T(8,128)}), f32[1024,512]{0,1:T(8,128)}) %all-reduce.23.cloned.1.call-update) | async-done | bytes 2097168 | tf_op jit(solution)/shard_map/psum | solution.py:14
  1182.2 84.6 %all-reduce.25.cloned.1.call-done = f32[512,512]{0,1:T(8,128)} async-done(((f32[512,512]{0,1:T(8,128)}), f32[512,512]{0,1:T(8,128)}) %all-reduce.25.cloned.1.call-update) | async-done | bytes 1048592 | tf_op jit(solution)/shard_map/psum | solution.py:14
  1268.7 11.7 cholesky.518
  1280.5 9.8 custom-call.39
  1290.9 11.7 cholesky.537
  1303.0 10.0 custom-call.40
  1315.0 11.7 cholesky.558
  1326.9 9.8 custom-call.41
  1338.3 11.7 cholesky.575
  1357.2 14.8 while.8
  1372.0 40.3 %custom-call.42 = f32[4,128,128]{1,2,0:T(8,128)S(1)} custom-call(f32[4,128,128]{2,1,0:T(8,128)} %get-tuple-element.29), custom_call_target="InvertDiagBlocksLowerTriangular" | custom-call | tf_op jit(solution)/shard_map/triangular_solve/custom-call.3 | solution.py:58
  1423.6 3.4 dynamic-slice_select_fusion
  1427.0 86.0 %all-reduce.27.cloned.1.call-done = f32[512,512]{0,1:T(8,128)} async-done(((f32[512,512]{0,1:T(8,128)}), f32[512,512]{0,1:T(8,128)}) %all-reduce.27.cloned.1.call-update) | async-done | bytes 1048592 | tf_op jit(solution)/shard_map/psum | solution.py:14
  1513.0 6.8 subtract_select_fusion
  (254 shorter events, 137.4 us)
Async XLA Ops:
  43.7 56.1 %all-to-all-start = ((f32[8,256,512]{1,2,0:T(8,128)}), f32[8,256,512]{1,2,0:T(8,128)}, u32[]{:S(2)}, u32[]{:S(2)}) async-start(f32[8,256,512]{1,2,0:T(8,128)} %copy.119), calls=%async_computation | async-start | bytes 8388608 | tf_op jit(solution)/shard_map/all_to_all | solution.py:40
  51.4 192.7 %all-reduce.11.cloned.1.call-start = ((), (), s32[]{:S(2)}) async-start(), calls=%async_computation.1 | async-start | bytes 4194304 | tf_op jit(solution)/shard_map/psum | solution.py:14
  99.9 5.5 copy-start
  122.8 208.7 %all-reduce.13.cloned.1.call-start = ((), (), s32[]{:S(2)}) async-start(), calls=%async_computation.2 | async-start | bytes 2097152 | tf_op jit(solution)/shard_map/psum | solution.py:14
  246.5 324.2 %all-reduce.15.cloned.1.call-start = ((), (), s32[]{:S(2)}) async-start(), calls=%async_computation.3 | async-start | bytes 2097152 | tf_op jit(solution)/shard_map/psum | solution.py:14
  331.5 1.7 copy-start.9
  417.9 53.5 %copy-start.6 = (f32[1024,512]{0,1:T(8,128)S(1)}, f32[1024,512]{0,1:T(8,128)}, u32[]{:S(2)}) copy-start(f32[1024,512]{0,1:T(8,128)} %all-reduce.11.cloned.1.call-done) | copy-start | bytes 6291460
  430.5 0.7 copy-start.14
  479.4 2.0 copy-start.5
  484.7 220.2 %all-reduce.17.cloned.1.call-start = ((), (), s32[]{:S(2)}) async-start(), calls=%async_computation.4 | async-start | bytes 4194304 | tf_op jit(solution)/shard_map/psum | solution.py:14
  578.6 213.7 %all-reduce.19.cloned.1.call-start = ((), (), s32[]{:S(2)}) async-start(), calls=%async_computation.5 | async-start | bytes 2097152 | tf_op jit(solution)/shard_map/psum | solution.py:14
  707.2 337.2 %all-reduce.21.cloned.1.call-start = ((), (), s32[]{:S(2)}) async-start(), calls=%async_computation.6 | async-start | bytes 2097152 | tf_op jit(solution)/shard_map/psum | solution.py:14
  792.2 2.6 copy-start.10
  796.3 1.0 copy-start.12
  903.4 0.7 copy-start.15
  944.3 4.2 copy-start.8
  953.8 4.6 copy-start.3
  958.4 221.0 %all-reduce.23.cloned.1.call-start = ((), (), s32[]{:S(2)}) async-start(), calls=%async_computation.7 | async-start | bytes 4194304 | tf_op jit(solution)/shard_map/psum | solution.py:14
  1050.2 1.4 copy-start.1
  1053.1 213.7 %all-reduce.25.cloned.1.call-start = ((), (), s32[]{:S(2)}) async-start(), calls=%async_computation.8 | async-start | bytes 2097152 | tf_op jit(solution)/shard_map/psum | solution.py:14
  1181.7 331.3 %all-reduce.27.cloned.1.call-start = ((), (), s32[]{:S(2)}) async-start(), calls=%async_computation.9 | async-start | bytes 2097152 | tf_op jit(solution)/shard_map/psum | solution.py:14
  1266.8 1.7 copy-start.11
  1268.7 34.4 %copy-start.13 = (f32[512,512]{1,0:T(8,128)}, f32[512,512]{1,0:T(8,128)S(1)}, u32[]{:S(2)}) copy-start(f32[512,512]{1,0:T(8,128)S(1)} %fusion.42) | copy-start | bytes 3145732
  1372.0 44.3 %copy-start.7 = (f32[1024,512]{0,1:T(8,128)S(1)}, f32[1024,512]{0,1:T(8,128)}, u32[]{:S(2)}) copy-start(f32[1024,512]{0,1:T(8,128)} %all-reduce.23.cloned.1.call-done) | copy-start | bytes 6291460
  1421.6 2.0 copy-start.4
  1423.6 89.4 %copy-start.2 = (f32[1024,512]{0,1:T(8,128)S(1)}, f32[1024,512]{0,1:T(8,128)}, u32[]{:S(2)}) copy-start(f32[1024,512]{0,1:T(8,128)} %copy-done.1) | copy-start | bytes 6291460
Sparse Core Ops, SparseCore 0:
  122.9 121.1 all-reduce.10
  246.6 84.8 all-reduce.12
  484.8 85.8 all-reduce.14
  578.7 126.2 all-reduce.16
  707.4 84.8 all-reduce.18
  958.5 85.8 all-reduce.20
  1053.2 126.1 all-reduce.22
  1181.9 84.8 all-reduce.24
  1427.1 85.8 all-reduce.26
where the time goes:
time: 1550 us; the launch traced here: 1530 us
  waiting for transfers between devices  933 us (60%)
  other arithmetic  405 us (26%)
  local copies, waits for them, and re-layouts  105 us (7%)
  matrix products  57.4 us (4%)
  between operations  21.9 us (1%)
    psum x9, waiting for transfers between devices, from_root(): return lax.psum(block, axis)  886 us
    another operation x44, other arithmetic, body(): pivot_factor = jnp.linalg.cholesky(pivot_block)  238 us
    another operation x7, other arithmetic, body(): lax.linalg.triangular_solve(pivot_factor, panel_rows, left_side=False, lo...  124 us
    all_to_all x1, waiting for transfers between devices, body(): lax.all_to_all(widened, 'row', split_axis=0, concat_axis=0, tiled=True)  47.7 us
    another operation x64, local copies, waits for them, and re-layouts, body(): lax.linalg.triangular_solve(pivot_factor, panel_rows, left_side=False, lo...  38.4 us
    scatter x2, local copies, waits for them, and re-layouts, body(): jnp.zeros((row_count, cyc_rows, cols_loc), jnp.float32).at[:, :, own_cols]  32 us
  transfers between devices with their start and end apart: 10, of which 10 were waited for; matrix products, arithmetic and copies ran while one was open for 0% of the time, Pallas kernels for 0%

commit v1 on v0

v1 whole, which is shorter than its diff:
```python
import functools

import jax
import jax.numpy as jnp
from jax import lax
from jax.experimental import pallas as pl
from jax.experimental.pallas import tpu as pltpu
from jax.sharding import PartitionSpec as P

CB = 4096
NKIDS = 4
BLOCK = 512
PANELS = 3
PICK = 256
LEAD = BLOCK * PANELS
F32 = jnp.float32
B16 = jnp.bfloat16


def split3(x):
    high = x.astype(B16).astype(F32)
    rest = x - high
    mid = rest.astype(B16).astype(F32)
    return high, mid, rest - mid


def outer_update(lhs, rhs):
    a_high, a_mid, a_low = split3(lhs)
    b_high, b_mid, b_low = split3(rhs)
    a = jnp.concatenate([a_high, a_high, a_mid, a_high, a_low, a_mid], 0).astype(B16)
    b = jnp.concatenate([b_high, b_mid, b_high, b_low, b_high, b_mid], 0).astype(B16)
    return lax.dot_general(a, b, (((0,), (0,)), ((), ())), preferred_element_type=F32)


def factor_tile(rows):
    count = len(rows)
    lane = lax.broadcasted_iota(jnp.int32, (8, 128), 1)
    sub = lax.broadcasted_iota(jnp.int32, (8, 128), 0)
    rows = list(rows)
    uppers, inverses = [], []
    for k in range(count):
        c0 = 8 * k
        own = (lane >= c0) & (lane < c0 + 8)
        cur = rows[k]
        nxt = rows[k + 1] if k + 1 < count else None
        top = [jnp.broadcast_to(cur[:, c0 + j : c0 + j + 1], (8, 128)) for j in range(8)]
        if nxt is not None:
            low = [jnp.broadcast_to(nxt[:, c0 + j : c0 + j + 1], (8, 128)) for j in range(8)]
            after = jnp.where(own, 0.0, nxt)
        upper = cur
        inv = jnp.where(own, jnp.where(lane - c0 == sub, 1.0, 0.0), cur)
        for j in range(8):
            scale = lax.rsqrt(jnp.broadcast_to(top[j][j : j + 1, :], (8, 128)))
            mult = jnp.where(sub > j, top[j] * scale, 0.0)
            if nxt is not None:
                low_mult = low[j] * scale
            for m in range(j + 1, 8):
                u = jnp.broadcast_to(top[m][j : j + 1, :], (8, 128)) * scale
                top[m] = top[m] - mult * u
                if nxt is not None:
                    low[m] = low[m] - low_mult * u
            u = jnp.broadcast_to(upper[j : j + 1, :], (8, 128)) * scale
            upper = jnp.where(sub == j, u, upper - mult * u)
            u = jnp.broadcast_to(inv[j : j + 1, :], (8, 128)) * scale
            inv = jnp.where(sub == j, u, inv - mult * u)
            if nxt is not None:
                after = after - low_mult * u
        uppers.append(jnp.where(lane - c0 >= sub, upper, 0.0))
        inverses.append(jnp.where(lane < c0 + 8, inv, 0.0))
        if nxt is not None:
            rows[k + 1] = after
        if k + 2 < count:
            update = outer_update(jnp.where(lane >= c0 + 16, upper, 0.0), inv)
            for i in range(k + 2, count):
                rows[i] = jnp.where(own, 0.0, rows[i]) - update[8 * i : 8 * i + 8, :]
    return uppers, inverses


def mm(a, b, flip=False):
    dims = (((1,), (1 if flip else 0,)), ((), ()))
    return lax.dot_general(a, b, dims, precision=lax.Precision.HIGHEST, preferred_element_type=F32)


def factor_block(l_ref, w_ref, s_ref):
    size = s_ref.shape[0]
    tiles = size // 128
    l_ref[...] = jnp.zeros_like(l_ref)
    w_ref[...] = jnp.zeros_like(w_ref)
    for k in range(tiles):
        o = 128 * k
        e = o + 128
        rows = [s_ref[o + 8 * i : o + 8 * i + 8, o:e] for i in range(16)]
        uppers, inverses = factor_tile(rows)
        inv = jnp.concatenate(inverses, 0)
        l_ref[o:e, o:e] = jnp.concatenate(uppers, 0).T
        w_ref[o:e, o:e] = inv
        if k + 1 < tiles:
            below = mm(s_ref[e:, o:e], inv, True)
            l_ref[e:, o:e] = below
            s_ref[e:, e:] = s_ref[e:, e:] - mm(below, below, True)
    half = 128
    while half < size:
        for o in range(0, size, 2 * half):
            m = o + half
            e = m + half
            t = mm(l_ref[m:e, o:m], w_ref[o:m, o:m])
            w_ref[m:e, o:m] = -mm(w_ref[m:e, m:e], t)
        half *= 2


def factor0(a_ref, l_ref, w_ref, s_ref):
    s_ref[...] = a_ref[...]
    factor_block(l_ref, w_ref, s_ref)


def factor1(a_ref, w0_ref, l_ref, w_ref, l10_ref, s_ref):
    l10 = mm(a_ref[:, :BLOCK], w0_ref[...], True)
    l10_ref[...] = l10
    s_ref[...] = a_ref[:, BLOCK:] - mm(l10, l10, True)
    factor_block(l_ref, w_ref, s_ref)


def factor2(a_ref, w0_ref, w1_ref, l10_ref, l_ref, w_ref, l20_ref, l21_ref, s_ref):
    l20 = mm(a_ref[:, :BLOCK], w0_ref[...], True)
    l20_ref[...] = l20
    l21 = mm(a_ref[:, BLOCK : 2 * BLOCK] - mm(l20, l10_ref[...], True), w1_ref[...], True)
    l21_ref[...] = l21
    s_ref[...] = a_ref[:, 2 * BLOCK :] - mm(l20, l20, True) - mm(l21, l21, True)
    factor_block(l_ref, w_ref, s_ref)


def factor_call(kernel, outs, *args):
    square = jax.ShapeDtypeStruct((BLOCK, BLOCK), F32)
    return pl.pallas_call(
        kernel,
        out_shape=[square] * outs,
        scratch_shapes=[pltpu.VMEM((BLOCK, BLOCK), F32)],
        compiler_params=pltpu.CompilerParams(vmem_limit_bytes=40 << 20),
        cost_estimate=pl.CostEstimate(flops=20_000_000_000, bytes_accessed=1 << 24, transcendentals=0),
    )(*args)


def dot3(a, b, flip=False):
    dims = (((1,), (1 if flip else 0,)), ((), ()))
    return lax.dot_general(a, b, dims, precision=lax.Precision.HIGH, preferred_element_type=F32)


def spread(a, axis, count):
    return lax.all_to_all(jnp.broadcast_to(a[None], (count,) + a.shape), axis, 0, 0, tiled=True)


def body(root_front, contrib, index_map):
    nr = lax.axis_size("row")
    nc = lax.axis_size("col")
    r = lax.axis_index("row")
    c = lax.axis_index("col")
    rows_loc, cols_loc = root_front.shape
    group = nr // NKIDS
    kid = r // group
    part = r % group
    place = jnp.arange(BLOCK, dtype=jnp.int32)

    def hot(kid_id, rng):
        own = lax.dynamic_slice(index_map, (kid_id, rng * PICK), (1, PICK))[0] - rng * BLOCK
        return (own[:, None] == place[None, :]).astype(F32)

    with jax.named_scope("slices"):
        own_cols = hot(kid, c)
        first = dot3(own_cols.T, contrib[:PICK].T)
        third = dot3(own_cols.T, contrib[PICK : 2 * PICK].T)
        first = dot3(first, hot(kid, part))
        root_t = root_front.T
        first = first + jnp.where(r == 0, root_t[:, :BLOCK], 0.0)
        second = jnp.where(r == 0, root_t[:, BLOCK:], root_t[:, :BLOCK])
        outgoing = jnp.concatenate([first, second, third], 1)
        outgoing = outgoing.reshape(nr, cols_loc // nr, 2 * BLOCK + PICK)
        got = lax.all_to_all(outgoing, "row", 0, 0, tiled=True)
        lead0 = got[0, :, :BLOCK] + got[2, :, :BLOCK] + got[4, :, :BLOCK] + got[6, :, :BLOCK]
        lead1 = got[1, :, :BLOCK] + got[3, :, :BLOCK] + got[5, :, :BLOCK] + got[7, :, :BLOCK]
        lead1 = lead1 + got[0, :, BLOCK : 2 * BLOCK]
        narrow = jnp.concatenate([got[group * q, :, 2 * BLOCK :] for q in range(NKIDS)], 1)
        lead2 = got[1, :, BLOCK : 2 * BLOCK] + dot3(
            narrow, jnp.concatenate([hot(q, 2) for q in range(NKIDS)], 0)
        )
        own_slice = jnp.concatenate([lead0, lead1, lead2], 1)

    with jax.named_scope("lead"):
        piece = own_slice.shape[0] // nc
        pieces = lax.all_to_all(own_slice.reshape(nc, piece, LEAD), "col", 0, 0, tiled=True)
        a00 = spread(pieces[0, :, :BLOCK], ("row", "col"), nr * nc).reshape(BLOCK, BLOCK)
        rest = jnp.concatenate([pieces[1, :, : 2 * BLOCK], pieces[2]], 1)
        rest = spread(rest, "row", nr)
        rest = lax.all_gather(rest, "col", axis=0, tiled=False)
        rest = rest.transpose(1, 0, 2, 3).reshape(BLOCK, 5 * BLOCK)

    with jax.named_scope("panel_rows"):
        perm = []
        for i in range(nr):
            for j in range(nc):
                front = j * cols_loc + i * (cols_loc // nr)
                perm.append((i * nc + j, front // rows_loc * nc + front % rows_loc // (rows_loc // nc)))
        other = lax.ppermute(own_slice, ("row", "col"), perm)
        row_rows = lax.all_gather(other, "col", axis=0, tiled=True)
        col_rows = spread(own_slice, "row", nr).reshape(cols_loc, LEAD)

    with jax.named_scope("factor"):
        l00, w0 = factor_call(factor0, 2, a00)
        l11, w1, l10 = factor_call(factor1, 3, rest[:, : 2 * BLOCK], w0)
        l22, w2, l20, l21 = factor_call(factor2, 4, rest[:, 2 * BLOCK :], w0, w1, l10)

    with jax.named_scope("extend_add"):
        arrived = lax.all_to_all(contrib.reshape(nr, PICK, PICK), "row", 0, 0, tiled=True)
        halves = []
        for h in range(group):
            rng = group * r + h
            wide = jnp.concatenate(
                [dot3(arrived[group * q + h], hot(q, c)) for q in range(NKIDS)], 0
            )
            picks = jnp.concatenate([hot(q, rng) for q in range(NKIDS)], 0)
            halves.append(dot3(picks.T, wide))
        assembled = root_front + jnp.concatenate(halves, 0)

    with jax.named_scope("solve"):
        both = jnp.concatenate([row_rows, col_rows], 0)
        s0 = dot3(both[:, :BLOCK], w0, True)
        s1 = dot3(both[:, BLOCK : 2 * BLOCK] - dot3(s0, l10, True), w1, True)
        s2 = dot3(both[:, 2 * BLOCK :] - dot3(s0, l20, True) - dot3(s1, l21, True), w2, True)
        solved = jnp.concatenate([s0, s1, s2], 1)

    with jax.named_scope("schur"):
        schur = assembled - dot3(solved[:rows_loc], solved[rows_loc:], True)
        panel = jnp.where(c == 0, s0, jnp.where(c == 1, s1, s2))[:rows_loc]
        diag = jnp.where(c == 0, l00, jnp.where(c == 1, l11, l22))
        rng = group * r + jnp.arange(rows_loc)[:, None] // BLOCK
        lead = jnp.where(rng > c, panel, jnp.where(rng == c, jnp.concatenate([diag] * group, 0), 0.0))
        return jnp.where(c < PANELS, lead, jnp.where(rng < PANELS, 0.0, schur))


def solution(mesh):
    placed = (P("row", "col"), P("row", "col"), P())
    return jax.shard_map(
        body, mesh=mesh, in_specs=placed, out_specs=P("row", "col"), check_vma=False
    )
```

time: 1550 us -> 382 us (0.25)
  the two profiles are of different devices: /device:TPU:7 before, /device:TPU:4 now
where the time goes in v1:
time: 382 us; the launch traced here: 375 us
  waiting for transfers between devices  88 us (23%)
  Pallas kernels  68.7 us (18%)
  matrix products  56.8 us (15%)
  starting transfers between devices  52.8 us (14%)
  local copies, waits for them, and re-layouts  44.1 us (12%)
  blocking collectives  26.2 us (7%)
  other arithmetic  24 us (6%)
  between operations  14.1 us (4%)
    pallas_call x3, Pallas kernels, factor_call(): pl.pallas_call(kernel, out_shape=[square] * outs, scratch_shapes=[pltpu.V...  68.7 us
    dot_general x21, matrix products, dot3(): lax.dot_general(a, b, dims, precision=lax.Precision.HIGH, preferred_eleme...  56.8 us
    all_to_all x1, waiting for transfers between devices, body(): lax.all_to_all(contrib.reshape(nr, PICK, PICK), 'row', 0, 0, tiled=True)  32.3 us
    all_to_all x1, waiting for transfers between devices, body(): got = lax.all_to_all(outgoing, 'row', 0, 0, tiled=True)  30.7 us
    all_to_all x2, starting transfers between devices, spread(): lax.all_to_all(jnp.broadcast_to(a[None], (count,) + a.shape), axis, 0, 0,...  23.1 us
    all_to_all x1, starting transfers between devices, body(): lax.all_to_all(contrib.reshape(nr, PICK, PICK), 'row', 0, 0, tiled=True)  17 us
    ppermute x1, waiting for transfers between devices, body(): other = lax.ppermute(own_slice, ('row', 'col'), perm)  15.8 us
    all_to_all x1, blocking collectives, body(): lax.all_to_all(own_slice.reshape(nc, piece, LEAD), 'col', 0, 0, tiled=True)  14.4 us
  transfers between devices with their start and end apart: 7, of which 4 were waited for; matrix products, arithmetic and copies ran while one was open for 11% of the time, Pallas kernels for 18%

profile of v1, /device:TPU:4, one launch (start us, length us, event | category | flops | bytes accessed | tf_op | source)
XLA Modules:
  0.0 374.6 jit_solution(16469761553167784958)
XLA Ops:
  6.5 1.7 dynamic-slice_subtract_fusion.11
  8.2 1.4 fusion.64
  9.6 1.4 fusion.66
  11.0 1.8 slice_select_fusion
  13.6 2.1 copy.13
  15.7 8.3 %all-to-all-start = ((f32[8,64,1280]{2,1,0:T(8,128)}), f32[8,64,1280]{2,1,0:T(8,128)S(1)}, u32[]{:S(2)}, u32[]{:S(2)}) async-start(f32[8,64,1280]{2,1,0:T(8,128)} %bitcast.3), calls=%async_computation | async-start | bytes 5242880 | tf_op jit(solution)/shard_map/slices/all_to_all | solution.py:177
  24.4 30.7 %all-to-all-done = f32[8,64,1280]{2,1,0:T(8,128)S(1)} async-done(((f32[8,64,1280]{2,1,0:T(8,128)}), f32[8,64,1280]{2,1,0:T(8,128)S(1)}, u32[]{:S(2)}, u32[]{:S(2)}) %all-to-all-start) | async-done | bytes 2621472 | tf_op jit(solution)/shard_map/slices/all_to_all | solution.py:177
  55.9 14.4 %all_to_all.30 = f32[16,4,1536]{2,1,0:T(4,128)S(1)} all-to-all(f32[16,4,1536]{2,1,0:T(4,128)S(1)} %reshape.202), channel_id=1, replica_groups=mesh['row'=8,'col'=16] {'col'}, dimensions={0} | all-to-all | bytes 786432 | tf_op jit(solution)/shard_map/lead/all_to_all | solution.py:189
  70.5 11.8 %all_to_all.31 = f32[8,4,2560]{2,1,0:T(4,128)S(1)} all-to-all(f32[8,4,2560]{2,1,0:T(4,128)S(1)} %broadcast_in_dim.36), channel_id=1, replica_groups=mesh['row'=8,'col'=16] {'row'}, dimensions={0} | all-to-all | bytes 655360 | tf_op jit(solution)/shard_map/lead/all_to_all | solution.py:149
  83.2 4.4 %collective-permute-start = (f32[64,1536]{1,0:T(8,128)S(1)}, f32[64,1536]{1,0:T(8,128)S(1)}, u32[]{:S(2)}, u32[]{:S(2)}) collective-permute-start(f32[64,1536]{1,0:T(8,128)S(1)} %pad_maximum_fusion.3), channel_id=1, source_target_pairs={{0,0},{1,8},{2,16},{3,24},{4,32},{5,40},{6,48},{7,56},{8,64},{9,72... | collective-permute-start | bytes 1179656 | tf_op jit(solution)/shard_map/panel_rows/ppermute | solution.py:202
  87.6 15.8 %collective-permute-done = f32[64,1536]{1,0:T(8,128)S(1)} collective-permute-done((f32[64,1536]{1,0:T(8,128)S(1)}, f32[64,1536]{1,0:T(8,128)S(1)}, u32[]{:S(2)}, u32[]{:S(2)}) %collective-permute-start) | collective-permute-done | bytes 393248 | tf_op jit(solution)/shard_map/panel_rows/ppermute | solution.py:202
  104.1 17.0 %all-to-all-start.5 = ((f32[8,256,256]{2,1,0:T(8,128)}), f32[8,256,256]{2,1,0:T(8,128)S(1)}, u32[]{:S(2)}, u32[]{:S(2)}) async-start(f32[8,256,256]{2,1,0:T(8,128)} %bitcast.102), calls=%async_computation.5 | async-start | bytes 4194304 | tf_op jit(solution)/shard_map/extend_add/all_to_all | solution.py:212
  126.0 32.3 %all-to-all-done.5 = f32[8,256,256]{2,1,0:T(8,128)S(1)} async-done(((f32[8,256,256]{2,1,0:T(8,128)}), f32[8,256,256]{2,1,0:T(8,128)S(1)}, u32[]{:S(2)}, u32[]{:S(2)}) %all-to-all-start.5) | async-done | bytes 2097184 | tf_op jit(solution)/shard_map/extend_add/all_to_all | solution.py:212
  158.3 1.3 convolution_bitcast_fusion
  159.6 1.2 convolution_bitcast_fusion.4
  160.8 1.2 convolution_bitcast_fusion.1
  162.0 1.2 convolution_bitcast_fusion.2
  163.2 1.2 convolution_bitcast_fusion.3
  164.5 1.1 broadcast_in_dim.35
  165.6 15.8 %all-to-all-start.3 = ((f32[128,4,512]{2,1,0:T(4,128)}), f32[128,4,512]{2,1,0:T(4,128)S(1)}, u32[]{:S(2)}, u32[]{:S(2)}) async-start(f32[128,4,512]{2,1,0:T(4,128)} %broadcast_in_dim.35), calls=%async_computation.3 | async-start | bytes 2097152 | tf_op jit(solution)/shard_map/lead/all_to_all | solution.py:149
  181.4 4.2 %fusion.29 = f32[512,512]{1,0:T(8,128)} fusion(f32[256,512]{1,0:T(8,128)} %convolution_bitcast_fusion, f32[256,512]{1,0:T(8,128)} %convolution_bitcast_fusion.1, f32[256,512]{1,0:T(8,128)} %convolution_bitcast_fusion.2, f32[256,512]{1,0:T(8,128)} %convolution_bitcast_fusion.3, pred[256,512]{1,0:T(32,128)(4,1)} %get-tuple-element.53, ...), kind=kOutput, calls=%fused_computation.34 | convolution fusion | flops 1613758464 | bytes 3670016 | tf_op jit(solution)/shard_map/extend_add/dot_general | solution.py:145
  186.9 2.3 fusion.21
  189.2 9.3 %all-to-all-done.3 = f32[128,4,512]{2,1,0:T(4,128)S(1)} async-done(((f32[128,4,512]{2,1,0:T(4,128)}), f32[128,4,512]{2,1,0:T(4,128)S(1)}, u32[]{:S(2)}, u32[]{:S(2)}) %all-to-all-start.3) | async-done | bytes 1048608 | tf_op jit(solution)/shard_map/lead/all_to_all | solution.py:149
  198.5 2.1 broadcast_in_dim.33
  200.5 7.3 %all-to-all-start.1 = ((f32[8,64,1536]{2,1,0:T(8,128)}), f32[8,64,1536]{2,1,0:T(8,128)}, u32[]{:S(2)}, u32[]{:S(2)}) async-start(f32[8,64,1536]{2,1,0:T(8,128)} %broadcast_in_dim.33), calls=%async_computation.1 | async-start | bytes 6291456 | tf_op jit(solution)/shard_map/panel_rows/all_to_all | solution.py:149
  208.2 18.8 %factor.3 = (f32[512,512]{1,0:T(8,128)S(1)}, f32[512,512]{1,0:T(8,128)S(1)}) custom-call(f32[512,512]{1,0:T(8,128)S(1)} %reshape.203.a_ref), custom_call_target="tpu_custom_call" | custom-call | flops 20000000000 | bytes 16777216 | tf_op jit(solution)/shard_map/factor/pallas_call | solution.py:134
  228.0 8.9 %copy.15 = f32[8,16,4,2560]{3,2,1,0:T(4,128)} copy(f32[8,16,4,2560]{3,0,1,2:T(8,128)} %bitcast.101) | data formatting | bytes 10485760 | tf_op jit(solution)/shard_map/lead/transpose | solution.py:194
  236.9 7.2 %reshape.204 = f32[512,2560]{1,0:T(8,128)} reshape(f32[8,16,4,2560]{3,2,1,0:T(4,128)} %copy.15) | data formatting | bytes 10485760 | tf_op jit(solution)/shard_map/lead/reshape | solution.py:194
  244.1 2.0 slice.172.a_ref
  246.1 22.4 %factor.4 = (f32[512,512]{1,0:T(8,128)S(1)}, f32[512,512]{1,0:T(8,128)S(1)}, f32[512,512]{1,0:T(8,128)S(1)}) custom-call(f32[512,1024]{1,0:T(8,128)S(1)} %slice.172.a_ref, f32[512,512]{1,0:T(8,128)S(1)} %get-tuple-element.14.w0_ref), custom_call_target="tpu_custom_call" | custom-call | flops 20000000000 | bytes 16777216 | tf_op jit(solution)/shard_map/factor/pallas_call | solution.py:134
  270.2 27.4 %factor.5 = (f32[512,512]{1,0:T(8,128)S(1)}, f32[512,512]{1,0:T(8,128)S(1)}, f32[512,512]{1,0:T(8,128)S(1)}, f32[512,512]{1,0:T(8,128)S(1)}) custom-call(f32[512,1536]{1,0:T(8,128)S(1)} %slice.173.a_ref, f32[512,512]{1,0:T(8,128)S(1)} %copy-done.7, f32[512,512]{1,0:T(8,128)S(1)} %get-tuple-element.16.w1_ref, f32[512,512]{1,0:T(8,128)S(1)} %get-tuple-element.15.l10_ref), custom_call_target="tpu_custom_call" | custom-call | flops 20000000000 | bytes 16777216 | tf_op jit(solution)/shard_map/factor/pallas_call | solution.py:134
  297.7 1.0 copy-done
  298.7 1.3 select_select_fusion
  300.0 4.9 %fusion.7 = f32[1536,512]{0,1:T(8,128)S(1)} fusion(f32[512,512]{1,0:T(8,128)} %copy-done.6, f32[1024,1536]{1,0:T(8,128)} %all-gather.4.cloned.1.call-done, f32[512,1536]{1,0:T(8,128)} %bitcast.15), kind=kOutput, calls=%fused_computation.11 | convolution fusion | flops 2416705536 | bytes 13631488 | tf_op jit(solution)/shard_map/solve/dot_general | solution.py:145
  304.9 5.6 %fusion.107 = f32[1536,512]{1,0:T(8,128)S(1)} fusion(f32[1536,512]{0,1:T(8,128)S(1)} %fusion.7, f32[512,512]{1,0:T(8,128)S(1)} %copy-done.3), kind=kOutput, calls=%fused_computation.186 | convolution fusion | flops 2415919104 | bytes 7340032 | tf_op jit(solution)/shard_map/solve/dot_general | solution.py:145
  310.5 1.6 slice.176
  312.1 3.9 %fusion.4 = f32[1536,512]{0,1:T(8,128)S(1)} fusion(f32[512,512]{1,0:T(8,128)S(1)} %get-tuple-element.16.w1_ref, f32[1536,512]{1,0:T(8,128)S(1)} %fusion.107, f32[1024,1536]{1,0:T(8,128)S(1)} %copy-done.12, f32[512,1536]{1,0:T(8,128)} %bitcast.15), kind=kOutput, calls=%fused_computation.9 | convolution fusion | flops 2417491968 | bytes 16777216 | tf_op jit(solution)/shard_map/solve/dot_general | solution.py:145
  316.0 2.0 copy-done.1
  318.0 5.1 %fusion.109 = f32[1536,512]{1,0:T(8,128)S(1)} fusion(f32[1536,512]{0,1:T(8,128)S(1)} %fusion.4, f32[512,512]{1,0:T(8,128)S(1)} %copy-done.1), kind=kOutput, calls=%fused_computation.188 | convolution fusion | flops 2415919104 | bytes 7340032 | tf_op jit(solution)/shard_map/solve/dot_general | solution.py:145
  323.1 5.2 %fusion.108 = f32[1536,512]{1,0:T(8,128)S(1)} fusion(f32[1536,512]{0,1:T(8,128)S(1)} %fusion.7, f32[512,512]{1,0:T(8,128)S(1)} %get-tuple-element.17), kind=kOutput, calls=%fused_computation.187 | convolution fusion | flops 2415919104 | bytes 7340032 | tf_op jit(solution)/shard_map/solve/dot_general | solution.py:145
  328.4 5.7 %fusion.16 = f32[1536,512]{0,1:T(8,128)} fusion(f32[512,512]{1,0:T(8,128)S(1)} %get-tuple-element.19, f32[1536,512]{1,0:T(8,128)S(1)} %fusion.109, f32[1536,512]{1,0:T(8,128)S(1)} %fusion.108, f32[512,1536]{1,0:T(8,128)} %bitcast.15, f32[1024,1536]{1,0:T(8,128)S(1)} %copy-done.12), kind=kOutput, calls=%fused_computation.20 | convolution fusion | flops 2418278400 | bytes 19922944 | tf_op jit(solution)/shard_map/solve/dot_general | solution.py:145
  334.1 8.4 %pad_maximum_fusion = f32[1536,1536]{0,1:T(8,128)} fusion(f32[1536,512]{0,1:T(8,128)} %fusion.16, f32[1536,512]{0,1:T(8,128)} %copy-done.10, f32[1536,512]{0,1:T(8,128)} %copy-done.8), kind=kLoop, calls=%fused_computation.4 | loop fusion | flops 4718592 | bytes 18874368 | tf_op jit(solution)/shard_map/solve/concatenate | solution.py:228
  342.5 3.3 slice.175
  345.8 8.6 %fusion = f32[1024,512]{1,0:T(8,128)} fusion(f32[1536,1536]{0,1:T(8,128)} %pad_maximum_fusion, f32[1536,512]{0,1:T(8,128)} %fusion.16, f32[1536,512]{0,1:T(8,128)S(1)} %copy-done.11, f32[1536,512]{0,1:T(8,128)S(1)} %copy-done.9), kind=kOutput, calls=%fused_computation.5 | convolution fusion | flops 4833411072 | bytes 17825792 | tf_op jit(solution)/shard_map/schur/dot_general | solution.py:145
  354.4 3.1 copy.19
  357.5 1.8 copy.20
  359.3 3.1 copy.21
  362.4 5.2 %fusion.20 = f32[1024,512]{1,0:T(8,128)} fusion(f32[512,512]{1,0:T(8,128)S(1)} %copy-done.15, f32[1024,512]{1,0:T(8,128)} %fusion, f32[1024,512]{1,0:T(8,128)S(1)} %copy-done.14, f32[512,512]{1,0:T(8,128)} %fusion.29, f32[512,512]{1,0:T(8,128)} %fusion.21, f32[1024,512]{1,0:T(8,128)} %copy.19, f32[1024,512]{1,0:T(8,128)} %copy.20, f32[1024,512]{1,0:T(8,128)} %copy.21, ...), kind=kLoop, calls=%fused_computation.25 | loop fusion | flops 5242880 | bytes 15731715 | tf_op jit(solution)/shard_map/schur/jit(_where)/select_n | solution.py:236
  (104 shorter events, 13.0 us)
Async XLA Ops:
  6.5 6.2 %copy-start.13 = (f32[1024,512]{1,0:T(8,128)S(1)}, f32[1024,512]{1,0:T(8,128)}, u32[]{:S(2)}) copy-start(f32[1024,512]{1,0:T(8,128)} %param.3) | copy-start | bytes 6291460
  15.7 39.4 %all-to-all-start = ((f32[8,64,1280]{2,1,0:T(8,128)}), f32[8,64,1280]{2,1,0:T(8,128)S(1)}, u32[]{:S(2)}, u32[]{:S(2)}) async-start(f32[8,64,1280]{2,1,0:T(8,128)} %bitcast.3), calls=%async_computation | async-start | bytes 5242880 | tf_op jit(solution)/shard_map/slices/all_to_all | solution.py:177
  24.0 204.0 %all-gather.6.cloned.1.call-start = ((), (), s32[]{:S(2)}) async-start(), calls=%async_computation.7 | async-start | bytes 5570560 | tf_op jit(solution)/shard_map/lead/all_gather | solution.py:193
  70.4 51.9 %copy-start.28 = (s32[1,256]{1,0:T(1,128)S(1)}, s32[1,256]{1,0:T(1,128)}, u32[]{:S(2)}) copy-start(s32[1,256]{1,0:T(1,128)} %get-tuple-element.45) | copy-start | bytes 3076
  70.4 51.9 %copy-start.29 = (s32[1,256]{1,0:T(1,128)S(1)}, s32[1,256]{1,0:T(1,128)}, u32[]{:S(2)}) copy-start(s32[1,256]{1,0:T(1,128)} %get-tuple-element.46) | copy-start | bytes 3076
  70.4 52.8 %copy-start.26 = (s32[1,256]{1,0:T(1,128)S(1)}, s32[1,256]{1,0:T(1,128)}, u32[]{:S(2)}) copy-start(s32[1,256]{1,0:T(1,128)} %get-tuple-element.30) | copy-start | bytes 3076
  70.4 52.8 %copy-start.27 = (s32[1,256]{1,0:T(1,128)S(1)}, s32[1,256]{1,0:T(1,128)}, u32[]{:S(2)}) copy-start(s32[1,256]{1,0:T(1,128)} %get-tuple-element.31) | copy-start | bytes 3076
  82.2 41.9 %copy-start.24 = (s32[1,256]{1,0:T(1,128)S(1)}, s32[1,256]{1,0:T(1,128)}, u32[]{:S(2)}) copy-start(s32[1,256]{1,0:T(1,128)} %get-tuple-element.36) | copy-start | bytes 3076
  82.2 41.9 %copy-start.25 = (s32[1,256]{1,0:T(1,128)S(1)}, s32[1,256]{1,0:T(1,128)}, u32[]{:S(2)}) copy-start(s32[1,256]{1,0:T(1,128)} %get-tuple-element.37) | copy-start | bytes 3076
  82.3 42.9 %copy-start.22 = (s32[1,256]{1,0:T(1,128)S(1)}, s32[1,256]{1,0:T(1,128)}, u32[]{:S(2)}) copy-start(s32[1,256]{1,0:T(1,128)} %get-tuple-element.29) | copy-start | bytes 3076
  82.3 42.9 %copy-start.23 = (s32[1,256]{1,0:T(1,128)S(1)}, s32[1,256]{1,0:T(1,128)}, u32[]{:S(2)}) copy-start(s32[1,256]{1,0:T(1,128)} %get-tuple-element.38) | copy-start | bytes 3076
  83.1 216.8 %all-gather.4.cloned.1.call-start = ((), (), s32[]{:S(2)}) async-start(), calls=%async_computation.6 | async-start | bytes 6684672 | tf_op jit(solution)/shard_map/panel_rows/all_gather | solution.py:203
  83.2 20.2 %collective-permute-start = (f32[64,1536]{1,0:T(8,128)S(1)}, f32[64,1536]{1,0:T(8,128)S(1)}, u32[]{:S(2)}, u32[]{:S(2)}) collective-permute-start(f32[64,1536]{1,0:T(8,128)S(1)} %pad_maximum_fusion.3), channel_id=1, source_target_pairs={{0,0},{1,8},{2,16},{3,24},{4,32},{5,40},{6,48},{7,56},{8,64},{9,72... | collective-permute-start | bytes 1179656 | tf_op jit(solution)/shard_map/panel_rows/ppermute | solution.py:202
  103.4 0.8 copy-start.17
  104.1 54.1 %all-to-all-start.5 = ((f32[8,256,256]{2,1,0:T(8,128)}), f32[8,256,256]{2,1,0:T(8,128)S(1)}, u32[]{:S(2)}, u32[]{:S(2)}) async-start(f32[8,256,256]{2,1,0:T(8,128)} %bitcast.102), calls=%async_computation.5 | async-start | bytes 4194304 | tf_op jit(solution)/shard_map/extend_add/all_to_all | solution.py:212
  165.6 32.9 %all-to-all-start.3 = ((f32[128,4,512]{2,1,0:T(4,128)}), f32[128,4,512]{2,1,0:T(4,128)S(1)}, u32[]{:S(2)}, u32[]{:S(2)}) async-start(f32[128,4,512]{2,1,0:T(4,128)} %broadcast_in_dim.35), calls=%async_computation.3 | async-start | bytes 2097152 | tf_op jit(solution)/shard_map/lead/all_to_all | solution.py:149
  181.3 5.5 %copy-start.16 = (f32[256,512]{1,0:T(8,128)S(1)}, f32[256,512]{1,0:T(8,128)}, u32[]{:S(2)}) copy-start(f32[256,512]{1,0:T(8,128)} %convolution_bitcast_fusion.4) | copy-start | bytes 1572868
  181.3 5.5 %copy-start.18 = (pred[256,512]{1,0:T(32,128)(4,1)S(1)}, pred[256,512]{1,0:T(32,128)(4,1)}, u32[]{:S(2)}) copy-start(pred[256,512]{1,0:T(32,128)(4,1)} %get-tuple-element.57) | copy-start | bytes 393220
  181.4 5.5 %copy-start.19 = (pred[256,512]{1,0:T(32,128)(4,1)S(1)}, pred[256,512]{1,0:T(32,128)(4,1)}, u32[]{:S(2)}) copy-start(pred[256,512]{1,0:T(32,128)(4,1)} %get-tuple-element.58) | copy-start | bytes 393220
  181.4 5.5 %copy-start.20 = (pred[256,512]{1,0:T(32,128)(4,1)S(1)}, pred[256,512]{1,0:T(32,128)(4,1)}, u32[]{:S(2)}) copy-start(pred[256,512]{1,0:T(32,128)(4,1)} %get-tuple-element.59) | copy-start | bytes 393220
  181.4 5.5 %copy-start.21 = (pred[256,512]{1,0:T(32,128)(4,1)S(1)}, pred[256,512]{1,0:T(32,128)(4,1)}, u32[]{:S(2)}) copy-start(pred[256,512]{1,0:T(32,128)(4,1)} %get-tuple-element.60) | copy-start | bytes 393220
  200.5 99.4 %all-to-all-start.1 = ((f32[8,64,1536]{2,1,0:T(8,128)}), f32[8,64,1536]{2,1,0:T(8,128)}, u32[]{:S(2)}, u32[]{:S(2)}) async-start(f32[8,64,1536]{2,1,0:T(8,128)} %broadcast_in_dim.33), calls=%async_computation.1 | async-start | bytes 6291456 | tf_op jit(solution)/shard_map/panel_rows/all_to_all | solution.py:149
  227.0 1.0 copy-start.4
  228.0 18.1 %copy-start.6 = (f32[512,512]{1,0:T(8,128)}, f32[512,512]{1,0:T(8,128)S(1)}, u32[]{:S(2)}) copy-start(f32[512,512]{1,0:T(8,128)S(1)} %get-tuple-element.14.w0_ref) | copy-start | bytes 3145732
  244.1 24.4 %slice-start.1 = ((s8[5242880]{0:T(1024)(128)(4,1)}), s8[4194304]{0:T(1024)(128)(4,1)S(1)}, s32[]{:S(2)}) async-start(s8[5242880]{0:T(1024)(128)(4,1)} %bitcast.97), calls=%async_computation.9 | async-start | bytes 8388608
  246.1 22.5 %slice-start.2 = ((s8[5242880]{0:T(1024)(128)(4,1)}), s8[1048576]{0:T(1024)(128)(4,1)S(1)}, s32[]{:S(2)}) async-start(s8[5242880]{0:T(1024)(128)(4,1)} %bitcast.97), calls=%async_computation.10 | async-start | bytes 2097152
  268.6 1.1 copy-start.2
  268.6 1.6 copy-start.7
  270.2 28.4 %copy-start.5 = (f32[512,512]{1,0:T(8,128)S(1)}, f32[512,512]{1,0:T(8,128)}, u32[]{:S(2)}) copy-start(f32[512,512]{1,0:T(8,128)} %copy-done.4) | copy-start | bytes 3145732
  297.7 1.0 copy-start
  300.0 4.9 %copy-start.3 = (f32[512,512]{1,0:T(8,128)S(1)}, f32[512,512]{1,0:T(8,128)}, u32[]{:S(2)}) copy-start(f32[512,512]{1,0:T(8,128)} %copy-done.2) | copy-start | bytes 3145732
  304.9 18.2 %copy-start.8 = (f32[1536,512]{0,1:T(8,128)}, f32[1536,512]{0,1:T(8,128)S(1)}, u32[]{:S(2)}) copy-start(f32[1536,512]{0,1:T(8,128)S(1)} %fusion.7) | copy-start | bytes 9437188
  304.9 7.2 %copy-start.12 = (f32[1024,1536]{1,0:T(8,128)S(1)}, f32[1024,1536]{1,0:T(8,128)}, u32[]{:S(2)}) copy-start(f32[1024,1536]{1,0:T(8,128)} %all-gather.4.cloned.1.call-done) | copy-start | bytes 18874372
  316.0 7.1 %copy-start.10 = (f32[1536,512]{0,1:T(8,128)}, f32[1536,512]{0,1:T(8,128)S(1)}, u32[]{:S(2)}) copy-start(f32[1536,512]{0,1:T(8,128)S(1)} %fusion.4) | copy-start | bytes 9437188
  316.0 2.0 copy-start.1
  334.1 11.7 %copy-start.11 = (f32[1536,512]{0,1:T(8,128)S(1)}, f32[1536,512]{0,1:T(8,128)}, u32[]{:S(2)}) copy-start(f32[1536,512]{0,1:T(8,128)} %copy-done.10) | copy-start | bytes 9437188
  342.5 3.3 copy-start.9
  354.4 3.1 slice-start
  359.3 3.1 copy-start.14
  359.3 3.1 copy-start.15
  359.3 3.1 copy-start.30
  359.3 3.1 copy-start.31
  359.3 3.1 copy-start.32
Sparse Core Ops, SparseCore 0:
  83.3 53.9 all-gather.5
  139.0 46.1 all-gather.3

commit v2 on v1

v2 whole, which is shorter than its diff:
```python
import jax
import jax.numpy as jnp
import numpy as np
from jax import lax
from jax.experimental import pallas as pl
from jax.experimental.pallas import tpu as pltpu
from jax.sharding import Mesh, PartitionSpec as P

CB = 4096
NKIDS = 4
BLOCK = 512
PANELS = 3
PICK = 256
LEAD = BLOCK * PANELS
F32 = jnp.float32
B16 = jnp.bfloat16


def split3(x):
    high = x.astype(B16).astype(F32)
    rest = x - high
    mid = rest.astype(B16).astype(F32)
    return high, mid, rest - mid


def outer_update(lhs, rhs):
    a_high, a_mid, a_low = split3(lhs)
    b_high, b_mid, b_low = split3(rhs)
    a = jnp.concatenate([a_high, a_high, a_mid, a_high, a_low, a_mid], 0).astype(B16)
    b = jnp.concatenate([b_high, b_mid, b_high, b_low, b_high, b_mid], 0).astype(B16)
    return lax.dot_general(a, b, (((0,), (0,)), ((), ())), preferred_element_type=F32)


def factor_tile(rows):
    count = len(rows)
    lane = lax.broadcasted_iota(jnp.int32, (8, 128), 1)
    sub = lax.broadcasted_iota(jnp.int32, (8, 128), 0)
    rows = list(rows)
    uppers, inverses = [], []
    for k in range(count):
        c0 = 8 * k
        own = (lane >= c0) & (lane < c0 + 8)
        cur = rows[k]
        nxt = rows[k + 1] if k + 1 < count else None
        top = [jnp.broadcast_to(cur[:, c0 + j : c0 + j + 1], (8, 128)) for j in range(8)]
        if nxt is not None:
            low = [jnp.broadcast_to(nxt[:, c0 + j : c0 + j + 1], (8, 128)) for j in range(8)]
            after = jnp.where(own, 0.0, nxt)
        upper = cur
        inv = jnp.where(own, jnp.where(lane - c0 == sub, 1.0, 0.0), cur)
        for j in range(8):
            scale = lax.rsqrt(jnp.broadcast_to(top[j][j : j + 1, :], (8, 128)))
            mult = jnp.where(sub > j, top[j] * scale, 0.0)
            if nxt is not None:
                low_mult = low[j] * scale
            for m in range(j + 1, 8):
                u = jnp.broadcast_to(top[m][j : j + 1, :], (8, 128)) * scale
                top[m] = top[m] - mult * u
                if nxt is not None:
                    low[m] = low[m] - low_mult * u
            u = jnp.broadcast_to(upper[j : j + 1, :], (8, 128)) * scale
            upper = jnp.where(sub == j, u, upper - mult * u)
            u = jnp.broadcast_to(inv[j : j + 1, :], (8, 128)) * scale
            inv = jnp.where(sub == j, u, inv - mult * u)
            if nxt is not None:
                after = after - low_mult * u
        uppers.append(jnp.where(lane - c0 >= sub, upper, 0.0))
        inverses.append(jnp.where(lane < c0 + 8, inv, 0.0))
        if nxt is not None:
            rows[k + 1] = after
        if k + 2 < count:
            update = outer_update(jnp.where(lane >= c0 + 16, upper, 0.0), inv)
            for i in range(k + 2, count):
                rows[i] = jnp.where(own, 0.0, rows[i]) - update[8 * i : 8 * i + 8, :]
    return uppers, inverses


def mm(a, b, flip=False):
    dims = (((1,), (1 if flip else 0,)), ((), ()))
    return lax.dot_general(a, b, dims, precision=lax.Precision.HIGHEST, preferred_element_type=F32)


def nt(a, b):
    return lax.dot_general(a, b, (((1,), (1,)), ((), ())), preferred_element_type=F32)


def split2(x):
    high = x.astype(B16)
    return high, (x - high.astype(F32)).astype(B16)


def left3(x):
    high, low = split2(x)
    return jnp.concatenate([high, high, low], 1)


def right3(x):
    high, low = split2(x)
    return jnp.concatenate([high, low, high], 1)


def mm3(a, b):
    return nt(left3(a), right3(b))


def whole(x):
    high, mid, low = split3(x)
    return jnp.concatenate([high, mid, low], 1).astype(B16)


def factor_block(l_ref, w_ref, s_ref):
    size = s_ref.shape[0]
    tiles = size // 128
    l_ref[...] = jnp.zeros_like(l_ref)
    w_ref[...] = jnp.zeros_like(w_ref)
    for k in range(tiles):
        o = 128 * k
        e = o + 128
        rows = [s_ref[o + 8 * i : o + 8 * i + 8, o:e] for i in range(16)]
        uppers, inverses = factor_tile(rows)
        inv = jnp.concatenate(inverses, 0)
        l_ref[o:e, o:e] = jnp.concatenate(uppers, 0).T
        w_ref[o:e, o:e] = inv
        if k + 1 < tiles:
            below = mm(s_ref[e:, o:e], inv, True)
            l_ref[e:, o:e] = below
            s_ref[e:, e:] = s_ref[e:, e:] - mm(below, below, True)
    half = 128
    while half < size:
        for o in range(0, size, 2 * half):
            m = o + half
            e = m + half
            t = mm(l_ref[m:e, o:m], w_ref[o:m, o:m])
            w_ref[m:e, o:m] = -mm(w_ref[m:e, m:e], t)
        half *= 2


def put_rows(dst, a_ref, b_ref, second, col):
    for q in range(8):
        for i in range(8):
            src = slice(64 * q + 8 * i, 64 * q + 8 * i + 8)
            cols = slice(col, col + BLOCK)
            dst[64 * i + 8 * q : 64 * i + 8 * q + 8, :] = jnp.where(second, b_ref[src, cols], a_ref[src, cols])


def factor0(odd_ref, mine_ref, other_ref, l_ref, w_ref, s_ref):
    put_rows(s_ref, mine_ref, other_ref, odd_ref[0] == 1, 0)
    factor_block(l_ref, w_ref, s_ref)


def factor1(odd_ref, mine_ref, other_ref, w0_ref, l_ref, w_ref, l10_ref, s_ref, x_ref):
    even = odd_ref[0] == 0
    put_rows(x_ref, mine_ref, other_ref, even, BLOCK)
    put_rows(s_ref, mine_ref, other_ref, even, 0)
    l10 = mm3(x_ref[...], w0_ref[...])
    l10_ref[...] = l10
    s_ref[...] = s_ref[...] - mm3(l10, l10)
    factor_block(l_ref, w_ref, s_ref)


def factor2(
    odd_ref, mine_ref, other_ref, w0_ref, w1_ref, l10_ref,
    l_ref, w_ref, l20_ref, l21_ref, s_ref, x_ref, y_ref,
):
    odd = odd_ref[0] == 1
    put_rows(x_ref, mine_ref, other_ref, odd, BLOCK)
    put_rows(y_ref, mine_ref, other_ref, jnp.logical_not(odd), 2 * BLOCK)
    put_rows(s_ref, mine_ref, other_ref, odd, 2 * BLOCK)
    l20 = mm3(x_ref[...].T, w0_ref[...])
    l20_ref[...] = l20
    l21 = mm3(y_ref[...].T - mm3(l20, l10_ref[...]), w1_ref[...])
    l21_ref[...] = l21
    both = jnp.concatenate([l20, l21], 1)
    s_ref[...] = s_ref[...] - mm3(both, both)
    factor_block(l_ref, w_ref, s_ref)


VMEM = pl.BlockSpec(memory_space=pltpu.VMEM)
SMEM = pl.BlockSpec(memory_space=pltpu.SMEM)
PARAMS = pltpu.CompilerParams(vmem_limit_bytes=60 << 20)


def factor_call(kernel, outs, scratch, *args):
    square = jax.ShapeDtypeStruct((BLOCK, BLOCK), F32)
    return pl.pallas_call(
        kernel,
        grid=(1,),
        in_specs=[SMEM] + [pl.BlockSpec(x.shape, lambda i: (0, 0)) for x in args[1:]],
        out_specs=[pl.BlockSpec((BLOCK, BLOCK), lambda i: (0, 0))] * outs,
        out_shape=[square] * outs,
        scratch_shapes=[pltpu.VMEM((BLOCK, BLOCK), F32)] * scratch,
        compiler_params=PARAMS,
        cost_estimate=pl.CostEstimate(flops=20_000_000_000, bytes_accessed=1 << 24, transcendentals=0),
    )(*args)


def hot_t(index, size=BLOCK):
    place = lax.broadcasted_iota(jnp.int32, (size, index.shape[1]), 0)
    return (place == index).astype(F32).astype(B16)


def three(x):
    return jnp.concatenate([x, x, x], 1)


def prepare(flag_ref, cols_ref, rows_ref, contrib_ref, root_ref, out_ref):
    cols = three(hot_t(cols_ref[...]))
    rows = three(hot_t(rows_ref[...]))
    first = nt(whole(nt(cols, whole(contrib_ref[:PICK, :]))), rows)
    third = nt(cols, whole(contrib_ref[PICK:, :]))
    root_a = root_ref[:BLOCK, :].T
    root_b = root_ref[BLOCK:, :].T
    is_first = flag_ref[0] == 0
    out_ref[:, :BLOCK] = first + jnp.where(is_first, root_a, 0.0)
    out_ref[:, BLOCK : 2 * BLOCK] = jnp.where(is_first, root_b, root_a)
    out_ref[:, 2 * BLOCK :] = third


def combine(index_ref, got_ref, out_ref):
    out_ref[:, :BLOCK] = (
        got_ref[0, :, :BLOCK] + got_ref[2, :, :BLOCK] + got_ref[4, :, :BLOCK] + got_ref[6, :, :BLOCK]
    )
    out_ref[:, BLOCK : 2 * BLOCK] = (
        got_ref[1, :, :BLOCK] + got_ref[3, :, :BLOCK] + got_ref[5, :, :BLOCK] + got_ref[7, :, :BLOCK]
        + got_ref[0, :, BLOCK : 2 * BLOCK]
    )
    total = got_ref[1, :, BLOCK : 2 * BLOCK]
    for q in range(NKIDS):
        rows = three(hot_t(index_ref[q : q + 1, :]))
        total = total + nt(whole(got_ref[2 * q, :, 2 * BLOCK :]), rows)
    out_ref[:, 2 * BLOCK :] = total


def extend_add(rows_ref, cols_ref, arrived_ref, root_ref, out_ref, wide_ref):
    for h in range(2):
        total = root_ref[h * BLOCK : (h + 1) * BLOCK, :]
        for q in range(NKIDS):
            cols = three(hot_t(cols_ref[q : q + 1, :]))
            rows = three(hot_t(rows_ref[h, q : q + 1, :]))
            wide = nt(cols, whole(arrived_ref[2 * q + h]))
            wide_ref[q] = nt(rows, whole(wide))
        out_ref[h * BLOCK : (h + 1) * BLOCK, :] = (
            total + ((wide_ref[0] + wide_ref[1]) + (wide_ref[2] + wide_ref[3]))
        )


STEP = 256


def finish(
    place_ref, cols_ref, rows_ref, front_ref, w0_ref, w1_ref, w2_ref, l10_ref, l20_ref, l21_ref,
    d0_ref, d1_ref, d2_ref, out_ref, w3_ref, m10_ref, m2_ref, c3_ref, x_ref, s_ref, raw_ref, sem,
):
    step = pl.program_id(0)
    r = place_ref[0]
    c = place_ref[1]
    sources = (w0_ref, l10_ref, w1_ref, l20_ref, l21_ref, w2_ref)
    copies = [
        pltpu.make_async_copy(src, raw_ref.at[n], sem.at[n]) for n, src in enumerate(sources)
    ]

    @pl.when(step == 0)
    def _():
        for copy in copies:
            copy.start()

    @pl.when(step < 2)
    def _():
        x_ref[...] = cols_ref[...].reshape(STEP, LEAD)

    @pl.when(step >= 2)
    def _():
        turn = 2 * ((step - 2) // 2) + lax.rem(r, 2)
        for z in range(4):
            x_ref[z * STEP // 4 : (z + 1) * STEP // 4, :] = rows_ref[lax.rem(z + turn, 4), 0, 0]

    @pl.when(step == 0)
    def _():
        copies[0].wait()
        w3_ref[0] = right3(raw_ref[0])

    s_ref[:, :BLOCK] = nt(left3(x_ref[:, :BLOCK]), w3_ref[0])

    @pl.when(step == 0)
    def _():
        copies[1].wait()
        m10_ref[...] = right3(raw_ref[1])
        copies[2].wait()
        w3_ref[1] = right3(raw_ref[2])

    s1 = nt(left3(x_ref[:, BLOCK : 2 * BLOCK] - nt(left3(s_ref[:, :BLOCK]), m10_ref[...])), w3_ref[1])
    s_ref[:, BLOCK : 2 * BLOCK] = s1

    @pl.when(step == 0)
    def _():
        copies[3].wait()
        copies[4].wait()
        m2_ref[...] = right3(jnp.concatenate([raw_ref[3], raw_ref[4]], 1))
        copies[5].wait()
        w3_ref[2] = right3(raw_ref[5])

    s2 = nt(left3(x_ref[:, 2 * BLOCK :] - nt(left3(s_ref[:, : 2 * BLOCK]), m2_ref[...])), w3_ref[2])
    s_ref[:, 2 * BLOCK :] = s2

    @pl.when(step < 2)
    def _():
        c3_ref[pl.ds(pl.multiple_of(step * STEP, STEP), STEP), :] = right3(s_ref[...])

    rng = 2 * r + (step - 2) // 2
    half = pl.ds(pl.multiple_of(lax.rem(step, 2) * STEP, STEP), STEP)

    @pl.when((step >= 2) & (c >= PANELS) & (rng >= PANELS))
    def _():
        out_ref[...] = front_ref[...] - nt(left3(s_ref[...]), c3_ref[...])

    @pl.when((step >= 2) & (rng < jnp.minimum(c, PANELS)))
    def _():
        out_ref[...] = jnp.zeros_like(out_ref)

    for p, d_ref in enumerate((d0_ref, d1_ref, d2_ref)):
        @pl.when((step >= 2) & (c == p) & (rng > p))
        def _():
            out_ref[...] = s_ref[:, p * BLOCK : (p + 1) * BLOCK]

        @pl.when((step >= 2) & (c == p) & (rng == p))
        def _():
            pltpu.sync_copy(d_ref.at[half, :], out_ref)


def finish_call(place, col_rows, row_rows, front, mats):
    blocks = lambda i: (jnp.maximum(i - 2, 0), 0)
    return pl.pallas_call(
        finish,
        grid=(6,),
        in_specs=[
            SMEM,
            pl.BlockSpec((4, 1, STEP // 4, LEAD), lambda i: (0, jnp.minimum(i, 1), 0, 0)),
            pl.BlockSpec(
                (4, 1, 1, STEP // 4, LEAD),
                lambda i: (0, jnp.maximum(i - 2, 0) % 2, jnp.maximum(i - 2, 0) // 2, 0, 0),
            ),
            pl.BlockSpec((STEP, BLOCK), blocks),
        ]
        + [pl.BlockSpec(memory_space=pl.ANY)] * 9,
        out_specs=pl.BlockSpec((STEP, BLOCK), blocks),
        out_shape=jax.ShapeDtypeStruct(front.shape, F32),
        scratch_shapes=[
            pltpu.VMEM((3, BLOCK, 3 * BLOCK), B16),
            pltpu.VMEM((BLOCK, 3 * BLOCK), B16),
            pltpu.VMEM((BLOCK, 6 * BLOCK), B16),
            pltpu.VMEM((BLOCK, 9 * BLOCK), B16),
            pltpu.VMEM((STEP, LEAD), F32),
            pltpu.VMEM((STEP, LEAD), F32),
            pltpu.VMEM((6, BLOCK, BLOCK), F32),
            pltpu.SemaphoreType.DMA((6,)),
        ],
        compiler_params=PARAMS,
        cost_estimate=pl.CostEstimate(flops=20_000_000_000, bytes_accessed=24 << 20, transcendentals=0),
    )(place, col_rows, row_rows, front, *mats)


ROW = ("x_hi", "z")
CHIP = ("y", "x_lo")
SHAPE = (2, 4, 4, 2, 2)
COL = CHIP + ("core",)


def spread(a, axis, count):
    return lax.all_to_all(jnp.broadcast_to(a[None], (count,) + a.shape), axis, 0, 0, tiled=True)


def body(root_front, contrib, index_map):
    nr = lax.axis_size(ROW)
    nc = lax.axis_size(COL)
    r = lax.axis_index(ROW)
    c = lax.axis_index(COL)
    rows_loc, cols_loc = root_front.shape
    group = nr // NKIDS
    kid = r // group
    part = r % group
    per = cols_loc // nr
    index = index_map.reshape(NKIDS, -1, PICK) - jnp.arange(CB // PICK, dtype=jnp.int32)[:, None] * BLOCK
    odd = lax.axis_index("core").reshape(1)

    def pick(kid_id, rng):
        return lax.dynamic_slice(index, (kid_id, rng, 0), (1, 1, PICK)).reshape(1, PICK)

    def gather(rows):
        mine = spread(rows, CHIP, nc // 2).reshape(-1, rows.shape[1])
        return mine, lax.ppermute(mine, "core", [(0, 1), (1, 0)])

    with jax.named_scope("slices"):
        outgoing = pl.pallas_call(
            prepare,
            grid=(1,),
            in_specs=[
                SMEM,
                VMEM,
                VMEM,
                pl.BlockSpec((2 * PICK, PICK), lambda i: (0, 0)),
                VMEM,
            ],
            out_specs=VMEM,
            out_shape=jax.ShapeDtypeStruct((cols_loc, 2 * BLOCK + PICK), F32),
            compiler_params=PARAMS,
        )(r.reshape(1), pick(kid, c), pick(kid, part), contrib, root_front)
        got = lax.all_to_all(outgoing.reshape(nr, per, -1), ROW, 0, 0, tiled=True)
        own_slice = pl.pallas_call(
            combine,
            in_specs=[VMEM, VMEM],
            out_specs=VMEM,
            out_shape=jax.ShapeDtypeStruct((per, LEAD), F32),
            compiler_params=PARAMS,
        )(index[:, 2, :], got)

    with jax.named_scope("panel_cols"):
        far = lax.ppermute(own_slice, "x_hi", [(0, 1), (1, 0)])

    with jax.named_scope("lead"):
        pieces = lax.all_to_all(own_slice.reshape(nc // 2, per // (nc // 2), LEAD), CHIP, 0, 0, tiled=True)
        pieces, far, early = lax.optimization_barrier((pieces, far, own_slice))
        top, last = pieces[0], pieces[1]
        even_blocks = [top[:, :BLOCK], top[:, 2 * BLOCK :], last[:, 2 * BLOCK :]]
        odd_blocks = [top[:, BLOCK : 2 * BLOCK], top[:, :BLOCK], top[:, 2 * BLOCK :]]
        strip = jnp.where(odd[0] == 1, jnp.concatenate(odd_blocks, 1), jnp.concatenate(even_blocks, 1))
        strip = spread(strip, ROW, nr).reshape(-1, LEAD)
        mine, other = gather(strip)
        mine, other, own_slice = lax.optimization_barrier((mine, other, own_slice))

    with jax.named_scope("panel_cols"):
        high = lax.axis_index("x_hi") == 1
        pair = jnp.stack([jnp.where(high, far, early), jnp.where(high, early, far)])
        col_rows = lax.all_gather(pair, "z", axis=0, tiled=False)

    with jax.named_scope("panel_rows"):
        perm = []
        for n in range(nr * nc):
            x_hi, z, y, x_lo, core = (int(v) for v in np.unravel_index(n, SHAPE))
            row = y * 2 + x_lo
            to = (row // 4, row % 4, (z + 2 * core + x_lo) % 4, x_hi, core)
            perm.append((n, int(np.ravel_multi_index(to, SHAPE))))
        share = lax.ppermute(own_slice, ROW + COL, perm)

    with jax.named_scope("factor"):
        l00, w0 = factor_call(factor0, 2, 1, odd, mine, other)

    with jax.named_scope("panel_rows"):
        w0, contrib, share = lax.optimization_barrier((w0, contrib, share))
        row_rows = lax.all_gather(share, COL, axis=0, tiled=False)
        row_rows = row_rows.reshape(4, 2, 2, per, LEAD)

    with jax.named_scope("exchange"):
        arrived = lax.all_to_all(contrib.reshape(nr, PICK, PICK), ROW, 0, 0, tiled=True)

    with jax.named_scope("factor"):
        l11, w1, l10 = factor_call(factor1, 3, 2, odd, mine, other, w0)
        l22, w2, l20, l21 = factor_call(factor2, 4, 3, odd, mine, other, w0, w1, l10)

    with jax.named_scope("extend_add"):
        w2, arrived = lax.optimization_barrier((w2, arrived))
        own_rows = lax.dynamic_slice(index, (0, group * r, 0), (NKIDS, group, PICK)).transpose(1, 0, 2)
        own_cols = lax.dynamic_slice(index, (0, c, 0), (NKIDS, 1, PICK)).reshape(NKIDS, PICK)
        front = pl.pallas_call(
            extend_add,
            in_specs=[VMEM] * 4,
            out_specs=VMEM,
            out_shape=jax.ShapeDtypeStruct(root_front.shape, F32),
            scratch_shapes=[pltpu.VMEM((NKIDS, BLOCK, BLOCK), F32)],
            compiler_params=PARAMS,
            cost_estimate=pl.CostEstimate(flops=5_000_000_000, bytes_accessed=6 << 20, transcendentals=0),
        )(own_rows, own_cols, arrived, root_front)

    with jax.named_scope("finish"):
        place = jnp.stack([r, c])
        return finish_call(
            place, col_rows, row_rows, front, (w0, w1, w2, l10, l20, l21, l00, l11, l22)
        )


def solution(mesh):
    torus = Mesh(mesh.devices.reshape(SHAPE), ROW + COL)
    placed = (P(ROW, COL), P(ROW, COL), P())
    return jax.shard_map(
        body, mesh=torus, in_specs=placed, out_specs=P(ROW, COL), check_vma=False
    )
```

time: 382 us -> 280 us (0.73)
  the two profiles are of different devices: /device:TPU:4 before, /device:TPU:7 now
where the time goes in v2:
time: 280 us; the launch traced here: 277 us
  Pallas kernels  128 us (46%)
  waiting for transfers between devices  76 us (27%)
  starting transfers between devices  35.4 us (13%)
  between operations  14 us (5%)
  blocking collectives  12.5 us (4%)
  local copies, waits for them, and re-layouts  7.42 us (3%)
  other arithmetic  3.64 us (1%)
    pallas_call x3, Pallas kernels, factor_call(): pl.pallas_call(kernel, grid=(1,), in_specs=[SMEM] + [pl.BlockSpec(x.shape...  77.3 us
    all_to_all x1, waiting for transfers between devices, spread(): lax.all_to_all(jnp.broadcast_to(a[None], (count,) + a.shape), axis, 0, 0,...  33 us
    pallas_call x1, Pallas kernels, finish_call(): pl.pallas_call(finish, grid=(6,), in_specs=[SMEM, pl.BlockSpec((4, 1, STE...  31.5 us
    all_to_all x1, waiting for transfers between devices, body(): got = lax.all_to_all(outgoing.reshape(nr, per, -1), ROW, 0, 0, tiled=True)  30.9 us
    all_to_all x1, blocking collectives, spread(): lax.all_to_all(jnp.broadcast_to(a[None], (count,) + a.shape), axis, 0, 0,...  12.5 us
    pallas_call x1, Pallas kernels, body(): pl.pallas_call(extend_add, in_specs=[VMEM] * 4, out_specs=VMEM, out_shape...  11 us
    all_to_all x1, waiting for transfers between devices, body(): lax.all_to_all(own_slice.reshape(nc // 2, per // (nc // 2), LEAD), CHIP,...  8.81 us
    all_to_all x1, starting transfers between devices, body(): got = lax.all_to_all(outgoing.reshape(nr, per, -1), ROW, 0, 0, tiled=True)  7.72 us
  transfers between devices with their start and end apart: 9, of which 4 were waited for; matrix products, arithmetic and copies ran while one was open for 2% of the time, Pallas kernels for 32%

profile of v2, /device:TPU:7, one launch (start us, length us, event | category | flops | bytes accessed | tf_op | source)
XLA Modules:
  0.0 276.6 jit_solution(12883032623088136366)
XLA Ops:
  6.5 0.9 broadcast_subtract_fusion
  7.5 0.0 copy-start.5
  7.5 0.6 dynamic-slice_bitcast_fusion.2
  8.1 4.3 %slices.2 = f32[512,1280]{1,0:T(8,128)} custom-call(s32[1]{0:T(128)} %bitcast.flag_ref, s32[1,256]{1,0:T(1,128)} %get-tuple-element.52.cols_ref, s32[1,256]{1,0:T(1,128)} %get-tuple-element.51.rows_ref, f32[2048,256]{1,0:T(8,128)} %contrib_ref.1, f32[1024,512]{1,0:T(8,128)} %root_ref.3), custom_call_target="tpu_custom_call" | custom-call | tf_op jit(solution)/shard_map/slices/pallas_call | solution.py:393
  12.4 7.7 %all-to-all-start = ((f32[8,64,1280]{2,1,0:T(8,128)}), f32[8,64,1280]{2,1,0:T(8,128)S(1)}, u32[]{:S(2)}, u32[]{:S(2)}) async-start(f32[8,64,1280]{2,1,0:T(8,128)} %bitcast.29), calls=%async_computation | async-start | bytes 5242880 | tf_op jit(solution)/shard_map/slices/all_to_all | solution.py:407
  20.1 0.0 copy-done.5
  20.1 0.6 dynamic-slice_bitcast_fusion.1
  20.7 30.9 %all-to-all-done.got_ref = f32[8,64,1280]{2,1,0:T(8,128)S(1)} async-done(((f32[8,64,1280]{2,1,0:T(8,128)}), f32[8,64,1280]{2,1,0:T(8,128)S(1)}, u32[]{:S(2)}, u32[]{:S(2)}) %all-to-all-start) | async-done | bytes 2621472 | tf_op jit(solution)/shard_map/slices/all_to_all | solution.py:407
  51.6 0.0 copy-start
  51.6 1.5 copy-done
  53.1 3.6 %slices.3 = f32[64,1536]{1,0:T(8,128)} custom-call(s32[4,256]{1,0:T(4,128)} %get-tuple-element.50.index_ref, f32[8,64,1280]{2,1,0:T(8,128)} %copy-done), custom_call_target="tpu_custom_call" | custom-call | tf_op jit(solution)/shard_map/slices/pallas_call | solution.py:408
  56.7 0.3 collective-permute-start
  57.0 5.4 %all-to-all-start.1 = ((f32[8,8,1536]{2,1,0:T(8,128)}), f32[8,8,1536]{2,1,0:T(8,128)S(1)}, u32[]{:S(2)}, u32[]{:S(2)}) async-start(f32[8,8,1536]{2,1,0:T(8,128)} %bitcast.30), calls=%async_computation.1 | async-start | bytes 786432 | tf_op jit(solution)/shard_map/lead/all_to_all | solution.py:420
  62.4 8.8 %all-to-all-done.1 = f32[8,8,1536]{2,1,0:T(8,128)S(1)} async-done(((f32[8,8,1536]{2,1,0:T(8,128)}), f32[8,8,1536]{2,1,0:T(8,128)S(1)}, u32[]{:S(2)}, u32[]{:S(2)}) %all-to-all-start.1) | async-done | bytes 393248 | tf_op jit(solution)/shard_map/lead/all_to_all | solution.py:420
  71.2 0.0 collective-permute-done
  71.2 0.0 copy-start.4
  71.3 12.5 %all_to_all.25 = f32[8,8,1536]{2,1,0:T(8,128)S(1)} all-to-all(f32[8,8,1536]{2,1,0:T(8,128)S(1)} %broadcast_in_dim.6), channel_id=1, replica_groups=mesh['x_hi'=2,'z'=4,'y'=4,'x_lo'=2,'core'=2] {'x_hi','z'}, dimensions={0} | all-to-all | bytes 786432 | tf_op jit(solution)/shard_map/lead/all_to_all | solution.py:369
  83.7 2.0 broadcast_in_dim.8
  85.7 0.0 copy-start.1
  85.7 0.0 copy-done.4
  85.8 4.5 %all-to-all-start.3 = ((f32[8,64,1536]{2,1,0:T(8,128)}), f32[8,64,1536]{2,1,0:T(8,128)S(1)}, u32[]{:S(2)}, u32[]{:S(2)}) async-start(f32[8,64,1536]{2,1,0:T(8,128)} %broadcast_in_dim.8), calls=%async_computation.3 | async-start | bytes 6291456 | tf_op jit(solution)/shard_map/lead/all_to_all | solution.py:369
  90.3 0.0 all-gather.5.cloned.1.call-start
  90.3 33.0 %all-to-all-done.3 = f32[8,64,1536]{2,1,0:T(8,128)S(1)} async-done(((f32[8,64,1536]{2,1,0:T(8,128)}), f32[8,64,1536]{2,1,0:T(8,128)S(1)}, u32[]{:S(2)}, u32[]{:S(2)}) %all-to-all-start.3) | async-done | bytes 3145760 | tf_op jit(solution)/shard_map/lead/all_to_all | solution.py:369
  123.3 0.0 copy-start.2
  123.3 5.2 %collective-permute-start.1 = (f32[512,1536]{1,0:T(8,128)S(1)}, f32[512,1536]{1,0:T(8,128)}, u32[]{:S(2)}, u32[]{:S(2)}) collective-permute-start(f32[512,1536]{1,0:T(8,128)S(1)} %bitcast.31), channel_id=1, source_target_pairs={{0,1},{1,0},{2,3},{3,2},{4,5},{5,4},{6,7},{7,6},{8,9},{9,8},{10,11... | collective-permute-start | bytes 9437192 | tf_op jit(solution)/shard_map/lead/ppermute | solution.py:390
  128.5 0.0 copy-done.1
  128.5 1.1 select_bitcast_fusion.1
  129.6 1.0 pad_maximum_fusion
  130.6 0.0 all-gather.5.cloned.1.call-update
  130.7 0.0 all-gather.7.cloned.1.call-start
  130.7 3.2 %collective-permute-done.1.other_ref = f32[512,1536]{1,0:T(8,128)} collective-permute-done((f32[512,1536]{1,0:T(8,128)S(1)}, f32[512,1536]{1,0:T(8,128)}, u32[]{:S(2)}, u32[]{:S(2)}) %collective-permute-start.1) | collective-permute-done | bytes 3145760 | tf_op jit(solution)/shard_map/lead/ppermute | solution.py:390
  134.0 6.2 %collective-permute-start.2 = (f32[64,1536]{1,0:T(8,128)S(1)}, f32[64,1536]{1,0:T(8,128)}, u32[]{:S(2)}, u32[]{:S(2)}) collective-permute-start(f32[64,1536]{1,0:T(8,128)S(1)} %copy-done.1), channel_id=1, source_target_pairs={{0,0},{1,9},{2,20},{3,29},{4,32},{5,41},{6,52},{7,61},{8,64},{9,73... | collective-permute-start | bytes 1179656 | tf_op jit(solution)/shard_map/panel_rows/ppermute | solution.py:442
  140.1 0.0 copy-done.2
  140.1 23.0 %factor.3 = (f32[512,512]{1,0:T(8,128)}, f32[512,512]{1,0:T(8,128)}) custom-call(s32[1]{0:T(128)} %bitcast.11.odd_ref, f32[512,1536]{1,0:T(8,128)} %bitcast.32, f32[512,1536]{1,0:T(8,128)} %collective-permute-done.1.other_ref), custom_call_target="tpu_custom_call" | custom-call | flops 20000000000 | bytes 16777216 | tf_op jit(solution)/shard_map/factor/pallas_call | solution.py:185
  163.1 0.0 collective-permute-done.2
  163.1 0.0 all-gather.7.cloned.1.call-update
  163.2 0.6 pad_add_fusion.place_ref
  163.8 1.3 dynamic-slice_bitcast_fusion.rows_ref
  165.1 6.1 %all-to-all-start.4 = ((f32[8,256,256]{2,1,0:T(8,128)}), f32[8,256,256]{2,1,0:T(8,128)S(1)}, u32[]{:S(2)}, u32[]{:S(2)}) async-start(f32[8,256,256]{2,1,0:T(8,128)} %bitcast.19), calls=%async_computation.4 | async-start | bytes 4194304 | tf_op jit(solution)/shard_map/exchange/all_to_all | solution.py:453
  171.2 25.2 %factor.4 = (f32[512,512]{1,0:T(8,128)}, f32[512,512]{1,0:T(8,128)}, f32[512,512]{1,0:T(8,128)}) custom-call(s32[1]{0:T(128)} %bitcast.11.odd_ref, f32[512,1536]{1,0:T(8,128)} %bitcast.33, f32[512,1536]{1,0:T(8,128)} %collective-permute-done.1.other_ref, f32[512,512]{1,0:T(8,128)} %get-tuple-element.33.w0_ref), custom_call_target="tpu_custom_call" | custom-call | flops 20000000000 | bytes 16777216 | tf_op jit(solution)/shard_map/factor/pallas_call | solution.py:185
  196.4 29.1 %factor.5 = (f32[512,512]{1,0:T(8,128)}, f32[512,512]{1,0:T(8,128)}, f32[512,512]{1,0:T(8,128)}, f32[512,512]{1,0:T(8,128)}) custom-call(s32[1]{0:T(128)} %bitcast.11.odd_ref, f32[512,1536]{1,0:T(8,128)} %bitcast.34, f32[512,1536]{1,0:T(8,128)} %collective-permute-done.1.other_ref, f32[512,512]{1,0:T(8,128)} %get-tuple-element.33.w0_ref, ...), custom_call_target="tpu_custom_call" | custom-call | flops 20000000000 | bytes 16777216 | tf_op jit(solution)/shard_map/factor/pallas_call | solution.py:185
  225.5 0.0 all-to-all-done.4.arrived_ref
  225.5 0.0 copy-start.3
  225.5 1.3 copy-done.3
  226.8 11.0 %extend_add.1.front_ref = f32[1024,512]{1,0:T(8,128)} custom-call(s32[2,4,256]{2,1,0:T(4,128)} %dynamic-slice_bitcast_fusion.rows_ref, s32[4,256]{1,0:T(4,128)} %get-tuple-element.49.cols_ref, f32[8,256,256]{2,1,0:T(8,128)} %copy-done.3, f32[1024,512]{1,0:T(8,128)} %root_ref.3), custom_call_target="tpu_custom_call" | custom-call | flops 5000000000 | bytes 6291456 | tf_op jit(solution)/shard_map/extend_add/pallas_call | solution.py:463
  237.8 0.0 all-gather.5.cloned.1.call-done
  237.8 0.0 all-gather.7.cloned.1.call-done
  237.8 31.5 %finish.1 = f32[1024,512]{1,0:T(8,128)} custom-call(s32[2]{0:T(128)} %pad_add_fusion.place_ref, f32[4,2,64,1536]{3,2,1,0:T(8,128)} %bitcast.38, f32[4,2,2,64,1536]{4,3,2,1,0:T(8,128)} %bitcast.37, f32[1024,512]{1,0:T(8,128)} %extend_add.1.front_ref, f32[512,512]{1,0:T(8,128)} %get-tuple-element.33.w0_ref, f32[512,512]{1,0:T(8,128)} %get-tuple-element.34.w1_ref, ...), custom_call_target="tpu_custom_call" | custom-call | flops 20000000000 | bytes 25165824 | tf_op jit(solution)/shard_map/finish/pallas_call | solution.py:332
  (6 shorter events, 0.1 us)
Async XLA Ops:
  7.5 12.7 %copy-start.5 = (s32[4,16,256]{2,0,1:T(4,128)}, s32[4,16,256]{2,0,1:T(4,128)S(1)}, u32[]{:S(2)}) copy-start(s32[4,16,256]{2,0,1:T(4,128)S(1)} %broadcast_subtract_fusion) | copy-start | bytes 196612
  12.4 39.2 %all-to-all-start = ((f32[8,64,1280]{2,1,0:T(8,128)}), f32[8,64,1280]{2,1,0:T(8,128)S(1)}, u32[]{:S(2)}, u32[]{:S(2)}) async-start(f32[8,64,1280]{2,1,0:T(8,128)} %bitcast.29), calls=%async_computation | async-start | bytes 5242880 | tf_op jit(solution)/shard_map/slices/all_to_all | solution.py:407
  51.6 1.5 copy-start
  56.7 14.5 %collective-permute-start = (f32[64,1536]{1,0:T(8,128)}, f32[64,1536]{1,0:T(8,128)S(1)}, u32[]{:S(2)}, u32[]{:S(2)}) collective-permute-start(f32[64,1536]{1,0:T(8,128)} %slices.3), channel_id=1, source_target_pairs={{0,64},{64,0},{1,65},{65,1},{2,66},{66,2},{3,67},{67,3},{4,68},{68... | collective-permute-start | bytes 1179656 | tf_op jit(solution)/shard_map/panel_cols/ppermute | solution.py:417
  57.0 14.2 %all-to-all-start.1 = ((f32[8,8,1536]{2,1,0:T(8,128)}), f32[8,8,1536]{2,1,0:T(8,128)S(1)}, u32[]{:S(2)}, u32[]{:S(2)}) async-start(f32[8,8,1536]{2,1,0:T(8,128)} %bitcast.30), calls=%async_computation.1 | async-start | bytes 786432 | tf_op jit(solution)/shard_map/lead/all_to_all | solution.py:420
  71.2 14.6 %copy-start.4 = (f32[64,1536]{1,0:T(8,128)}, f32[64,1536]{1,0:T(8,128)S(1)}, u32[]{:S(2)}) copy-start(f32[64,1536]{1,0:T(8,128)S(1)} %collective-permute-done) | copy-start | bytes 1179652
  85.7 42.8 %copy-start.1 = (f32[64,1536]{1,0:T(8,128)S(1)}, f32[64,1536]{1,0:T(8,128)}, u32[]{:S(2)}) copy-start(f32[64,1536]{1,0:T(8,128)} %slices.3) | copy-start | bytes 1179652
  85.8 37.5 %all-to-all-start.3 = ((f32[8,64,1536]{2,1,0:T(8,128)}), f32[8,64,1536]{2,1,0:T(8,128)S(1)}, u32[]{:S(2)}, u32[]{:S(2)}) async-start(f32[8,64,1536]{2,1,0:T(8,128)} %broadcast_in_dim.8), calls=%async_computation.3 | async-start | bytes 6291456 | tf_op jit(solution)/shard_map/lead/all_to_all | solution.py:369
  90.3 147.6 %all-gather.5.cloned.1.call-start = ((), (), s32[]{:S(2)}) async-start(), calls=%async_computation.5 | async-start | bytes 3932160 | tf_op jit(solution)/shard_map/panel_cols/all_gather | solution.py:433
  123.3 16.8 %copy-start.2 = (f32[8,64,1536]{2,1,0:T(8,128)}, f32[8,64,1536]{2,1,0:T(8,128)S(1)}, u32[]{:S(2)}) copy-start(f32[8,64,1536]{2,1,0:T(8,128)S(1)} %all-to-all-done.3) | copy-start | bytes 9437188
  123.3 10.7 %collective-permute-start.1 = (f32[512,1536]{1,0:T(8,128)S(1)}, f32[512,1536]{1,0:T(8,128)}, u32[]{:S(2)}, u32[]{:S(2)}) collective-permute-start(f32[512,1536]{1,0:T(8,128)S(1)} %bitcast.31), channel_id=1, source_target_pairs={{0,1},{1,0},{2,3},{3,2},{4,5},{5,4},{6,7},{7,6},{8,9},{9,8},{10,11... | collective-permute-start | bytes 9437192 | tf_op jit(solution)/shard_map/lead/ppermute | solution.py:390
  130.7 107.2 %all-gather.7.cloned.1.call-start = ((), (), s32[]{:S(2)}) async-start(), calls=%async_computation.6 | async-start | bytes 6684672 | tf_op jit(solution)/shard_map/panel_rows/all_gather | solution.py:449
  134.0 29.2 %collective-permute-start.2 = (f32[64,1536]{1,0:T(8,128)S(1)}, f32[64,1536]{1,0:T(8,128)}, u32[]{:S(2)}, u32[]{:S(2)}) collective-permute-start(f32[64,1536]{1,0:T(8,128)S(1)} %copy-done.1), channel_id=1, source_target_pairs={{0,0},{1,9},{2,20},{3,29},{4,32},{5,41},{6,52},{7,61},{8,64},{9,73... | collective-permute-start | bytes 1179656 | tf_op jit(solution)/shard_map/panel_rows/ppermute | solution.py:442
  165.1 60.5 %all-to-all-start.4 = ((f32[8,256,256]{2,1,0:T(8,128)}), f32[8,256,256]{2,1,0:T(8,128)S(1)}, u32[]{:S(2)}, u32[]{:S(2)}) async-start(f32[8,256,256]{2,1,0:T(8,128)} %bitcast.19), calls=%async_computation.4 | async-start | bytes 4194304 | tf_op jit(solution)/shard_map/exchange/all_to_all | solution.py:453
  225.5 1.3 copy-start.3
Sparse Core Ops, SparseCore 0:
  130.8 41.7 all-gather.4
  174.2 57.3 all-gather.6

commit v3 on v2

v3 whole, which is shorter than its diff:
```python
import jax
import jax.numpy as jnp
from jax import lax
from jax.experimental import pallas as pl
from jax.experimental.pallas import tpu as pltpu
from jax.sharding import Mesh, PartitionSpec as P

CB = 4096
NKIDS = 4
BLOCK = 512
PANELS = 3
PICK = 256
LEAD = BLOCK * PANELS
F32 = jnp.float32
B16 = jnp.bfloat16


def split3(x):
    high = x.astype(B16).astype(F32)
    rest = x - high
    mid = rest.astype(B16).astype(F32)
    return high, mid, rest - mid


def outer_update(lhs, rhs):
    a_high, a_mid, a_low = split3(lhs)
    b_high, b_mid, b_low = split3(rhs)
    a = jnp.concatenate([a_high, a_high, a_mid, a_high, a_low, a_mid], 0).astype(B16)
    b = jnp.concatenate([b_high, b_mid, b_high, b_low, b_high, b_mid], 0).astype(B16)
    return lax.dot_general(a, b, (((0,), (0,)), ((), ())), preferred_element_type=F32)


def factor_tile(rows):
    count = len(rows)
    lane = lax.broadcasted_iota(jnp.int32, (8, 128), 1)
    sub = lax.broadcasted_iota(jnp.int32, (8, 128), 0)
    wide = lambda x: jnp.broadcast_to(x, (8, 128))
    rows = list(rows)
    uppers, inverses = [], []
    for k in range(count):
        c0 = 8 * k
        own = (lane >= c0) & (lane < c0 + 8)
        cur = rows[k]
        top = [wide(cur[:, c0 + j : c0 + j + 1]) for j in range(8)]
        near = range(k + 1, min(k + 3, count))
        lows = [[wide(rows[n][:, c0 + j : c0 + j + 1]) for j in range(8)] for n in near]
        afters = [jnp.where(own, 0.0, rows[n]) for n in near]
        upper = cur
        inv = jnp.where(own, jnp.where(lane - c0 == sub, 1.0, 0.0), cur)
        for j in range(8):
            scale = lax.rsqrt(wide(top[j][j : j + 1, :]))
            mult = jnp.where(sub > j, top[j] * scale, 0.0)
            low_mults = [low[j] * scale for low in lows]
            for m in range(j + 1, 8):
                u = wide(top[m][j : j + 1, :]) * scale
                top[m] = top[m] - mult * u
                for low, low_mult in zip(lows, low_mults):
                    low[m] = low[m] - low_mult * u
            u = wide(upper[j : j + 1, :]) * scale
            upper = jnp.where(sub == j, u, upper - mult * u)
            u = wide(inv[j : j + 1, :]) * scale
            inv = jnp.where(sub == j, u, inv - mult * u)
            afters = [after - low_mult * u for after, low_mult in zip(afters, low_mults)]
        uppers.append(jnp.where(lane - c0 >= sub, upper, 0.0))
        inverses.append(jnp.where(lane < c0 + 8, inv, 0.0))
        for n, after in zip(near, afters):
            rows[n] = after
        if k + 3 < count:
            update = outer_update(jnp.where(lane >= c0 + 24, upper, 0.0), inv)
            for i in range(k + 3, count):
                rows[i] = jnp.where(own, 0.0, rows[i]) - update[8 * i : 8 * i + 8, :]
    return uppers, inverses


def mm(a, b, flip=False):
    dims = (((1,), (1 if flip else 0,)), ((), ()))
    return lax.dot_general(a, b, dims, precision=lax.Precision.HIGHEST, preferred_element_type=F32)


def nt(a, b):
    return lax.dot_general(a, b, (((1,), (1,)), ((), ())), preferred_element_type=F32)


def split2(x):
    high = x.astype(B16)
    return high, (x - high.astype(F32)).astype(B16)


def left3(x):
    high, low = split2(x)
    return jnp.concatenate([high, high, low], 1)


def right3(x):
    high, low = split2(x)
    return jnp.concatenate([high, low, high], 1)


def mm3(a, b):
    return nt(left3(a), right3(b))


def whole(x):
    high, mid, low = split3(x)
    return jnp.concatenate([high, mid, low], 1).astype(B16)


def factor_block(l_ref, w_ref, s_ref):
    size = s_ref.shape[0]
    tiles = size // 128
    l_ref[...] = jnp.zeros_like(l_ref)
    w_ref[...] = jnp.zeros_like(w_ref)
    for k in range(tiles):
        o = 128 * k
        e = o + 128
        rows = [s_ref[o + 8 * i : o + 8 * i + 8, o:e] for i in range(16)]
        uppers, inverses = factor_tile(rows)
        inv = jnp.concatenate(inverses, 0)
        l_ref[o:e, o:e] = jnp.concatenate(uppers, 0).T
        w_ref[o:e, o:e] = inv
        if k + 1 < tiles:
            below = mm(s_ref[e:, o:e], inv, True)
            l_ref[e:, o:e] = below
            s_ref[e:, e:] = s_ref[e:, e:] - mm(below, below, True)
    half = 128
    while half < size:
        for o in range(0, size, 2 * half):
            m = o + half
            e = m + half
            t = mm(l_ref[m:e, o:m], w_ref[o:m, o:m])
            w_ref[m:e, o:m] = -mm(w_ref[m:e, m:e], t)
        half *= 2


def put_rows(dst, a_ref, b_ref, second, col):
    for q in range(8):
        for i in range(8):
            src = slice(64 * q + 8 * i, 64 * q + 8 * i + 8)
            cols = slice(col, col + BLOCK)
            dst[64 * i + 8 * q : 64 * i + 8 * q + 8, :] = jnp.where(second, b_ref[src, cols], a_ref[src, cols])


def factor0(odd_ref, mine_ref, other_ref, l_ref, w_ref, s_ref):
    put_rows(s_ref, mine_ref, other_ref, odd_ref[0] == 1, 0)
    factor_block(l_ref, w_ref, s_ref)


def factor1(odd_ref, mine1_ref, other1_ref, mine2_ref, other2_ref, w0_ref, l_ref, w_ref, l10_ref, s_ref, x_ref):
    even = odd_ref[0] == 0
    put_rows(x_ref, mine2_ref, other2_ref, even, 0)
    put_rows(s_ref, mine1_ref, other1_ref, even, 0)
    l10 = mm3(x_ref[...], w0_ref[...])
    l10_ref[...] = l10
    s_ref[...] = s_ref[...] - mm3(l10, l10)
    factor_block(l_ref, w_ref, s_ref)


def factor2(
    odd_ref, mine_ref, other_ref, w0_ref, w1_ref, l10_ref,
    l_ref, w_ref, l20_ref, l21_ref, s_ref, x_ref, y_ref,
):
    odd = odd_ref[0] == 1
    put_rows(x_ref, mine_ref, other_ref, odd, 0)
    put_rows(y_ref, mine_ref, other_ref, jnp.logical_not(odd), BLOCK)
    put_rows(s_ref, mine_ref, other_ref, odd, BLOCK)
    l20 = mm3(x_ref[...].T, w0_ref[...])
    l20_ref[...] = l20
    l21 = mm3(y_ref[...].T - mm3(l20, l10_ref[...]), w1_ref[...])
    l21_ref[...] = l21
    both = jnp.concatenate([l20, l21], 1)
    s_ref[...] = s_ref[...] - mm3(both, both)
    factor_block(l_ref, w_ref, s_ref)


VMEM = pl.BlockSpec(memory_space=pltpu.VMEM)
SMEM = pl.BlockSpec(memory_space=pltpu.SMEM)
PARAMS = pltpu.CompilerParams(vmem_limit_bytes=60 << 20)


def factor_call(kernel, outs, scratch, *args):
    square = jax.ShapeDtypeStruct((BLOCK, BLOCK), F32)
    return pl.pallas_call(
        kernel,
        grid=(1,),
        in_specs=[SMEM] + [pl.BlockSpec(x.shape, lambda i: (0, 0)) for x in args[1:]],
        out_specs=[pl.BlockSpec((BLOCK, BLOCK), lambda i: (0, 0))] * outs,
        out_shape=[square] * outs,
        scratch_shapes=[pltpu.VMEM((BLOCK, BLOCK), F32)] * scratch,
        compiler_params=PARAMS,
        cost_estimate=pl.CostEstimate(flops=20_000_000_000, bytes_accessed=1 << 24, transcendentals=0),
    )(*args)


def hot_t(index, size=BLOCK):
    place = lax.broadcasted_iota(jnp.int32, (size, index.shape[1]), 0)
    return (place == index).astype(F32).astype(B16)


def three(x):
    return jnp.concatenate([x, x, x], 1)


def prepare(flag_ref, cols_ref, rows_ref, contrib_ref, root_ref, out_ref):
    cols = three(hot_t(cols_ref[...]))
    rows = three(hot_t(rows_ref[...]))
    first = nt(whole(nt(cols, whole(contrib_ref[:PICK, :]))), rows)
    third = nt(cols, whole(contrib_ref[PICK:, :]))
    root_a = root_ref[:BLOCK, :].T
    root_b = root_ref[BLOCK:, :].T
    is_first = flag_ref[0] == 0
    out_ref[:, :BLOCK] = first + jnp.where(is_first, root_a, 0.0)
    out_ref[:, BLOCK : 2 * BLOCK] = jnp.where(is_first, root_b, root_a)
    out_ref[:, 2 * BLOCK :] = third


def combine(index_ref, first_ref, second_ref, third_ref, out_ref):
    out_ref[:, :BLOCK] = (first_ref[0] + first_ref[2]) + (first_ref[4] + first_ref[6])
    out_ref[:, BLOCK : 2 * BLOCK] = (
        (first_ref[1] + first_ref[3]) + (first_ref[5] + first_ref[7]) + second_ref[0]
    )
    total = second_ref[1]
    for q in range(NKIDS):
        total = total + nt(whole(third_ref[2 * q]), three(hot_t(index_ref[q : q + 1, :])))
    out_ref[:, 2 * BLOCK :] = total


def two(x):
    return jnp.concatenate([x, x], 1)


def finish(
    place_ref, cols_ref, rows_ref, front_ref, arrived_ref, row_hot_ref, col_hot_ref, w0_ref, w1_ref, w2_ref, l10_ref, l20_ref, l21_ref,
    d0_ref, d1_ref, d2_ref, out_ref, w3_ref, m10_ref, m2_ref, c3_ref, x_ref, s_ref, raw_ref, sem,
):
    step = pl.program_id(0)
    r = place_ref[0]
    c = place_ref[1]
    part = x_ref.shape[0] // 8
    sources = (w0_ref, l10_ref, w1_ref, l20_ref, l21_ref, w2_ref)
    copies = [
        pltpu.make_async_copy(src, raw_ref.at[n], sem.at[n]) for n, src in enumerate(sources)
    ]

    @pl.when(step == 0)
    def _():
        for copy in copies:
            copy.start()
        for n in range(8):
            x_ref[n * part : (n + 1) * part, :] = cols_ref[n % 4, n // 4]

    @pl.when(step > 0)
    def _():
        for q in range(8):
            for n in range(8):
                to = n * part + 8 * q
                x_ref[to : to + 8, :] = rows_ref[q, 0, 8 * n : 8 * n + 8, :]

    @pl.when(step == 0)
    def _():
        copies[0].wait()
        w3_ref[0] = right3(raw_ref[0])

    s_ref[:, :BLOCK] = nt(left3(x_ref[:, :BLOCK]), w3_ref[0])

    @pl.when(step == 0)
    def _():
        copies[1].wait()
        m10_ref[...] = right3(raw_ref[1])
        copies[2].wait()
        w3_ref[1] = right3(raw_ref[2])

    s1 = nt(left3(x_ref[:, BLOCK : 2 * BLOCK] - nt(left3(s_ref[:, :BLOCK]), m10_ref[...])), w3_ref[1])
    s_ref[:, BLOCK : 2 * BLOCK] = s1

    @pl.when(step == 0)
    def _():
        copies[3].wait()
        copies[4].wait()
        m2_ref[...] = right3(jnp.concatenate([raw_ref[3], raw_ref[4]], 1))
        copies[5].wait()
        w3_ref[2] = right3(raw_ref[5])

    s2 = nt(left3(x_ref[:, 2 * BLOCK :] - nt(left3(s_ref[:, : 2 * BLOCK]), m2_ref[...])), w3_ref[2])
    s_ref[:, 2 * BLOCK :] = s2

    @pl.when(step == 0)
    def _():
        c3_ref[...] = right3(s_ref[...])

    rng = 2 * r + step - 1

    @pl.when((step > 0) & (c >= PANELS) & (rng >= PANELS))
    def _():
        total = front_ref[...]
        for q in range(NKIDS):
            cols = two(hot_t(col_hot_ref[q : q + 1, :]))
            rows = two(hot_t(row_hot_ref[step - 1, q : q + 1, :]))
            spread_cols = nt(cols, jnp.concatenate(split2(arrived_ref[q, 0]), 1))
            total = total + nt(rows, jnp.concatenate(split2(spread_cols), 1))
        out_ref[...] = total - nt(left3(s_ref[...]), c3_ref[...])

    @pl.when((step > 0) & (rng < jnp.minimum(c, PANELS)))
    def _():
        out_ref[...] = jnp.zeros_like(out_ref)

    for p, d_ref in enumerate((d0_ref, d1_ref, d2_ref)):
        @pl.when((step > 0) & (c == p) & (rng > p))
        def _():
            out_ref[...] = s_ref[:, p * BLOCK : (p + 1) * BLOCK]

        @pl.when((step > 0) & (c == p) & (rng == p))
        def _():
            pltpu.sync_copy(d_ref, out_ref)


def finish_call(place, col_rows, row_rows, front, arrived, row_hot, col_hot, mats):
    half = lambda i: jnp.maximum(i - 1, 0)
    return pl.pallas_call(
        finish,
        grid=(3,),
        in_specs=[
            SMEM,
            pl.BlockSpec((4, 2, BLOCK // 8, LEAD), lambda i: (0, 0, 0, 0)),
            pl.BlockSpec((8, 1, BLOCK // 8, LEAD), lambda i: (0, half(i), 0, 0)),
            pl.BlockSpec((BLOCK, BLOCK), lambda i: (half(i), 0)),
            pl.BlockSpec((NKIDS, 1, PICK, PICK), lambda i: (0, half(i), 0, 0)),
            VMEM,
            VMEM,
        ]
        + [pl.BlockSpec(memory_space=pl.ANY)] * 9,
        out_specs=pl.BlockSpec((BLOCK, BLOCK), lambda i: (half(i), 0)),
        out_shape=jax.ShapeDtypeStruct(front.shape, F32),
        scratch_shapes=[
            pltpu.VMEM((3, BLOCK, 3 * BLOCK), B16),
            pltpu.VMEM((BLOCK, 3 * BLOCK), B16),
            pltpu.VMEM((BLOCK, 6 * BLOCK), B16),
            pltpu.VMEM((BLOCK, 9 * BLOCK), B16),
            pltpu.VMEM((BLOCK, LEAD), F32),
            pltpu.VMEM((BLOCK, LEAD), F32),
            pltpu.VMEM((6, BLOCK, BLOCK), F32),
            pltpu.SemaphoreType.DMA((6,)),
        ],
        compiler_params=PARAMS,
        cost_estimate=pl.CostEstimate(flops=20_000_000_000, bytes_accessed=24 << 20, transcendentals=0),
    )(place, col_rows, row_rows, front, arrived, row_hot, col_hot, *mats)


ROW = ("x_hi", "z")
CHIP = ("y", "x_lo")
SHAPE = (2, 4, 4, 2, 2)
COL = CHIP + ("core",)


def copies_of(a, count):
    return jnp.broadcast_to(a[None], (count,) + a.shape)


def spread(a, axis, count):
    return lax.all_to_all(copies_of(a, count), axis, 0, 0, tiled=True)


def body(root_front, contrib, index_map):
    nr = lax.axis_size(ROW)
    nc = lax.axis_size(COL)
    r = lax.axis_index(ROW)
    c = lax.axis_index(COL)
    rows_loc, cols_loc = root_front.shape
    group = nr // NKIDS
    kid = r // group
    part = r % group
    per = cols_loc // nr
    index = index_map.reshape(NKIDS, -1, PICK) - jnp.arange(CB // PICK, dtype=jnp.int32)[:, None] * BLOCK
    odd = lax.axis_index("core").reshape(1)

    def pick(kid_id, rng):
        return lax.dynamic_slice(index, (kid_id, rng, 0), (1, 1, PICK)).reshape(1, PICK)

    def swap(rows):
        return lax.ppermute(rows, "core", [(0, 1), (1, 0)])

    with jax.named_scope("slices"):
        outgoing = pl.pallas_call(
            prepare,
            grid=(1,),
            in_specs=[
                SMEM,
                VMEM,
                VMEM,
                pl.BlockSpec((2 * PICK, PICK), lambda i: (0, 0)),
                VMEM,
            ],
            out_specs=VMEM,
            out_shape=jax.ShapeDtypeStruct((cols_loc, 2 * BLOCK + PICK), F32),
            compiler_params=PARAMS,
        )(r.reshape(1), pick(kid, c), pick(kid, part), contrib, root_front)
        got = lax.all_to_all(outgoing.reshape(nr, per, -1), ROW, 0, 0, tiled=True)
        own_slice = pl.pallas_call(
            combine,
            grid=(1,),
            in_specs=[
                VMEM,
                pl.BlockSpec((nr, per, BLOCK), lambda i: (0, 0, 0)),
                pl.BlockSpec((2, per, BLOCK), lambda i: (0, 0, 1)),
                pl.BlockSpec((nr, per, PICK), lambda i: (0, 0, 2 * BLOCK // PICK)),
            ],
            out_specs=VMEM,
            out_shape=jax.ShapeDtypeStruct((per, LEAD), F32),
            compiler_params=PARAMS,
        )(index[:, 2, :], got, got, got)

    with jax.named_scope("panel_cols"):
        far = lax.ppermute(own_slice, "x_hi", [(0, 1), (1, 0)])

    with jax.named_scope("lead"):
        pieces = lax.all_to_all(own_slice.reshape(nc // 2, per // (nc // 2), LEAD), CHIP, 0, 0, tiled=True)
        pieces, far, early = lax.optimization_barrier((pieces, far, own_slice))
        top, last = pieces[0], pieces[1]
        even_blocks = [top[:, :BLOCK], top[:, 2 * BLOCK :], last[:, 2 * BLOCK :]]
        odd_blocks = [top[:, BLOCK : 2 * BLOCK], top[:, :BLOCK], top[:, 2 * BLOCK :]]
        strip = jnp.where(odd[0] == 1, jnp.concatenate(odd_blocks, 1), jnp.concatenate(even_blocks, 1))
        both = jnp.concatenate([copies_of(strip, nr), pieces], 1)
        both = lax.all_to_all(both, ROW, 0, 0, tiled=True)
        strip = both[:, : pieces.shape[1]].reshape(-1, LEAD)
        share = both[:, pieces.shape[1] :].reshape(-1, LEAD)
        mine1 = spread(strip[:, :BLOCK], CHIP, nc // 2).reshape(-1, BLOCK)
        other1 = swap(mine1)
        fan = copies_of(strip[:, BLOCK:], nc // 2)
        mine1, other1, fan = lax.optimization_barrier((mine1, other1, fan))
        mine2 = lax.all_to_all(fan, CHIP, 0, 0, tiled=True).reshape(-1, 2 * BLOCK)

    with jax.named_scope("panel_cols"):
        high = lax.axis_index("x_hi") == 1
        pair = jnp.stack([jnp.where(high, far, early), jnp.where(high, early, far)])
        col_rows = lax.all_gather(pair, "z", axis=0, tiled=False)

    with jax.named_scope("factor"):
        l00, w0 = factor_call(factor0, 2, 1, odd, mine1, other1)

    with jax.named_scope("panel_rows"):
        w0, contrib, mine2, share = lax.optimization_barrier((w0, contrib, mine2, share))
        other2 = swap(mine2)
        row_rows = lax.all_gather(share, COL, axis=0, tiled=False)
        row_rows = row_rows.reshape(nc // 2, 2, per, LEAD)

    with jax.named_scope("exchange"):
        arrived = lax.all_to_all(contrib.reshape(nr, PICK, PICK), ROW, 0, 0, tiled=True)

    with jax.named_scope("factor"):
        l11, w1, l10 = factor_call(factor1, 3, 2, odd, mine1, other1, mine2, other2, w0)
        l22, w2, l20, l21 = factor_call(factor2, 4, 3, odd, mine2, other2, w0, w1, l10)

    with jax.named_scope("finish"):
        row_hot = lax.dynamic_slice(index, (0, group * r, 0), (NKIDS, group, PICK)).transpose(1, 0, 2)
        col_hot = lax.dynamic_slice(index, (0, c, 0), (NKIDS, 1, PICK)).reshape(NKIDS, PICK)
        return finish_call(
            jnp.stack([r, c]),
            col_rows,
            row_rows,
            root_front,
            arrived.reshape(NKIDS, group, PICK, PICK),
            row_hot,
            col_hot,
            (w0, w1, w2, l10, l20, l21, l00, l11, l22),
        )


def solution(mesh):
    torus = Mesh(mesh.devices.reshape(SHAPE), ROW + COL)
    placed = (P(ROW, COL), P(ROW, COL), P())
    return jax.shard_map(
        body, mesh=torus, in_specs=placed, out_specs=P(ROW, COL), check_vma=False
    )
```

time: 280 us -> 255 us (0.911)
  Pallas kernels: 128 us -> 113 us
  waiting for transfers between devices: 76 us -> 62.4 us
  blocking collectives: 12.5 us -> 17.6 us
    all_to_all x1 -> x2, waiting for transfers between devices: 33 us -> 15.9 us  [the longest x1 10.8 us: body(): both = lax.all_to_all(both, ROW, 0, 0, tiled=True)]
    pallas_call x3 -> x2, Pallas kernels: 46 us -> 37.6 us  [the longest x1 34.3 us: finish_call(): pl.pallas_call(finish, grid=(3,), in_specs=[SMEM, pl.BlockSpec((4, 2, BLO...]
    ppermute x2, starting transfers between devices: 11.4 us -> 3.35 us  [swap(): return lax.ppermute(rows, 'core', [(0, 1), (1, 0)])]
    all_to_all x1 -> x2, starting transfers between devices: 4.51 us -> 11.6 us  [the longest x1 7.16 us: body(): both = lax.all_to_all(both, ROW, 0, 0, tiled=True)]
    pallas_call x3, Pallas kernels: 77.3 us -> 71.6 us  [factor_call(): pl.pallas_call(kernel, grid=(1,), in_specs=[SMEM] + [pl.BlockSpec(x.shape...]
    all_to_all x1, blocking collectives: 12.5 us -> 17.6 us  [spread(): return lax.all_to_all(copies_of(a, count), axis, 0, 0, tiled=True)]
    all_gather x1, waiting for transfers between devices: 0.01 us -> 4.44 us  [body(): row_rows = lax.all_gather(share, COL, axis=0, tiled=False)]
  transfers between devices with their start and end apart: 9 -> 10, of which waited for: 4 -> 6; matrix products, arithmetic and copies ran while one was open for 2% -> 2% of each run, Pallas kernels for 32% -> 29%
where the time goes in v3:
time: 255 us; the launch traced here: 251 us
  Pallas kernels  113 us (44%)
  waiting for transfers between devices  62.4 us (24%)
  starting transfers between devices  34.5 us (14%)
  blocking collectives  17.6 us (7%)
  between operations  13.7 us (5%)
  local copies, waits for them, and re-layouts  5.85 us (2%)
  other arithmetic  3.51 us (1%)
    pallas_call x3, Pallas kernels, factor_call(): pl.pallas_call(kernel, grid=(1,), in_specs=[SMEM] + [pl.BlockSpec(x.shape...  71.6 us
    pallas_call x1, Pallas kernels, finish_call(): pl.pallas_call(finish, grid=(3,), in_specs=[SMEM, pl.BlockSpec((4, 2, BLO...  34.3 us
    all_to_all x1, waiting for transfers between devices, body(): got = lax.all_to_all(outgoing.reshape(nr, per, -1), ROW, 0, 0, tiled=True)  30.9 us
    all_to_all x1, blocking collectives, spread(): return lax.all_to_all(copies_of(a, count), axis, 0, 0, tiled=True)  17.6 us
    all_to_all x1, waiting for transfers between devices, body(): both = lax.all_to_all(both, ROW, 0, 0, tiled=True)  10.8 us
    all_to_all x1, waiting for transfers between devices, body(): lax.all_to_all(own_slice.reshape(nc // 2, per // (nc // 2), LEAD), CHIP,...  8.8 us
    all_to_all x1, starting transfers between devices, body(): got = lax.all_to_all(outgoing.reshape(nr, per, -1), ROW, 0, 0, tiled=True)  7.72 us
    all_to_all x1, starting transfers between devices, body(): both = lax.all_to_all(both, ROW, 0, 0, tiled=True)  7.16 us
  transfers between devices with their start and end apart: 10, of which 6 were waited for; matrix products, arithmetic and copies ran while one was open for 2% of the time, Pallas kernels for 29%

profile of v3, /device:TPU:7, one launch (start us, length us, event | category | flops | bytes accessed | tf_op | source)
XLA Modules:
  0.0 251.0 jit_solution(3580898779209483207)
XLA Ops:
  6.5 0.9 broadcast_subtract_fusion
  7.5 0.6 dynamic-slice_bitcast_fusion.2
  8.1 4.3 %slices.2 = f32[512,1280]{1,0:T(8,128)} custom-call(s32[1]{0:T(128)} %bitcast.flag_ref, s32[1,256]{1,0:T(1,128)} %get-tuple-element.52.cols_ref, s32[1,256]{1,0:T(1,128)} %get-tuple-element.51.rows_ref, f32[2048,256]{1,0:T(8,128)} %contrib_ref.1, f32[1024,512]{1,0:T(8,128)} %front_ref.1), custom_call_target="tpu_custom_call" | custom-call | tf_op jit(solution)/shard_map/slices/pallas_call | solution.py:382
  12.4 7.7 %all-to-all-start = ((f32[8,64,1280]{2,1,0:T(8,128)}), f32[8,64,1280]{2,1,0:T(8,128)S(1)}, u32[]{:S(2)}, u32[]{:S(2)}) async-start(f32[8,64,1280]{2,1,0:T(8,128)} %bitcast.34), calls=%async_computation | async-start | bytes 5242880 | tf_op jit(solution)/shard_map/slices/all_to_all | solution.py:396
  20.1 0.6 dynamic-slice_bitcast_fusion.1
  20.7 30.9 %all-to-all-done.first_ref.second_ref.third_ref = f32[8,64,1280]{2,1,0:T(8,128)S(1)} async-done(((f32[8,64,1280]{2,1,0:T(8,128)}), f32[8,64,1280]{2,1,0:T(8,128)S(1)}, u32[]{:S(2)}, u32[]{:S(2)}) %all-to-all-start) | async-done | bytes 2621472 | tf_op jit(solution)/shard_map/slices/all_to_all | solution.py:396
  51.6 0.0 copy-start
  51.6 1.5 copy-done
  53.1 3.3 %slices.3 = f32[64,1536]{1,0:T(8,128)} custom-call(s32[4,256]{1,0:T(4,128)} %get-tuple-element.50.index_ref, f32[8,64,1280]{2,1,0:T(8,128)} %copy-done, f32[8,64,1280]{2,1,0:T(8,128)} %copy-done, f32[8,64,1280]{2,1,0:T(8,128)} %copy-done), custom_call_target="tpu_custom_call" | custom-call | tf_op jit(solution)/shard_map/slices/pallas_call | solution.py:397
  56.4 0.3 collective-permute-start
  56.6 5.4 %all-to-all-start.1 = ((f32[8,8,1536]{2,1,0:T(8,128)}), f32[8,8,1536]{2,1,0:T(8,128)S(1)}, u32[]{:S(2)}, u32[]{:S(2)}) async-start(f32[8,8,1536]{2,1,0:T(8,128)} %bitcast.35), calls=%async_computation.1 | async-start | bytes 786432 | tf_op jit(solution)/shard_map/lead/all_to_all | solution.py:415
  62.0 0.0 copy-start.1
  62.0 8.8 %all-to-all-done.1 = f32[8,8,1536]{2,1,0:T(8,128)S(1)} async-done(((f32[8,8,1536]{2,1,0:T(8,128)}), f32[8,8,1536]{2,1,0:T(8,128)S(1)}, u32[]{:S(2)}, u32[]{:S(2)}) %all-to-all-start.1) | async-done | bytes 393248 | tf_op jit(solution)/shard_map/lead/all_to_all | solution.py:415
  70.8 0.0 collective-permute-done
  70.9 0.9 pad_maximum_fusion.1
  71.9 7.2 %all-to-all-start.2 = ((f32[8,16,1536]{2,1,0:T(8,128)}), f32[8,16,1536]{2,1,0:T(8,128)S(1)}, u32[]{:S(2)}, u32[]{:S(2)}) async-start(f32[8,16,1536]{2,1,0:T(8,128)} %pad_maximum_fusion.1), calls=%async_computation.2 | async-start | bytes 1572864 | tf_op jit(solution)/shard_map/lead/all_to_all | solution.py:422
  79.0 0.0 all-gather.5.cloned.1.call-start
  79.0 0.0 copy-done.1
  79.0 0.1 select_bitcast_fusion.1
  79.1 1.0 pad_maximum_fusion
  80.1 0.0 all-gather.5.cloned.1.call-update
  80.1 10.8 %all-to-all-done.2 = f32[8,16,1536]{2,1,0:T(8,128)S(1)} async-done(((f32[8,16,1536]{2,1,0:T(8,128)}), f32[8,16,1536]{2,1,0:T(8,128)S(1)}, u32[]{:S(2)}, u32[]{:S(2)}) %all-to-all-start.2) | async-done | bytes 786464 | tf_op jit(solution)/shard_map/lead/all_to_all | solution.py:422
  90.8 0.8 slice_bitcast_fusion
  91.6 0.1 broadcast_in_dim.7
  91.8 17.6 %all_to_all.30 = f32[8,64,512]{2,1,0:T(8,128)S(1)} all-to-all(f32[8,64,512]{2,1,0:T(8,128)S(1)} %broadcast_in_dim.7), channel_id=1, replica_groups=mesh['x_hi'=2,'z'=4,'y'=4,'x_lo'=2,'core'=2] {'y','x_lo'}, dimensions={0} | all-to-all | bytes 2097152 | tf_op jit(solution)/shard_map/lead/all_to_all | solution.py:359
  109.3 0.0 copy-start.3
  109.3 2.1 collective-permute-start.1
  111.4 2.4 collective-permute-done.1.other_ref.other1_ref
  113.8 1.6 broadcast_in_dim.8
  115.4 0.0 copy-done.3
  115.4 4.4 %all-to-all-start.4 = ((f32[8,64,1024]{2,1,0:T(8,128)}), f32[8,64,1024]{2,1,0:T(8,128)S(1)}, u32[]{:S(2)}, u32[]{:S(2)}) async-start(f32[8,64,1024]{2,1,0:T(8,128)} %broadcast_in_dim.8), calls=%async_computation.4 | async-start | bytes 4194304 | tf_op jit(solution)/shard_map/lead/all_to_all | solution.py:429
  119.8 0.5 all-gather.7.cloned.1.call-start
  120.3 20.2 %factor.3 = (f32[512,512]{1,0:T(8,128)}, f32[512,512]{1,0:T(8,128)}) custom-call(s32[1]{0:T(128)} %bitcast.11.odd_ref, f32[512,512]{1,0:T(8,128)} %bitcast.40, f32[512,512]{1,0:T(8,128)} %collective-permute-done.1.other_ref.other1_ref), custom_call_target="tpu_custom_call" | custom-call | flops 20000000000 | bytes 16777216 | tf_op jit(solution)/shard_map/factor/pallas_call | solution.py:182
  140.5 5.1 %all-to-all-done.4 = f32[8,64,1024]{2,1,0:T(8,128)S(1)} async-done(((f32[8,64,1024]{2,1,0:T(8,128)}), f32[8,64,1024]{2,1,0:T(8,128)S(1)}, u32[]{:S(2)}, u32[]{:S(2)}) %all-to-all-start.4) | async-done | bytes 2097184 | tf_op jit(solution)/shard_map/lead/all_to_all | solution.py:429
  145.6 0.0 copy-start.2
  145.6 0.0 all-gather.7.cloned.1.call-update
  145.7 1.3 collective-permute-start.2
  146.9 0.6 pad_add_fusion.place_ref
  147.6 0.6 dynamic-slice_bitcast_fusion.row_hot_ref
  148.1 0.0 copy-done.2
  148.2 5.7 %all-to-all-start.5 = ((f32[8,256,256]{2,1,0:T(8,128)}), f32[8,256,256]{2,1,0:T(8,128)}, u32[]{:S(2)}, u32[]{:S(2)}) async-start(f32[8,256,256]{2,1,0:T(8,128)} %bitcast.19), calls=%async_computation.5 | async-start | bytes 4194304 | tf_op jit(solution)/shard_map/exchange/all_to_all | solution.py:446
  153.9 0.0 collective-permute-done.2.other2_ref.other_ref
  153.9 24.6 %factor.4 = (f32[512,512]{1,0:T(8,128)}, f32[512,512]{1,0:T(8,128)}, f32[512,512]{1,0:T(8,128)}) custom-call(s32[1]{0:T(128)} %bitcast.11.odd_ref, f32[512,512]{1,0:T(8,128)} %bitcast.41, f32[512,512]{1,0:T(8,128)} %collective-permute-done.1.other_ref.other1_ref, f32[512,1024]{1,0:T(8,128)} %bitcast.37, ...), custom_call_target="tpu_custom_call" | custom-call | flops 20000000000 | bytes 16777216 | tf_op jit(solution)/shard_map/factor/pallas_call | solution.py:182
  178.5 26.7 %factor.5 = (f32[512,512]{1,0:T(8,128)}, f32[512,512]{1,0:T(8,128)}, f32[512,512]{1,0:T(8,128)}, f32[512,512]{1,0:T(8,128)}) custom-call(s32[1]{0:T(128)} %bitcast.11.odd_ref, f32[512,1024]{1,0:T(8,128)} %bitcast.38, f32[512,1024]{1,0:T(8,128)} %collective-permute-done.2.other2_ref.other_ref, f32[512,512]{1,0:T(8,128)} %get-tuple-element.33.w0_ref, ...), custom_call_target="tpu_custom_call" | custom-call | flops 20000000000 | bytes 16777216 | tf_op jit(solution)/shard_map/factor/pallas_call | solution.py:182
  205.2 0.0 all-gather.5.cloned.1.call-done
  205.2 0.0 all-to-all-done.5
  205.2 4.4 %all-gather.7.cloned.1.call-done = f32[1024,1536]{1,0:T(8,128)} async-done(((f32[64,1536]{1,0:T(8,128)}), f32[1024,1536]{1,0:T(8,128)}) %all-gather.7.cloned.1.call-update) | async-done | bytes 6291472 | tf_op jit(solution)/shard_map/panel_rows/all_gather | solution.py:442
  209.7 34.3 %finish.1 = f32[1024,512]{1,0:T(8,128)} custom-call(s32[2]{0:T(128)} %pad_add_fusion.place_ref, f32[4,2,64,1536]{3,2,1,0:T(8,128)} %bitcast.44, f32[8,2,64,1536]{3,2,1,0:T(8,128)} %bitcast.43, f32[1024,512]{1,0:T(8,128)} %front_ref.1, f32[4,2,256,256]{3,2,1,0:T(8,128)} %bitcast.20.arrived_ref, s32[2,4,256]{2,1,0:T(4,128)} %dynamic-slice_bitcast_fusion.row_hot_ref, ...), custom_call_target="tpu_custom_call" | custom-call | flops 20000000000 | bytes 25165824 | tf_op jit(solution)/shard_map/finish/pallas_call | solution.py:318
  (8 shorter events, 0.1 us)
Async XLA Ops:
  12.4 39.2 %all-to-all-start = ((f32[8,64,1280]{2,1,0:T(8,128)}), f32[8,64,1280]{2,1,0:T(8,128)S(1)}, u32[]{:S(2)}, u32[]{:S(2)}) async-start(f32[8,64,1280]{2,1,0:T(8,128)} %bitcast.34), calls=%async_computation | async-start | bytes 5242880 | tf_op jit(solution)/shard_map/slices/all_to_all | solution.py:396
  51.6 1.5 copy-start
  56.4 14.5 %collective-permute-start = (f32[64,1536]{1,0:T(8,128)}, f32[64,1536]{1,0:T(8,128)S(1)}, u32[]{:S(2)}, u32[]{:S(2)}) collective-permute-start(f32[64,1536]{1,0:T(8,128)} %slices.3), channel_id=1, source_target_pairs={{0,64},{64,0},{1,65},{65,1},{2,66},{66,2},{3,67},{67,3},{4,68},{68... | collective-permute-start | bytes 1179656 | tf_op jit(solution)/shard_map/panel_cols/ppermute | solution.py:412
  56.6 14.2 %all-to-all-start.1 = ((f32[8,8,1536]{2,1,0:T(8,128)}), f32[8,8,1536]{2,1,0:T(8,128)S(1)}, u32[]{:S(2)}, u32[]{:S(2)}) async-start(f32[8,8,1536]{2,1,0:T(8,128)} %bitcast.35), calls=%async_computation.1 | async-start | bytes 786432 | tf_op jit(solution)/shard_map/lead/all_to_all | solution.py:415
  62.0 17.0 %copy-start.1 = (f32[64,1536]{1,0:T(8,128)S(1)}, f32[64,1536]{1,0:T(8,128)}, u32[]{:S(2)}) copy-start(f32[64,1536]{1,0:T(8,128)} %slices.3) | copy-start | bytes 1179652
  71.9 19.0 %all-to-all-start.2 = ((f32[8,16,1536]{2,1,0:T(8,128)}), f32[8,16,1536]{2,1,0:T(8,128)S(1)}, u32[]{:S(2)}, u32[]{:S(2)}) async-start(f32[8,16,1536]{2,1,0:T(8,128)} %pad_maximum_fusion.1), calls=%async_computation.2 | async-start | bytes 1572864 | tf_op jit(solution)/shard_map/lead/all_to_all | solution.py:422
  79.0 126.2 %all-gather.5.cloned.1.call-start = ((), (), s32[]{:S(2)}) async-start(), calls=%async_computation.6 | async-start | bytes 3932160 | tf_op jit(solution)/shard_map/panel_cols/all_gather | solution.py:434
  109.3 6.1 %copy-start.3 = (f32[8,64,512]{2,1,0:T(8,128)}, f32[8,64,512]{2,1,0:T(8,128)S(1)}, u32[]{:S(2)}) copy-start(f32[8,64,512]{2,1,0:T(8,128)S(1)} %all_to_all.30) | copy-start | bytes 3145732
  109.3 4.5 %collective-permute-start.1 = (f32[512,512]{1,0:T(8,128)S(1)}, f32[512,512]{1,0:T(8,128)}, u32[]{:S(2)}, u32[]{:S(2)}) collective-permute-start(f32[512,512]{1,0:T(8,128)S(1)} %bitcast.39), channel_id=1, source_target_pairs={{0,1},{1,0},{2,3},{3,2},{4,5},{5,4},{6,7},{7,6},{8,9},{9,8},{10,11... | collective-permute-start | bytes 3145736 | tf_op jit(solution)/shard_map/lead/ppermute | solution.py:379
  115.4 30.2 %all-to-all-start.4 = ((f32[8,64,1024]{2,1,0:T(8,128)}), f32[8,64,1024]{2,1,0:T(8,128)S(1)}, u32[]{:S(2)}, u32[]{:S(2)}) async-start(f32[8,64,1024]{2,1,0:T(8,128)} %broadcast_in_dim.8), calls=%async_computation.4 | async-start | bytes 4194304 | tf_op jit(solution)/shard_map/lead/all_to_all | solution.py:429
  119.8 89.9 %all-gather.7.cloned.1.call-start = ((), (), s32[]{:S(2)}) async-start(), calls=%async_computation.7 | async-start | bytes 6684672 | tf_op jit(solution)/shard_map/panel_rows/all_gather | solution.py:442
  145.6 2.5 %copy-start.2 = (f32[8,64,1024]{2,1,0:T(8,128)}, f32[8,64,1024]{2,1,0:T(8,128)S(1)}, u32[]{:S(2)}) copy-start(f32[8,64,1024]{2,1,0:T(8,128)S(1)} %all-to-all-done.4) | copy-start | bytes 6291460
  145.7 8.2 %collective-permute-start.2 = (f32[512,1024]{1,0:T(8,128)S(1)}, f32[512,1024]{1,0:T(8,128)}, u32[]{:S(2)}, u32[]{:S(2)}) collective-permute-start(f32[512,1024]{1,0:T(8,128)S(1)} %bitcast.36), channel_id=1, source_target_pairs={{0,1},{1,0},{2,3},{3,2},{4,5},{5,4},{6,7},{7,6},{8,9},{9,8},{10,11... | collective-permute-start | bytes 6291464 | tf_op jit(solution)/shard_map/panel_rows/ppermute | solution.py:379
  148.2 57.1 %all-to-all-start.5 = ((f32[8,256,256]{2,1,0:T(8,128)}), f32[8,256,256]{2,1,0:T(8,128)}, u32[]{:S(2)}, u32[]{:S(2)}) async-start(f32[8,256,256]{2,1,0:T(8,128)} %bitcast.19), calls=%async_computation.5 | async-start | bytes 4194304 | tf_op jit(solution)/shard_map/exchange/all_to_all | solution.py:446
Sparse Core Ops, SparseCore 0:
  81.5 41.1 all-gather.4
  145.8 63.8 all-gather.6

commit v4 on v3

--- a/solution.py
+++ b/solution.py
@@ -175,18 +175,20 @@
 VMEM = pl.BlockSpec(memory_space=pltpu.VMEM)
 SMEM = pl.BlockSpec(memory_space=pltpu.SMEM)
 PARAMS = pltpu.CompilerParams(vmem_limit_bytes=60 << 20)
+SMALL = pltpu.CompilerParams(vmem_limit_bytes=16 << 20)
+MIDDLE = pltpu.CompilerParams(vmem_limit_bytes=28 << 20)
+LARGE = pltpu.CompilerParams(vmem_limit_bytes=46 << 20)
 
 
 def factor_call(kernel, outs, scratch, *args):
     square = jax.ShapeDtypeStruct((BLOCK, BLOCK), F32)
     return pl.pallas_call(
         kernel,
-        grid=(1,),
-        in_specs=[SMEM] + [pl.BlockSpec(x.shape, lambda i: (0, 0)) for x in args[1:]],
-        out_specs=[pl.BlockSpec((BLOCK, BLOCK), lambda i: (0, 0))] * outs,
+        in_specs=[SMEM] + [VMEM] * (len(args) - 1),
+        out_specs=[VMEM] * outs,
         out_shape=[square] * outs,
         scratch_shapes=[pltpu.VMEM((BLOCK, BLOCK), F32)] * scratch,
-        compiler_params=PARAMS,
+        compiler_params=MIDDLE,
         cost_estimate=pl.CostEstimate(flops=20_000_000_000, bytes_accessed=1 << 24, transcendentals=0),
     )(*args)
 
@@ -213,14 +215,16 @@
     out_ref[:, 2 * BLOCK :] = third
 
 
-def combine(index_ref, first_ref, second_ref, third_ref, out_ref):
-    out_ref[:, :BLOCK] = (first_ref[0] + first_ref[2]) + (first_ref[4] + first_ref[6])
+def combine(index_ref, got_ref, out_ref):
+    first = lambda n: got_ref[n, :, :BLOCK]
+    out_ref[:, :BLOCK] = (first(0) + first(2)) + (first(4) + first(6))
     out_ref[:, BLOCK : 2 * BLOCK] = (
-        (first_ref[1] + first_ref[3]) + (first_ref[5] + first_ref[7]) + second_ref[0]
+        (first(1) + first(3)) + (first(5) + first(7)) + got_ref[0, :, BLOCK : 2 * BLOCK]
     )
-    total = second_ref[1]
+    total = got_ref[1, :, BLOCK : 2 * BLOCK]
     for q in range(NKIDS):
-        total = total + nt(whole(third_ref[2 * q]), three(hot_t(index_ref[q : q + 1, :])))
+        rows = three(hot_t(index_ref[q : q + 1, :]))
+        total = total + nt(whole(got_ref[2 * q, :, 2 * BLOCK :]), rows)
     out_ref[:, 2 * BLOCK :] = total
 
 
@@ -228,107 +232,102 @@
     return jnp.concatenate([x, x], 1)
 
 
+def solve_cols(cols_ref, w0_ref, w1_ref, w2_ref, l10_ref, l20_ref, l21_ref, out_ref, x_ref):
+    part = x_ref.shape[0] // 8
+    for n in range(8):
+        x_ref[n * part : (n + 1) * part, :] = cols_ref[n % 4, n // 4]
+    s0 = mm3(x_ref[:, :BLOCK], w0_ref[...])
+    out_ref[:, :BLOCK] = s0
+    s1 = mm3(x_ref[:, BLOCK : 2 * BLOCK] - mm3(s0, l10_ref[...]), w1_ref[...])
+    out_ref[:, BLOCK : 2 * BLOCK] = s1
+    early = mm3(jnp.concatenate([s0, s1], 1), jnp.concatenate([l20_ref[...], l21_ref[...]], 1))
+    out_ref[:, 2 * BLOCK :] = mm3(x_ref[:, 2 * BLOCK :] - early, w2_ref[...])
+
+
+def solve_cols_call(col_rows, mats):
+    return pl.pallas_call(
+        solve_cols,
+        in_specs=[VMEM] * 7,
+        out_specs=VMEM,
+        out_shape=jax.ShapeDtypeStruct((BLOCK, LEAD), F32),
+        scratch_shapes=[pltpu.VMEM((BLOCK, LEAD), F32)],
+        compiler_params=MIDDLE,
+        cost_estimate=pl.CostEstimate(flops=10_000_000_000, bytes_accessed=12 << 20, transcendentals=0),
+    )(col_rows, *mats)
+
+
 def finish(
-    place_ref, cols_ref, rows_ref, front_ref, arrived_ref, row_hot_ref, col_hot_ref, w0_ref, w1_ref, w2_ref, l10_ref, l20_ref, l21_ref,
-    d0_ref, d1_ref, d2_ref, out_ref, w3_ref, m10_ref, m2_ref, c3_ref, x_ref, s_ref, raw_ref, sem,
+    place_ref, rows_ref, front_ref, arrived_ref, row_hot_ref, col_hot_ref,
+    solved_ref, w0_ref, w1_ref, w2_ref, l10_ref, l20_ref, l21_ref, d0_ref, d1_ref, d2_ref, out_ref, w3_ref, m10_ref, m2_ref, c3_ref, x_ref, s_ref,
 ):
     step = pl.program_id(0)
     r = place_ref[0]
     c = place_ref[1]
     part = x_ref.shape[0] // 8
-    sources = (w0_ref, l10_ref, w1_ref, l20_ref, l21_ref, w2_ref)
-    copies = [
-        pltpu.make_async_copy(src, raw_ref.at[n], sem.at[n]) for n, src in enumerate(sources)
-    ]
 
     @pl.when(step == 0)
     def _():
-        for copy in copies:
-            copy.start()
+        w3_ref[0] = right3(w0_ref[...])
+        w3_ref[1] = right3(w1_ref[...])
+        w3_ref[2] = right3(w2_ref[...])
+        m10_ref[...] = right3(l10_ref[...])
+        m2_ref[...] = right3(jnp.concatenate([l20_ref[...], l21_ref[...]], 1))
+        c3_ref[...] = right3(solved_ref[...])
+
+    for q in range(8):
         for n in range(8):
-            x_ref[n * part : (n + 1) * part, :] = cols_ref[n % 4, n // 4]
-
-    @pl.when(step > 0)
-    def _():
-        for q in range(8):
-            for n in range(8):
-                to = n * part + 8 * q
-                x_ref[to : to + 8, :] = rows_ref[q, 0, 8 * n : 8 * n + 8, :]
-
-    @pl.when(step == 0)
-    def _():
-        copies[0].wait()
-        w3_ref[0] = right3(raw_ref[0])
+            to = n * part + 8 * q
+            x_ref[to : to + 8, :] = rows_ref[q, 0, 8 * n : 8 * n + 8, :]
 
     s_ref[:, :BLOCK] = nt(left3(x_ref[:, :BLOCK]), w3_ref[0])
-
-    @pl.when(step == 0)
-    def _():
-        copies[1].wait()
-        m10_ref[...] = right3(raw_ref[1])
-        copies[2].wait()
-        w3_ref[1] = right3(raw_ref[2])
 
     s1 = nt(left3(x_ref[:, BLOCK : 2 * BLOCK] - nt(left3(s_ref[:, :BLOCK]), m10_ref[...])), w3_ref[1])
     s_ref[:, BLOCK : 2 * BLOCK] = s1
 
-    @pl.when(step == 0)
-    def _():
-        copies[3].wait()
-        copies[4].wait()
-        m2_ref[...] = right3(jnp.concatenate([raw_ref[3], raw_ref[4]], 1))
-        copies[5].wait()
-        w3_ref[2] = right3(raw_ref[5])
-
     s2 = nt(left3(x_ref[:, 2 * BLOCK :] - nt(left3(s_ref[:, : 2 * BLOCK]), m2_ref[...])), w3_ref[2])
     s_ref[:, 2 * BLOCK :] = s2
 
-    @pl.when(step == 0)
-    def _():
-        c3_ref[...] = right3(s_ref[...])
-
-    rng = 2 * r + step - 1
-
-    @pl.when((step > 0) & (c >= PANELS) & (rng >= PANELS))
+    rng = 2 * r + step
+
+    @pl.when((c >= PANELS) & (rng >= PANELS))
     def _():
         total = front_ref[...]
         for q in range(NKIDS):
             cols = two(hot_t(col_hot_ref[q : q + 1, :]))
-            rows = two(hot_t(row_hot_ref[step - 1, q : q + 1, :]))
+            rows = two(hot_t(row_hot_ref[step, q : q + 1, :]))
             spread_cols = nt(cols, jnp.concatenate(split2(arrived_ref[q, 0]), 1))
             total = total + nt(rows, jnp.concatenate(split2(spread_cols), 1))
         out_ref[...] = total - nt(left3(s_ref[...]), c3_ref[...])
 
-    @pl.when((step > 0) & (rng < jnp.minimum(c, PANELS)))
+    @pl.when((rng < jnp.minimum(c, PANELS)))
     def _():
         out_ref[...] = jnp.zeros_like(out_ref)
 
     for p, d_ref in enumerate((d0_ref, d1_ref, d2_ref)):
-        @pl.when((step > 0) & (c == p) & (rng > p))
+        @pl.when((c == p) & (rng > p))
         def _():
             out_ref[...] = s_ref[:, p * BLOCK : (p + 1) * BLOCK]
 
-        @pl.when((step > 0) & (c == p) & (rng == p))
+        @pl.when((c == p) & (rng == p))
         def _():
             pltpu.sync_copy(d_ref, out_ref)
 
 
-def finish_call(place, col_rows, row_rows, front, arrived, row_hot, col_hot, mats):
-    half = lambda i: jnp.maximum(i - 1, 0)
+def finish_call(place, row_rows, front, arrived, row_hot, col_hot, mats):
     return pl.pallas_call(
         finish,
-        grid=(3,),
+        grid=(2,),
         in_specs=[
             SMEM,
-            pl.BlockSpec((4, 2, BLOCK // 8, LEAD), lambda i: (0, 0, 0, 0)),
-            pl.BlockSpec((8, 1, BLOCK // 8, LEAD), lambda i: (0, half(i), 0, 0)),
-            pl.BlockSpec((BLOCK, BLOCK), lambda i: (half(i), 0)),
-            pl.BlockSpec((NKIDS, 1, PICK, PICK), lambda i: (0, half(i), 0, 0)),
+            pl.BlockSpec((8, 1, BLOCK // 8, LEAD), lambda i: (0, i, 0, 0)),
+            pl.BlockSpec((BLOCK, BLOCK), lambda i: (i, 0)),
+            pl.BlockSpec((NKIDS, 1, PICK, PICK), lambda i: (0, i, 0, 0)),
             VMEM,
             VMEM,
         ]
-        + [pl.BlockSpec(memory_space=pl.ANY)] * 9,
-        out_specs=pl.BlockSpec((BLOCK, BLOCK), lambda i: (half(i), 0)),
+        + [VMEM] * 7
+        + [pl.BlockSpec(memory_space=pl.ANY)] * 3,
+        out_specs=pl.BlockSpec((BLOCK, BLOCK), lambda i: (i, 0)),
         out_shape=jax.ShapeDtypeStruct(front.shape, F32),
         scratch_shapes=[
             pltpu.VMEM((3, BLOCK, 3 * BLOCK), B16),
@@ -337,12 +336,10 @@
             pltpu.VMEM((BLOCK, 9 * BLOCK), B16),
             pltpu.VMEM((BLOCK, LEAD), F32),
             pltpu.VMEM((BLOCK, LEAD), F32),
-            pltpu.VMEM((6, BLOCK, BLOCK), F32),
-            pltpu.SemaphoreType.DMA((6,)),
         ],
-        compiler_params=PARAMS,
+        compiler_params=LARGE,
         cost_estimate=pl.CostEstimate(flops=20_000_000_000, bytes_accessed=24 << 20, transcendentals=0),
-    )(place, col_rows, row_rows, front, arrived, row_hot, col_hot, *mats)
+    )(place, row_rows, front, arrived, row_hot, col_hot, *mats)
 
 
 ROW = ("x_hi", "z")
@@ -396,17 +393,11 @@
         got = lax.all_to_all(outgoing.reshape(nr, per, -1), ROW, 0, 0, tiled=True)
         own_slice = pl.pallas_call(
             combine,
-            grid=(1,),
-            in_specs=[
-                VMEM,
-                pl.BlockSpec((nr, per, BLOCK), lambda i: (0, 0, 0)),
-                pl.BlockSpec((2, per, BLOCK), lambda i: (0, 0, 1)),
-                pl.BlockSpec((nr, per, PICK), lambda i: (0, 0, 2 * BLOCK // PICK)),
-            ],
+            in_specs=[VMEM, VMEM],
             out_specs=VMEM,
             out_shape=jax.ShapeDtypeStruct((per, LEAD), F32),
-            compiler_params=PARAMS,
-        )(index[:, 2, :], got, got, got)
+            compiler_params=SMALL,
+        )(index[:, 2, :], got)
 
     with jax.named_scope("panel_cols"):
         far = lax.ppermute(own_slice, "x_hi", [(0, 1), (1, 0)])
@@ -450,17 +441,18 @@
         l22, w2, l20, l21 = factor_call(factor2, 4, 3, odd, mine2, other2, w0, w1, l10)
 
     with jax.named_scope("finish"):
+        mats = (w0, w1, w2, l10, l20, l21)
+        solved = solve_cols_call(col_rows, mats)
         row_hot = lax.dynamic_slice(index, (0, group * r, 0), (NKIDS, group, PICK)).transpose(1, 0, 2)
         col_hot = lax.dynamic_slice(index, (0, c, 0), (NKIDS, 1, PICK)).reshape(NKIDS, PICK)
         return finish_call(
             jnp.stack([r, c]),
-            col_rows,
             row_rows,
             root_front,
             arrived.reshape(NKIDS, group, PICK, PICK),
             row_hot,
             col_hot,
-            (w0, w1, w2, l10, l20, l21, l00, l11, l22),
+            (solved, *mats, l00, l11, l22),
         )
 
 

time: 255 us -> 263 us (1.031)
  local copies, waits for them, and re-layouts: 5.85 us -> 31.6 us
  Pallas kernels: 113 us -> 100 us
  waiting for transfers between devices: 62.4 us -> 57 us
    unnamed x8 -> x52, local copies, waits for them, and re-layouts: 1.52 us -> 28.4 us
    pallas_call x5 -> x6, Pallas kernels: 109 us -> 95.8 us  [the longest x3 62.4 us: factor_call(): pl.pallas_call(kernel, in_specs=[SMEM] + [VMEM] * (len(args) - 1), out_sp...]
    all_gather x1, waiting for transfers between devices: 4.44 us -> 0.01 us  [body(): row_rows = lax.all_gather(share, COL, axis=0, tiled=False)]
  transfers between devices with their start and end apart: 10 -> 10, of which waited for: 6 -> 5; matrix products, arithmetic and copies ran while one was open for 2% -> 2% of each run, Pallas kernels for 29% -> 26%
where the time goes in v4:
time: 263 us; the launch traced here: 259 us
  Pallas kernels  100 us (38%)
  waiting for transfers between devices  57 us (22%)
  starting transfers between devices  34.5 us (13%)
  local copies, waits for them, and re-layouts  31.6 us (12%)
  blocking collectives  17.6 us (7%)
  between operations  13.8 us (5%)
  other arithmetic  3.95 us (2%)
    pallas_call x3, Pallas kernels, factor_call(): pl.pallas_call(kernel, in_specs=[SMEM] + [VMEM] * (len(args) - 1), out_sp...  62.4 us
    all_to_all x1, waiting for transfers between devices, body(): got = lax.all_to_all(outgoing.reshape(nr, per, -1), ROW, 0, 0, tiled=True)  31.5 us
    unnamed x52, local copies, waits for them, and re-layouts  28.4 us
    pallas_call x1, Pallas kernels, finish_call(): pl.pallas_call(finish, grid=(2,), in_specs=[SMEM, pl.BlockSpec((8, 1, BLO...  26.5 us
    all_to_all x1, blocking collectives, spread(): return lax.all_to_all(copies_of(a, count), axis, 0, 0, tiled=True)  17.6 us
    all_to_all x1, waiting for transfers between devices, body(): both = lax.all_to_all(both, ROW, 0, 0, tiled=True)  9.77 us
    all_to_all x1, waiting for transfers between devices, body(): lax.all_to_all(own_slice.reshape(nc // 2, per // (nc // 2), LEAD), CHIP,...  8.81 us
    all_to_all x1, starting transfers between devices, body(): got = lax.all_to_all(outgoing.reshape(nr, per, -1), ROW, 0, 0, tiled=True)  7.72 us
  transfers between devices with their start and end apart: 10, of which 5 were waited for; matrix products, arithmetic and copies ran while one was open for 2% of the time, Pallas kernels for 26%

profile of v4, /device:TPU:7, one launch (start us, length us, event | category | flops | bytes accessed | tf_op | source)
XLA Modules:
  0.0 258.5 jit_solution(4790531169490967530)
XLA Ops:
  8.1 4.3 %slices.2 = f32[512,1280]{1,0:T(8,128)} custom-call(s32[1]{0:T(128)} %bitcast.flag_ref, s32[1,256]{1,0:T(1,128)} %get-tuple-element.52.cols_ref, s32[1,256]{1,0:T(1,128)} %get-tuple-element.51.rows_ref, f32[2048,256]{1,0:T(8,128)} %contrib_ref.1, f32[1024,512]{1,0:T(8,128)} %front_ref.1), custom_call_target="tpu_custom_call" | custom-call | tf_op jit(solution)/shard_map/slices/pallas_call | solution.py:379
  12.4 7.7 %all-to-all-start = ((f32[8,64,1280]{2,1,0:T(8,128)}), f32[8,64,1280]{2,1,0:T(8,128)S(1)}, u32[]{:S(2)}, u32[]{:S(2)}) async-start(f32[8,64,1280]{2,1,0:T(8,128)} %bitcast.41), calls=%async_computation | async-start | bytes 5242880 | tf_op jit(solution)/shard_map/slices/all_to_all | solution.py:393
  20.1 31.5 %all-to-all-done.got_ref = f32[8,64,1280]{2,1,0:T(8,128)S(1)} async-done(((f32[8,64,1280]{2,1,0:T(8,128)}), f32[8,64,1280]{2,1,0:T(8,128)S(1)}, u32[]{:S(2)}, u32[]{:S(2)}) %all-to-all-start) | async-done | bytes 2621472 | tf_op jit(solution)/shard_map/slices/all_to_all | solution.py:393
  51.6 1.8 slices.3
  53.7 5.4 %all-to-all-start.1 = ((f32[8,8,1536]{2,1,0:T(8,128)}), f32[8,8,1536]{2,1,0:T(8,128)S(1)}, u32[]{:S(2)}, u32[]{:S(2)}) async-start(f32[8,8,1536]{2,1,0:T(8,128)} %bitcast.8), calls=%async_computation.1 | async-start | bytes 786432 | tf_op jit(solution)/shard_map/lead/all_to_all | solution.py:406
  59.0 8.8 %all-to-all-done.1 = f32[8,8,1536]{2,1,0:T(8,128)S(1)} async-done(((f32[8,8,1536]{2,1,0:T(8,128)}), f32[8,8,1536]{2,1,0:T(8,128)S(1)}, u32[]{:S(2)}, u32[]{:S(2)}) %all-to-all-start.1) | async-done | bytes 393248 | tf_op jit(solution)/shard_map/lead/all_to_all | solution.py:406
  67.9 0.9 pad_maximum_fusion
  68.9 7.2 %all-to-all-start.2 = ((f32[8,16,1536]{2,1,0:T(8,128)}), f32[8,16,1536]{2,1,0:T(8,128)S(1)}, u32[]{:S(2)}, u32[]{:S(2)}) async-start(f32[8,16,1536]{2,1,0:T(8,128)} %pad_maximum_fusion), calls=%async_computation.2 | async-start | bytes 1572864 | tf_op jit(solution)/shard_map/lead/all_to_all | solution.py:413
  76.0 1.1 select_bitcast_fusion.1
  77.1 0.9 pad_maximum_fusion.1
  78.1 9.8 %all-to-all-done.2 = f32[8,16,1536]{2,1,0:T(8,128)S(1)} async-done(((f32[8,16,1536]{2,1,0:T(8,128)}), f32[8,16,1536]{2,1,0:T(8,128)S(1)}, u32[]{:S(2)}, u32[]{:S(2)}) %all-to-all-start.2) | async-done | bytes 786464 | tf_op jit(solution)/shard_map/lead/all_to_all | solution.py:413
  88.8 17.6 %all_to_all.30 = f32[8,64,512]{2,1,0:T(8,128)S(1)} all-to-all(f32[8,64,512]{2,1,0:T(8,128)S(1)} %broadcast_in_dim.7), channel_id=1, replica_groups=mesh['x_hi'=2,'z'=4,'y'=4,'x_lo'=2,'core'=2] {'y','x_lo'}, dimensions={0} | all-to-all | bytes 2097152 | tf_op jit(solution)/shard_map/lead/all_to_all | solution.py:356
  106.4 2.1 collective-permute-start.1
  108.5 2.3 collective-permute-done.1.other_ref.other1_ref
  110.8 1.0 copy-done.1
  111.7 1.6 broadcast_in_dim.8
  113.3 4.4 %all-to-all-start.4 = ((f32[8,64,1024]{2,1,0:T(8,128)}), f32[8,64,1024]{2,1,0:T(8,128)S(1)}, u32[]{:S(2)}, u32[]{:S(2)}) async-start(f32[8,64,1024]{2,1,0:T(8,128)} %broadcast_in_dim.8), calls=%async_computation.4 | async-start | bytes 4194304 | tf_op jit(solution)/shard_map/lead/all_to_all | solution.py:420
  118.3 1.2 copy-done.2
  119.5 17.4 %factor.3 = (f32[512,512]{1,0:T(8,128)S(1)}, f32[512,512]{1,0:T(8,128)S(1)}) custom-call(s32[1]{0:T(128)} %bitcast.2.odd_ref, f32[512,512]{1,0:T(8,128)S(1)} %bitcast.38, f32[512,512]{1,0:T(8,128)S(1)} %copy-done.2), custom_call_target="tpu_custom_call" | custom-call | flops 20000000000 | bytes 16777216 | tf_op jit(solution)/shard_map/factor/pallas_call | solution.py:185
  136.9 1.0 copy-done.5
  137.9 1.0 copy-done.22
  138.9 4.7 %all-to-all-done.4 = f32[8,64,1024]{2,1,0:T(8,128)S(1)} async-done(((f32[8,64,1024]{2,1,0:T(8,128)}), f32[8,64,1024]{2,1,0:T(8,128)S(1)}, u32[]{:S(2)}, u32[]{:S(2)}) %all-to-all-start.4) | async-done | bytes 2097184 | tf_op jit(solution)/shard_map/lead/all_to_all | solution.py:420
  143.6 1.3 collective-permute-start.2
  144.9 5.7 %all-to-all-start.5 = ((f32[8,256,256]{2,1,0:T(8,128)}), f32[8,256,256]{2,1,0:T(8,128)}, u32[]{:S(2)}, u32[]{:S(2)}) async-start(f32[8,256,256]{2,1,0:T(8,128)} %bitcast.42), calls=%async_computation.5 | async-start | bytes 4194304 | tf_op jit(solution)/shard_map/exchange/all_to_all | solution.py:437
  150.7 1.2 copy-done.3
  151.9 1.5 copy-done.6
  153.4 21.1 %factor.4 = (f32[512,512]{1,0:T(8,128)S(1)}, f32[512,512]{1,0:T(8,128)S(1)}, f32[512,512]{1,0:T(8,128)S(1)}) custom-call(s32[1]{0:T(128)} %bitcast.2.odd_ref, f32[512,512]{1,0:T(8,128)S(1)} %bitcast.39, f32[512,512]{1,0:T(8,128)S(1)} %copy-done.3, f32[512,1024]{1,0:T(8,128)S(1)} %bitcast.35, f32[512,1024]{1,0:T(8,128)} %collective-permute-done.2.other2_ref.other_ref, ...), custom_call_target="tpu_custom_call" | custom-call | flops 20000000000 | bytes 16777216 | tf_op jit(solution)/shard_map/factor/pallas_call | solution.py:185
  174.5 1.0 copy-done.24
  175.4 23.9 %factor.5 = (f32[512,512]{1,0:T(8,128)S(1)}, f32[512,512]{1,0:T(8,128)S(1)}, f32[512,512]{1,0:T(8,128)S(1)}, f32[512,512]{1,0:T(8,128)S(1)}) custom-call(s32[1]{0:T(128)} %bitcast.2.odd_ref, f32[512,1024]{1,0:T(8,128)S(1)} %bitcast.36, f32[512,1024]{1,0:T(8,128)} %collective-permute-done.2.other2_ref.other_ref, f32[512,512]{1,0:T(8,128)S(1)} %copy-done.6, ...), custom_call_target="tpu_custom_call" | custom-call | flops 20000000000 | bytes 16777216 | tf_op jit(solution)/shard_map/factor/pallas_call | solution.py:185
  199.3 1.0 copy-done.8
  200.3 1.0 copy-done.11
  201.3 1.0 copy-done.13
  202.2 1.0 copy-done.16
  203.2 1.0 copy-done.19
  204.2 1.0 copy-done.25
  205.2 1.9 copy-done
  207.2 1.2 copy-done.9
  208.4 1.2 copy-done.12
  209.6 1.2 copy-done.14
  210.8 1.2 copy-done.17
  212.1 1.2 copy-done.20
  213.3 5.1 %finish.2.solved_ref = f32[512,1536]{1,0:T(8,128)S(1)} custom-call(f32[4,2,64,1536]{3,2,1,0:T(8,128)S(1)} %bitcast.40, f32[512,512]{1,0:T(8,128)S(1)} %copy-done.7, f32[512,512]{1,0:T(8,128)S(1)} %copy-done.9, f32[512,512]{1,0:T(8,128)S(1)} %copy-done.14, f32[512,512]{1,0:T(8,128)S(1)} %copy-done.12, f32[512,512]{1,0:T(8,128)S(1)} %copy-done.17, ...), custom_call_target="tpu_custom_call" | custom-call | flops 10000000000 | bytes 12582912 | tf_op jit(solution)/shard_map/finish/pallas_call | solution.py:248
  218.4 1.7 copy-done.4
  220.2 1.2 copy-done.15
  221.4 1.2 copy-done.18
  222.6 1.2 copy-done.21
  223.8 1.2 copy-done.23
  225.1 26.5 %finish.3 = f32[1024,512]{1,0:T(8,128)} custom-call(s32[2]{0:T(128)S(1)} %pad_add_fusion.place_ref, f32[8,2,64,1536]{3,2,1,0:T(8,128)} %bitcast.44, f32[1024,512]{1,0:T(8,128)} %front_ref.1, f32[4,2,256,256]{3,2,1,0:T(8,128)} %bitcast.17.arrived_ref, s32[2,4,256]{2,1,0:T(4,128)S(1)} %dynamic-slice_bitcast_fusion.row_hot_ref, ...), custom_call_target="tpu_custom_call" | custom-call | flops 20000000000 | bytes 25165824 | tf_op jit(solution)/shard_map/finish/pallas_call | solution.py:317
  (53 shorter events, 3.5 us)
Async XLA Ops:
  12.4 39.2 %all-to-all-start = ((f32[8,64,1280]{2,1,0:T(8,128)}), f32[8,64,1280]{2,1,0:T(8,128)S(1)}, u32[]{:S(2)}, u32[]{:S(2)}) async-start(f32[8,64,1280]{2,1,0:T(8,128)} %bitcast.41), calls=%async_computation | async-start | bytes 5242880 | tf_op jit(solution)/shard_map/slices/all_to_all | solution.py:393
  53.4 14.5 %collective-permute-start = (f32[64,1536]{1,0:T(8,128)}, f32[64,1536]{1,0:T(8,128)S(1)}, u32[]{:S(2)}, u32[]{:S(2)}) collective-permute-start(f32[64,1536]{1,0:T(8,128)} %slices.3), channel_id=1, source_target_pairs={{0,64},{64,0},{1,65},{65,1},{2,66},{66,2},{3,67},{67,3},{4,68},{68... | collective-permute-start | bytes 1179656 | tf_op jit(solution)/shard_map/panel_cols/ppermute | solution.py:403
  53.7 14.2 %all-to-all-start.1 = ((f32[8,8,1536]{2,1,0:T(8,128)}), f32[8,8,1536]{2,1,0:T(8,128)S(1)}, u32[]{:S(2)}, u32[]{:S(2)}) async-start(f32[8,8,1536]{2,1,0:T(8,128)} %bitcast.8), calls=%async_computation.1 | async-start | bytes 786432 | tf_op jit(solution)/shard_map/lead/all_to_all | solution.py:406
  68.9 19.0 %all-to-all-start.2 = ((f32[8,16,1536]{2,1,0:T(8,128)}), f32[8,16,1536]{2,1,0:T(8,128)S(1)}, u32[]{:S(2)}, u32[]{:S(2)}) async-start(f32[8,16,1536]{2,1,0:T(8,128)} %pad_maximum_fusion), calls=%async_computation.2 | async-start | bytes 1572864 | tf_op jit(solution)/shard_map/lead/all_to_all | solution.py:413
  76.0 129.2 %all-gather.7.cloned.1.call-start = ((), (), s32[]{:S(2)}) async-start(), calls=%async_computation.7 | async-start | bytes 3932160 | tf_op jit(solution)/shard_map/panel_cols/all_gather | solution.py:425
  106.4 4.4 %collective-permute-start.1 = (f32[512,512]{1,0:T(8,128)S(1)}, f32[512,512]{1,0:T(8,128)S(1)}, u32[]{:S(2)}, u32[]{:S(2)}) collective-permute-start(f32[512,512]{1,0:T(8,128)S(1)} %bitcast.37), channel_id=1, source_target_pairs={{0,1},{1,0},{2,3},{3,2},{4,5},{5,4},{6,7},{7,6},{8,9},{9,8},{10,11... | collective-permute-start | bytes 3145736 | tf_op jit(solution)/shard_map/lead/ppermute | solution.py:376
  110.8 1.0 copy-start.1
  113.3 30.2 %all-to-all-start.4 = ((f32[8,64,1024]{2,1,0:T(8,128)}), f32[8,64,1024]{2,1,0:T(8,128)S(1)}, u32[]{:S(2)}, u32[]{:S(2)}) async-start(f32[8,64,1024]{2,1,0:T(8,128)} %broadcast_in_dim.8), calls=%async_computation.4 | async-start | bytes 4194304 | tf_op jit(solution)/shard_map/lead/all_to_all | solution.py:420
  117.7 102.4 %all-gather.5.cloned.1.call-start = ((), (), s32[]{:S(2)}) async-start(), calls=%async_computation.6 | async-start | bytes 6684672 | tf_op jit(solution)/shard_map/panel_rows/all_gather | solution.py:433
  118.2 1.2 copy-start.2
  136.9 1.0 copy-start.5
  137.9 1.0 copy-start.22
  143.6 7.1 %collective-permute-start.2 = (f32[512,1024]{1,0:T(8,128)S(1)}, f32[512,1024]{1,0:T(8,128)}, u32[]{:S(2)}, u32[]{:S(2)}) collective-permute-start(f32[512,1024]{1,0:T(8,128)S(1)} %bitcast.34), channel_id=1, source_target_pairs={{0,1},{1,0},{2,3},{3,2},{4,5},{5,4},{6,7},{7,6},{8,9},{9,8},{10,11... | collective-permute-start | bytes 6291464 | tf_op jit(solution)/shard_map/panel_rows/ppermute | solution.py:376
  144.9 75.2 %all-to-all-start.5 = ((f32[8,256,256]{2,1,0:T(8,128)}), f32[8,256,256]{2,1,0:T(8,128)}, u32[]{:S(2)}, u32[]{:S(2)}) async-start(f32[8,256,256]{2,1,0:T(8,128)} %bitcast.42), calls=%async_computation.5 | async-start | bytes 4194304 | tf_op jit(solution)/shard_map/exchange/all_to_all | solution.py:437
  150.7 1.2 copy-start.3
  151.9 1.5 copy-start.6
  174.4 1.0 copy-start.24
  175.4 29.8 %copy-start.7 = (f32[512,512]{1,0:T(8,128)S(1)}, f32[512,512]{1,0:T(8,128)}, u32[]{:S(2)}) copy-start(f32[512,512]{1,0:T(8,128)} %copy-done.5) | copy-start | bytes 3145732
  199.3 1.0 copy-start.8
  200.3 1.0 copy-start.11
  201.2 1.0 copy-start.13
  202.2 1.0 copy-start.16
  203.2 1.0 copy-start.19
  204.2 1.0 copy-start.25
  205.2 1.9 copy-start
  207.2 1.2 copy-start.9
  208.4 1.2 copy-start.12
  209.6 1.2 copy-start.14
  210.8 1.2 copy-start.17
  212.1 1.2 copy-start.20
  213.3 6.9 %copy-start.10 = (f32[512,512]{1,0:T(8,128)S(1)}, f32[512,512]{1,0:T(8,128)}, u32[]{:S(2)}) copy-start(f32[512,512]{1,0:T(8,128)} %copy-done.8) | copy-start | bytes 3145732
  218.4 1.7 copy-start.4
  220.1 1.2 copy-start.15
  221.4 1.2 copy-start.18
  222.6 1.2 copy-start.21
  223.8 1.2 copy-start.23
Sparse Core Ops, SparseCore 0:
  78.5 41.1 all-gather.6
  143.7 62.9 all-gather.4

commit v5 on v4

--- a/solution.py
+++ b/solution.py
@@ -156,9 +156,11 @@
 
 
 def factor2(
-    odd_ref, mine_ref, other_ref, w0_ref, w1_ref, l10_ref,
-    l_ref, w_ref, l20_ref, l21_ref, s_ref, x_ref, y_ref,
+    odd_ref, mine_ref, other_ref, w0_ref, w1_ref, l10_ref, cols_ref,
+    l_ref, w_ref, l20_ref, l21_ref, solved_ref, s_ref, x_ref, y_ref, c_ref, sem,
 ):
+    copy = pltpu.make_async_copy(cols_ref, c_ref, sem)
+    copy.start()
     odd = odd_ref[0] == 1
     put_rows(x_ref, mine_ref, other_ref, odd, 0)
     put_rows(y_ref, mine_ref, other_ref, jnp.logical_not(odd), BLOCK)
@@ -171,24 +173,42 @@
     s_ref[...] = s_ref[...] - mm3(both, both)
     factor_block(l_ref, w_ref, s_ref)
 
+    copy.wait()
+    part = BLOCK // 8
+
+    def rows(p):
+        cols = slice(p * BLOCK, (p + 1) * BLOCK)
+        for n in range(8):
+            x_ref[n * part : (n + 1) * part, :] = c_ref[n % 4, n // 4, :, cols]
+        return x_ref[...]
+
+    s0 = mm3(rows(0), w0_ref[...])
+    solved_ref[:, :BLOCK] = s0
+    s1 = mm3(rows(1) - mm3(s0, l10_ref[...]), w1_ref[...])
+    solved_ref[:, BLOCK : 2 * BLOCK] = s1
+    early = mm3(s0, l20_ref[...]) + mm3(s1, l21_ref[...])
+    solved_ref[:, 2 * BLOCK :] = mm3(rows(2) - early, w_ref[...])
+
 
 VMEM = pl.BlockSpec(memory_space=pltpu.VMEM)
 SMEM = pl.BlockSpec(memory_space=pltpu.SMEM)
 PARAMS = pltpu.CompilerParams(vmem_limit_bytes=60 << 20)
 SMALL = pltpu.CompilerParams(vmem_limit_bytes=16 << 20)
-MIDDLE = pltpu.CompilerParams(vmem_limit_bytes=28 << 20)
-LARGE = pltpu.CompilerParams(vmem_limit_bytes=46 << 20)
+
+
+SQUARE = jax.ShapeDtypeStruct((BLOCK, BLOCK), F32)
 
 
 def factor_call(kernel, outs, scratch, *args):
-    square = jax.ShapeDtypeStruct((BLOCK, BLOCK), F32)
+    specs = [pl.BlockSpec(memory_space=pl.ANY) if x.ndim > 2 else pl.BlockSpec(x.shape, lambda i: (0, 0)) for x in args[1:]]
     return pl.pallas_call(
         kernel,
-        in_specs=[SMEM] + [VMEM] * (len(args) - 1),
-        out_specs=[VMEM] * outs,
-        out_shape=[square] * outs,
-        scratch_shapes=[pltpu.VMEM((BLOCK, BLOCK), F32)] * scratch,
-        compiler_params=MIDDLE,
+        grid=(1,),
+        in_specs=[SMEM] + specs,
+        out_specs=[pl.BlockSpec(x.shape, lambda i: (0, 0)) for x in outs],
+        out_shape=outs,
+        scratch_shapes=scratch,
+        compiler_params=PARAMS,
         cost_estimate=pl.CostEstimate(flops=20_000_000_000, bytes_accessed=1 << 24, transcendentals=0),
     )(*args)
 
@@ -232,60 +252,61 @@
     return jnp.concatenate([x, x], 1)
 
 
-def solve_cols(cols_ref, w0_ref, w1_ref, w2_ref, l10_ref, l20_ref, l21_ref, out_ref, x_ref):
-    part = x_ref.shape[0] // 8
-    for n in range(8):
-        x_ref[n * part : (n + 1) * part, :] = cols_ref[n % 4, n // 4]
-    s0 = mm3(x_ref[:, :BLOCK], w0_ref[...])
-    out_ref[:, :BLOCK] = s0
-    s1 = mm3(x_ref[:, BLOCK : 2 * BLOCK] - mm3(s0, l10_ref[...]), w1_ref[...])
-    out_ref[:, BLOCK : 2 * BLOCK] = s1
-    early = mm3(jnp.concatenate([s0, s1], 1), jnp.concatenate([l20_ref[...], l21_ref[...]], 1))
-    out_ref[:, 2 * BLOCK :] = mm3(x_ref[:, 2 * BLOCK :] - early, w2_ref[...])
-
-
-def solve_cols_call(col_rows, mats):
-    return pl.pallas_call(
-        solve_cols,
-        in_specs=[VMEM] * 7,
-        out_specs=VMEM,
-        out_shape=jax.ShapeDtypeStruct((BLOCK, LEAD), F32),
-        scratch_shapes=[pltpu.VMEM((BLOCK, LEAD), F32)],
-        compiler_params=MIDDLE,
-        cost_estimate=pl.CostEstimate(flops=10_000_000_000, bytes_accessed=12 << 20, transcendentals=0),
-    )(col_rows, *mats)
-
-
 def finish(
     place_ref, rows_ref, front_ref, arrived_ref, row_hot_ref, col_hot_ref,
-    solved_ref, w0_ref, w1_ref, w2_ref, l10_ref, l20_ref, l21_ref, d0_ref, d1_ref, d2_ref, out_ref, w3_ref, m10_ref, m2_ref, c3_ref, x_ref, s_ref,
+    solved_ref, w0_ref, w1_ref, w2_ref, l10_ref, l20_ref, l21_ref, d0_ref, d1_ref, d2_ref, out_ref, w3_ref, m10_ref, m2_ref, c3_ref, x_ref, s_ref, raw_ref, cols_ref, sem,
 ):
     step = pl.program_id(0)
     r = place_ref[0]
     c = place_ref[1]
     part = x_ref.shape[0] // 8
+    sources = (w0_ref, l10_ref, w1_ref, l20_ref, l21_ref, w2_ref)
+    copies = [
+        pltpu.make_async_copy(src, raw_ref.at[n], sem.at[n]) for n, src in enumerate(sources)
+    ] + [pltpu.make_async_copy(solved_ref, cols_ref, sem.at[len(sources)])]
 
     @pl.when(step == 0)
     def _():
-        w3_ref[0] = right3(w0_ref[...])
-        w3_ref[1] = right3(w1_ref[...])
-        w3_ref[2] = right3(w2_ref[...])
-        m10_ref[...] = right3(l10_ref[...])
-        m2_ref[...] = right3(jnp.concatenate([l20_ref[...], l21_ref[...]], 1))
-        c3_ref[...] = right3(solved_ref[...])
+        for copy in copies:
+            copy.start()
 
     for q in range(8):
         for n in range(8):
             to = n * part + 8 * q
             x_ref[to : to + 8, :] = rows_ref[q, 0, 8 * n : 8 * n + 8, :]
 
+    @pl.when(step == 0)
+    def _():
+        copies[0].wait()
+        w3_ref[0] = right3(raw_ref[0])
+
     s_ref[:, :BLOCK] = nt(left3(x_ref[:, :BLOCK]), w3_ref[0])
+
+    @pl.when(step == 0)
+    def _():
+        copies[1].wait()
+        m10_ref[...] = right3(raw_ref[1])
+        copies[2].wait()
+        w3_ref[1] = right3(raw_ref[2])
 
     s1 = nt(left3(x_ref[:, BLOCK : 2 * BLOCK] - nt(left3(s_ref[:, :BLOCK]), m10_ref[...])), w3_ref[1])
     s_ref[:, BLOCK : 2 * BLOCK] = s1
 
+    @pl.when(step == 0)
+    def _():
+        copies[3].wait()
+        copies[4].wait()
+        m2_ref[...] = right3(jnp.concatenate([raw_ref[3], raw_ref[4]], 1))
+        copies[5].wait()
+        w3_ref[2] = right3(raw_ref[5])
+
     s2 = nt(left3(x_ref[:, 2 * BLOCK :] - nt(left3(s_ref[:, : 2 * BLOCK]), m2_ref[...])), w3_ref[2])
     s_ref[:, 2 * BLOCK :] = s2
+
+    @pl.when(step == 0)
+    def _():
+        copies[6].wait()
+        c3_ref[...] = right3(cols_ref[...])
 
     rng = 2 * r + step
 
@@ -325,8 +346,7 @@
             VMEM,
             VMEM,
         ]
-        + [VMEM] * 7
-        + [pl.BlockSpec(memory_space=pl.ANY)] * 3,
+        + [pl.BlockSpec(memory_space=pl.ANY)] * 10,
         out_specs=pl.BlockSpec((BLOCK, BLOCK), lambda i: (i, 0)),
         out_shape=jax.ShapeDtypeStruct(front.shape, F32),
         scratch_shapes=[
@@ -336,8 +356,11 @@
             pltpu.VMEM((BLOCK, 9 * BLOCK), B16),
             pltpu.VMEM((BLOCK, LEAD), F32),
             pltpu.VMEM((BLOCK, LEAD), F32),
+            pltpu.VMEM((6, BLOCK, BLOCK), F32),
+            pltpu.VMEM((BLOCK, LEAD), F32),
+            pltpu.SemaphoreType.DMA((7,)),
         ],
-        compiler_params=LARGE,
+        compiler_params=PARAMS,
         cost_estimate=pl.CostEstimate(flops=20_000_000_000, bytes_accessed=24 << 20, transcendentals=0),
     )(place, row_rows, front, arrived, row_hot, col_hot, *mats)
 
@@ -425,7 +448,8 @@
         col_rows = lax.all_gather(pair, "z", axis=0, tiled=False)
 
     with jax.named_scope("factor"):
-        l00, w0 = factor_call(factor0, 2, 1, odd, mine1, other1)
+        square = pltpu.VMEM((BLOCK, BLOCK), F32)
+        l00, w0 = factor_call(factor0, [SQUARE] * 2, [square], odd, mine1, other1)
 
     with jax.named_scope("panel_rows"):
         w0, contrib, mine2, share = lax.optimization_barrier((w0, contrib, mine2, share))
@@ -437,12 +461,18 @@
         arrived = lax.all_to_all(contrib.reshape(nr, PICK, PICK), ROW, 0, 0, tiled=True)
 
     with jax.named_scope("factor"):
-        l11, w1, l10 = factor_call(factor1, 3, 2, odd, mine1, other1, mine2, other2, w0)
-        l22, w2, l20, l21 = factor_call(factor2, 4, 3, odd, mine2, other2, w0, w1, l10)
+        l11, w1, l10 = factor_call(
+            factor1, [SQUARE] * 3, [square] * 2, odd, mine1, other1, mine2, other2, w0
+        )
+        l22, w2, l20, l21, solved = factor_call(
+            factor2,
+            [SQUARE] * 4 + [jax.ShapeDtypeStruct((cols_loc, LEAD), F32)],
+            [square] * 3 + [pltpu.VMEM(col_rows.shape, F32), pltpu.SemaphoreType.DMA],
+            odd, mine2, other2, w0, w1, l10, col_rows,
+        )
 
     with jax.named_scope("finish"):
         mats = (w0, w1, w2, l10, l20, l21)
-        solved = solve_cols_call(col_rows, mats)
         row_hot = lax.dynamic_slice(index, (0, group * r, 0), (NKIDS, group, PICK)).transpose(1, 0, 2)
         col_hot = lax.dynamic_slice(index, (0, c, 0), (NKIDS, 1, PICK)).reshape(NKIDS, PICK)
         return finish_call(

time: 263 us -> 248 us (0.943)
  local copies, waits for them, and re-layouts: 31.6 us -> 4.35 us
  Pallas kernels: 100 us -> 112 us
    unnamed x52 -> x4, local copies, waits for them, and re-layouts: 28.4 us -> 0.01 us
    pallas_call x4 -> x3, Pallas kernels: 67.5 us -> 77.7 us  [factor_call(): pl.pallas_call(kernel, grid=(1,), in_specs=[SMEM] + specs, out_specs=[pl....]
  transfers between devices with their start and end apart: 10 -> 10, of which waited for: 5 -> 5; matrix products, arithmetic and copies ran while one was open for 2% -> 3% of each run, Pallas kernels for 26% -> 32%
where the time goes in v5:
time: 248 us; the launch traced here: 244 us
  Pallas kernels  112 us (45%)
  waiting for transfers between devices  57 us (23%)
  starting transfers between devices  34.5 us (14%)
  blocking collectives  17.6 us (7%)
  between operations  13.7 us (6%)
  other arithmetic  4.56 us (2%)
  local copies, waits for them, and re-layouts  4.35 us (2%)
    pallas_call x3, Pallas kernels, factor_call(): pl.pallas_call(kernel, grid=(1,), in_specs=[SMEM] + specs, out_specs=[pl....  77.7 us
    all_to_all x1, waiting for transfers between devices, body(): got = lax.all_to_all(outgoing.reshape(nr, per, -1), ROW, 0, 0, tiled=True)  30.9 us
    pallas_call x1, Pallas kernels, finish_call(): pl.pallas_call(finish, grid=(2,), in_specs=[SMEM, pl.BlockSpec((8, 1, BLO...  28.5 us
    all_to_all x1, blocking collectives, spread(): return lax.all_to_all(copies_of(a, count), axis, 0, 0, tiled=True)  17.6 us
    all_to_all x1, waiting for transfers between devices, body(): both = lax.all_to_all(both, ROW, 0, 0, tiled=True)  9.76 us
    all_to_all x1, waiting for transfers between devices, body(): lax.all_to_all(own_slice.reshape(nc // 2, per // (nc // 2), LEAD), CHIP,...  8.8 us
    all_to_all x1, starting transfers between devices, body(): got = lax.all_to_all(outgoing.reshape(nr, per, -1), ROW, 0, 0, tiled=True)  7.72 us
    all_to_all x1, starting transfers between devices, body(): both = lax.all_to_all(both, ROW, 0, 0, tiled=True)  7.17 us
  transfers between devices with their start and end apart: 10, of which 5 were waited for; matrix products, arithmetic and copies ran while one was open for 3% of the time, Pallas kernels for 32%

profile of v5, /device:TPU:7, one launch (start us, length us, event | category | flops | bytes accessed | tf_op | source)
XLA Modules:
  0.0 244.0 jit_solution(10041645191565072185)
XLA Ops:
  6.5 0.9 broadcast_subtract_fusion
  7.5 0.6 dynamic-slice_bitcast_fusion.2
  8.1 4.3 %slices.2 = f32[512,1280]{1,0:T(8,128)} custom-call(s32[1]{0:T(128)} %bitcast.flag_ref, s32[1,256]{1,0:T(1,128)} %get-tuple-element.54.cols_ref, s32[1,256]{1,0:T(1,128)} %get-tuple-element.53.rows_ref, f32[2048,256]{1,0:T(8,128)} %contrib_ref.1, f32[1024,512]{1,0:T(8,128)} %front_ref.1), custom_call_target="tpu_custom_call" | custom-call | tf_op jit(solution)/shard_map/slices/pallas_call | solution.py:402
  12.4 7.7 %all-to-all-start = ((f32[8,64,1280]{2,1,0:T(8,128)}), f32[8,64,1280]{2,1,0:T(8,128)S(1)}, u32[]{:S(2)}, u32[]{:S(2)}) async-start(f32[8,64,1280]{2,1,0:T(8,128)} %bitcast.34), calls=%async_computation | async-start | bytes 5242880 | tf_op jit(solution)/shard_map/slices/all_to_all | solution.py:416
  20.1 0.6 dynamic-slice_bitcast_fusion.1
  20.7 30.9 %all-to-all-done.got_ref = f32[8,64,1280]{2,1,0:T(8,128)S(1)} async-done(((f32[8,64,1280]{2,1,0:T(8,128)}), f32[8,64,1280]{2,1,0:T(8,128)S(1)}, u32[]{:S(2)}, u32[]{:S(2)}) %all-to-all-start) | async-done | bytes 2621472 | tf_op jit(solution)/shard_map/slices/all_to_all | solution.py:416
  51.6 1.8 slices.3
  53.4 0.3 collective-permute-start
  53.7 5.4 %all-to-all-start.1 = ((f32[8,8,1536]{2,1,0:T(8,128)}), f32[8,8,1536]{2,1,0:T(8,128)S(1)}, u32[]{:S(2)}, u32[]{:S(2)}) async-start(f32[8,8,1536]{2,1,0:T(8,128)} %bitcast.8), calls=%async_computation.1 | async-start | bytes 786432 | tf_op jit(solution)/shard_map/lead/all_to_all | solution.py:429
  59.1 8.8 %all-to-all-done.1 = f32[8,8,1536]{2,1,0:T(8,128)S(1)} async-done(((f32[8,8,1536]{2,1,0:T(8,128)}), f32[8,8,1536]{2,1,0:T(8,128)S(1)}, u32[]{:S(2)}, u32[]{:S(2)}) %all-to-all-start.1) | async-done | bytes 393248 | tf_op jit(solution)/shard_map/lead/all_to_all | solution.py:429
  67.9 0.0 collective-permute-done
  68.0 0.9 pad_maximum_fusion
  68.9 7.2 %all-to-all-start.2 = ((f32[8,16,1536]{2,1,0:T(8,128)}), f32[8,16,1536]{2,1,0:T(8,128)S(1)}, u32[]{:S(2)}, u32[]{:S(2)}) async-start(f32[8,16,1536]{2,1,0:T(8,128)} %pad_maximum_fusion), calls=%async_computation.2 | async-start | bytes 1572864 | tf_op jit(solution)/shard_map/lead/all_to_all | solution.py:436
  76.1 0.0 all-gather.7.cloned.1.call-start
  76.1 1.1 select_bitcast_fusion.1
  77.2 1.0 pad_maximum_fusion.1
  78.1 0.0 all-gather.7.cloned.1.call-update
  78.2 9.8 %all-to-all-done.2 = f32[8,16,1536]{2,1,0:T(8,128)S(1)} async-done(((f32[8,16,1536]{2,1,0:T(8,128)}), f32[8,16,1536]{2,1,0:T(8,128)S(1)}, u32[]{:S(2)}, u32[]{:S(2)}) %all-to-all-start.2) | async-done | bytes 786464 | tf_op jit(solution)/shard_map/lead/all_to_all | solution.py:436
  87.9 0.8 slice_bitcast_fusion
  88.7 0.1 broadcast_in_dim.7
  88.8 17.6 %all_to_all.30 = f32[8,64,512]{2,1,0:T(8,128)S(1)} all-to-all(f32[8,64,512]{2,1,0:T(8,128)S(1)} %broadcast_in_dim.7), channel_id=1, replica_groups=mesh['x_hi'=2,'z'=4,'y'=4,'x_lo'=2,'core'=2] {'y','x_lo'}, dimensions={0} | all-to-all | bytes 2097152 | tf_op jit(solution)/shard_map/lead/all_to_all | solution.py:379
  106.4 0.0 copy-start.1
  106.4 2.1 collective-permute-start.1
  108.5 2.4 collective-permute-done.1.other_ref.other1_ref
  110.9 1.6 broadcast_in_dim.8
  112.5 0.0 copy-done.1
  112.5 4.4 %all-to-all-start.4 = ((f32[8,64,1024]{2,1,0:T(8,128)}), f32[8,64,1024]{2,1,0:T(8,128)S(1)}, u32[]{:S(2)}, u32[]{:S(2)}) async-start(f32[8,64,1024]{2,1,0:T(8,128)} %broadcast_in_dim.8), calls=%async_computation.4 | async-start | bytes 4194304 | tf_op jit(solution)/shard_map/lead/all_to_all | solution.py:443
  116.9 0.5 all-gather.5.cloned.1.call-start
  117.4 20.2 %factor.3 = (f32[512,512]{1,0:T(8,128)}, f32[512,512]{1,0:T(8,128)}) custom-call(s32[1]{0:T(128)} %bitcast.2.odd_ref, f32[512,512]{1,0:T(8,128)} %bitcast.39, f32[512,512]{1,0:T(8,128)} %collective-permute-done.1.other_ref.other1_ref), custom_call_target="tpu_custom_call" | custom-call | flops 20000000000 | bytes 16777216 | tf_op jit(solution)/shard_map/factor/pallas_call | solution.py:204
  137.7 5.1 %all-to-all-done.4 = f32[8,64,1024]{2,1,0:T(8,128)S(1)} async-done(((f32[8,64,1024]{2,1,0:T(8,128)}), f32[8,64,1024]{2,1,0:T(8,128)S(1)}, u32[]{:S(2)}, u32[]{:S(2)}) %all-to-all-start.4) | async-done | bytes 2097184 | tf_op jit(solution)/shard_map/lead/all_to_all | solution.py:443
  142.7 0.0 copy-start
  142.7 0.0 all-gather.5.cloned.1.call-update
  142.7 1.3 collective-permute-start.2
  144.0 0.7 pad_add_fusion.place_ref
  144.7 0.6 dynamic-slice_bitcast_fusion.row_hot_ref
  145.3 0.0 copy-done
  145.3 5.7 %all-to-all-start.5 = ((f32[8,256,256]{2,1,0:T(8,128)}), f32[8,256,256]{2,1,0:T(8,128)}, u32[]{:S(2)}, u32[]{:S(2)}) async-start(f32[8,256,256]{2,1,0:T(8,128)} %bitcast.16), calls=%async_computation.5 | async-start | bytes 4194304 | tf_op jit(solution)/shard_map/exchange/all_to_all | solution.py:461
  151.0 0.0 collective-permute-done.2.other2_ref.other_ref
  151.0 24.5 %factor.4 = (f32[512,512]{1,0:T(8,128)}, f32[512,512]{1,0:T(8,128)}, f32[512,512]{1,0:T(8,128)}) custom-call(s32[1]{0:T(128)} %bitcast.2.odd_ref, f32[512,512]{1,0:T(8,128)} %bitcast.40, f32[512,512]{1,0:T(8,128)} %collective-permute-done.1.other_ref.other1_ref, f32[512,1024]{1,0:T(8,128)} %bitcast.36, ...), custom_call_target="tpu_custom_call" | custom-call | flops 20000000000 | bytes 16777216 | tf_op jit(solution)/shard_map/factor/pallas_call | solution.py:204
  175.5 0.0 all-gather.7.cloned.1.call-done
  175.5 32.9 %factor.5 = (f32[512,512]{1,0:T(8,128)}, f32[512,512]{1,0:T(8,128)}, f32[512,512]{1,0:T(8,128)}, f32[512,512]{1,0:T(8,128)}, f32[512,1536]{1,0:T(8,128)}) custom-call(s32[1]{0:T(128)} %bitcast.2.odd_ref, f32[512,1024]{1,0:T(8,128)} %bitcast.37, f32[512,1024]{1,0:T(8,128)} %collective-permute-done.2.other2_ref.other_ref, ...), custom_call_target="tpu_custom_call" | custom-call | flops 20000000000 | bytes 16777216 | tf_op jit(solution)/shard_map/factor/pallas_call | solution.py:204
  208.5 0.0 all-to-all-done.5
  208.5 0.0 all-gather.5.cloned.1.call-done
  208.5 28.5 %finish.1 = f32[1024,512]{1,0:T(8,128)} custom-call(s32[2]{0:T(128)} %pad_add_fusion.place_ref, f32[8,2,64,1536]{3,2,1,0:T(8,128)} %bitcast.42, f32[1024,512]{1,0:T(8,128)} %front_ref.1, f32[4,2,256,256]{3,2,1,0:T(8,128)} %bitcast.17.arrived_ref, s32[2,4,256]{2,1,0:T(4,128)} %dynamic-slice_bitcast_fusion.row_hot_ref, ...), custom_call_target="tpu_custom_call" | custom-call | flops 20000000000 | bytes 25165824 | tf_op jit(solution)/shard_map/finish/pallas_call | solution.py:338
  (8 shorter events, 0.1 us)
Async XLA Ops:
  12.4 39.2 %all-to-all-start = ((f32[8,64,1280]{2,1,0:T(8,128)}), f32[8,64,1280]{2,1,0:T(8,128)S(1)}, u32[]{:S(2)}, u32[]{:S(2)}) async-start(f32[8,64,1280]{2,1,0:T(8,128)} %bitcast.34), calls=%async_computation | async-start | bytes 5242880 | tf_op jit(solution)/shard_map/slices/all_to_all | solution.py:416
  53.4 14.5 %collective-permute-start = (f32[64,1536]{1,0:T(8,128)}, f32[64,1536]{1,0:T(8,128)S(1)}, u32[]{:S(2)}, u32[]{:S(2)}) collective-permute-start(f32[64,1536]{1,0:T(8,128)} %slices.3), channel_id=1, source_target_pairs={{0,64},{64,0},{1,65},{65,1},{2,66},{66,2},{3,67},{67,3},{4,68},{68... | collective-permute-start | bytes 1179656 | tf_op jit(solution)/shard_map/panel_cols/ppermute | solution.py:426
  53.7 14.2 %all-to-all-start.1 = ((f32[8,8,1536]{2,1,0:T(8,128)}), f32[8,8,1536]{2,1,0:T(8,128)S(1)}, u32[]{:S(2)}, u32[]{:S(2)}) async-start(f32[8,8,1536]{2,1,0:T(8,128)} %bitcast.8), calls=%async_computation.1 | async-start | bytes 786432 | tf_op jit(solution)/shard_map/lead/all_to_all | solution.py:429
  68.9 19.0 %all-to-all-start.2 = ((f32[8,16,1536]{2,1,0:T(8,128)}), f32[8,16,1536]{2,1,0:T(8,128)S(1)}, u32[]{:S(2)}, u32[]{:S(2)}) async-start(f32[8,16,1536]{2,1,0:T(8,128)} %pad_maximum_fusion), calls=%async_computation.2 | async-start | bytes 1572864 | tf_op jit(solution)/shard_map/lead/all_to_all | solution.py:436
  76.1 99.4 %all-gather.7.cloned.1.call-start = ((), (), s32[]{:S(2)}) async-start(), calls=%async_computation.7 | async-start | bytes 3932160 | tf_op jit(solution)/shard_map/panel_cols/all_gather | solution.py:448
  106.4 6.1 %copy-start.1 = (f32[8,64,512]{2,1,0:T(8,128)}, f32[8,64,512]{2,1,0:T(8,128)S(1)}, u32[]{:S(2)}) copy-start(f32[8,64,512]{2,1,0:T(8,128)S(1)} %all_to_all.30) | copy-start | bytes 3145732
  106.4 4.5 %collective-permute-start.1 = (f32[512,512]{1,0:T(8,128)S(1)}, f32[512,512]{1,0:T(8,128)}, u32[]{:S(2)}, u32[]{:S(2)}) collective-permute-start(f32[512,512]{1,0:T(8,128)S(1)} %bitcast.38), channel_id=1, source_target_pairs={{0,1},{1,0},{2,3},{3,2},{4,5},{5,4},{6,7},{7,6},{8,9},{9,8},{10,11... | collective-permute-start | bytes 3145736 | tf_op jit(solution)/shard_map/lead/ppermute | solution.py:399
  112.5 30.2 %all-to-all-start.4 = ((f32[8,64,1024]{2,1,0:T(8,128)}), f32[8,64,1024]{2,1,0:T(8,128)S(1)}, u32[]{:S(2)}, u32[]{:S(2)}) async-start(f32[8,64,1024]{2,1,0:T(8,128)} %broadcast_in_dim.8), calls=%async_computation.4 | async-start | bytes 4194304 | tf_op jit(solution)/shard_map/lead/all_to_all | solution.py:443
  116.9 91.6 %all-gather.5.cloned.1.call-start = ((), (), s32[]{:S(2)}) async-start(), calls=%async_computation.6 | async-start | bytes 6684672 | tf_op jit(solution)/shard_map/panel_rows/all_gather | solution.py:457
  142.7 2.6 %copy-start = (f32[8,64,1024]{2,1,0:T(8,128)}, f32[8,64,1024]{2,1,0:T(8,128)S(1)}, u32[]{:S(2)}) copy-start(f32[8,64,1024]{2,1,0:T(8,128)S(1)} %all-to-all-done.4) | copy-start | bytes 6291460
  142.7 8.3 %collective-permute-start.2 = (f32[512,1024]{1,0:T(8,128)S(1)}, f32[512,1024]{1,0:T(8,128)}, u32[]{:S(2)}, u32[]{:S(2)}) collective-permute-start(f32[512,1024]{1,0:T(8,128)S(1)} %bitcast.35), channel_id=1, source_target_pairs={{0,1},{1,0},{2,3},{3,2},{4,5},{5,4},{6,7},{7,6},{8,9},{9,8},{10,11... | collective-permute-start | bytes 6291464 | tf_op jit(solution)/shard_map/panel_rows/ppermute | solution.py:399
  145.3 63.2 %all-to-all-start.5 = ((f32[8,256,256]{2,1,0:T(8,128)}), f32[8,256,256]{2,1,0:T(8,128)}, u32[]{:S(2)}, u32[]{:S(2)}) async-start(f32[8,256,256]{2,1,0:T(8,128)} %bitcast.16), calls=%async_computation.5 | async-start | bytes 4194304 | tf_op jit(solution)/shard_map/exchange/all_to_all | solution.py:461
Sparse Core Ops, SparseCore 0:
  78.6 41.1 all-gather.6
  142.9 63.8 all-gather.4

commit v6 on v5

--- a/solution.py
+++ b/solution.py
@@ -73,8 +73,17 @@
 
 
 def mm(a, b, flip=False):
-    dims = (((1,), (1 if flip else 0,)), ((), ()))
-    return lax.dot_general(a, b, dims, precision=lax.Precision.HIGHEST, preferred_element_type=F32)
+    a_high, a_mid, a_low = (x.astype(B16) for x in split3(a))
+    b_high, b_mid, b_low = (x.astype(B16) for x in split3(b))
+    left = jnp.concatenate([a_high, a_high, a_mid, a_high, a_low, a_mid], 1)
+    right = [b_high, b_mid, b_high, b_low, b_high, b_mid]
+    if flip:
+        return nt(left, jnp.concatenate(right, 1))
+    return nn(left, jnp.concatenate(right, 0))
+
+
+def nn(a, b):
+    return lax.dot_general(a, b, (((1,), (0,)), ((), ())), preferred_element_type=F32)
 
 
 def nt(a, b):
@@ -389,11 +398,12 @@
     kid = r // group
     part = r % group
     per = cols_loc // nr
-    index = index_map.reshape(NKIDS, -1, PICK) - jnp.arange(CB // PICK, dtype=jnp.int32)[:, None] * BLOCK
+    stored = index_map.reshape(NKIDS, -1, PICK)
+    index = stored - jnp.arange(CB // PICK, dtype=jnp.int32)[:, None] * BLOCK
     odd = lax.axis_index("core").reshape(1)
 
     def pick(kid_id, rng):
-        return lax.dynamic_slice(index, (kid_id, rng, 0), (1, 1, PICK)).reshape(1, PICK)
+        return lax.dynamic_slice(stored, (kid_id, rng, 0), (1, 1, PICK)).reshape(1, PICK) - rng * BLOCK
 
     def swap(rows):
         return lax.ppermute(rows, "core", [(0, 1), (1, 0)])
@@ -452,10 +462,11 @@
         l00, w0 = factor_call(factor0, [SQUARE] * 2, [square], odd, mine1, other1)
 
     with jax.named_scope("panel_rows"):
-        w0, contrib, mine2, share = lax.optimization_barrier((w0, contrib, mine2, share))
-        other2 = swap(mine2)
+        w0, share = lax.optimization_barrier((w0, share))
         row_rows = lax.all_gather(share, COL, axis=0, tiled=False)
         row_rows = row_rows.reshape(nc // 2, 2, per, LEAD)
+        w0, contrib, mine2 = lax.optimization_barrier((w0, contrib, mine2))
+        other2 = swap(mine2)
 
     with jax.named_scope("exchange"):
         arrived = lax.all_to_all(contrib.reshape(nr, PICK, PICK), ROW, 0, 0, tiled=True)

time: 248 us -> 277 us (1.12)
  blocking collectives: 17.6 us -> 56.7 us
  waiting for transfers between devices: 57 us -> 51.8 us
  starting transfers between devices: 34.5 us -> 31.5 us
    all_to_all x0 -> x1, blocking collectives: none -> 39.2 us  [body(): mine2 = lax.all_to_all(fan, CHIP, 0, 0, tiled=True).reshape(-1, 2 * BLOCK)]
    all_to_all x1 -> x0, waiting for transfers between devices: 5.06 us -> none  [body(): mine2 = lax.all_to_all(fan, CHIP, 0, 0, tiled=True).reshape(-1, 2 * BLOCK)]
    all_to_all x1 -> x0, starting transfers between devices: 4.39 us -> none  [body(): mine2 = lax.all_to_all(fan, CHIP, 0, 0, tiled=True).reshape(-1, 2 * BLOCK)]
  transfers between devices with their start and end apart: 10 -> 9, of which waited for: 5 -> 4; matrix products, arithmetic and copies ran while one was open for 3% -> 2% of each run, Pallas kernels for 32% -> 28%
where the time goes in v6:
time: 277 us; the launch traced here: 272 us
  Pallas kernels  110 us (40%)
  blocking collectives  56.7 us (20%)
  waiting for transfers between devices  51.8 us (19%)
  starting transfers between devices  31.5 us (11%)
  between operations  13.8 us (5%)
  other arithmetic  4.94 us (2%)
  local copies, waits for them, and re-layouts  3.8 us (1%)
    pallas_call x3, Pallas kernels, factor_call(): pl.pallas_call(kernel, grid=(1,), in_specs=[SMEM] + specs, out_specs=[pl....  75.5 us
    all_to_all x1, blocking collectives, body(): mine2 = lax.all_to_all(fan, CHIP, 0, 0, tiled=True).reshape(-1, 2 * BLOCK)  39.2 us
    all_to_all x1, waiting for transfers between devices, body(): got = lax.all_to_all(outgoing.reshape(nr, per, -1), ROW, 0, 0, tiled=True)  30.8 us
    pallas_call x1, Pallas kernels, finish_call(): pl.pallas_call(finish, grid=(2,), in_specs=[SMEM, pl.BlockSpec((8, 1, BLO...  28.2 us
    all_to_all x1, blocking collectives, spread(): return lax.all_to_all(copies_of(a, count), axis, 0, 0, tiled=True)  17.6 us
    all_to_all x1, waiting for transfers between devices, body(): both = lax.all_to_all(both, ROW, 0, 0, tiled=True)  9.72 us
    all_to_all x1, waiting for transfers between devices, body(): lax.all_to_all(own_slice.reshape(nc // 2, per // (nc // 2), LEAD), CHIP,...  8.8 us
    all_to_all x1, starting transfers between devices, body(): got = lax.all_to_all(outgoing.reshape(nr, per, -1), ROW, 0, 0, tiled=True)  7.85 us
  transfers between devices with their start and end apart: 9, of which 4 were waited for; matrix products, arithmetic and copies ran while one was open for 2% of the time, Pallas kernels for 28%

profile of v6, /device:TPU:7, one launch (start us, length us, event | category | flops | bytes accessed | tf_op | source)
XLA Modules:
  0.0 272.4 jit_solution(17231589636788212426)
XLA Ops:
  6.5 1.3 subtract_bitcast_fusion
  7.8 4.3 %slices.2 = f32[512,1280]{1,0:T(8,128)} custom-call(s32[1]{0:T(128)} %bitcast.flag_ref, s32[1,256]{1,0:T(1,128)} %get-tuple-element.56.cols_ref, s32[1,256]{1,0:T(1,128)} %get-tuple-element.55.rows_ref, f32[2048,256]{1,0:T(8,128)} %contrib_ref.1, f32[1024,512]{1,0:T(8,128)} %front_ref.1), custom_call_target="tpu_custom_call" | custom-call | tf_op jit(solution)/shard_map/slices/pallas_call | solution.py:412
  12.1 0.0 copy-start.2
  12.1 7.8 %all-to-all-start = ((f32[8,64,1280]{2,1,0:T(8,128)}), f32[8,64,1280]{2,1,0:T(8,128)S(1)}, u32[]{:S(2)}, u32[]{:S(2)}) async-start(f32[8,64,1280]{2,1,0:T(8,128)} %bitcast.34), calls=%async_computation | async-start | bytes 5242880 | tf_op jit(solution)/shard_map/slices/all_to_all | solution.py:426
  20.0 0.0 copy-done.2
  20.0 0.1 broadcast_subtract_fusion
  20.1 0.6 dynamic-slice_bitcast_fusion.1
  20.7 30.8 %all-to-all-done.got_ref = f32[8,64,1280]{2,1,0:T(8,128)S(1)} async-done(((f32[8,64,1280]{2,1,0:T(8,128)}), f32[8,64,1280]{2,1,0:T(8,128)S(1)}, u32[]{:S(2)}, u32[]{:S(2)}) %all-to-all-start) | async-done | bytes 2621472 | tf_op jit(solution)/shard_map/slices/all_to_all | solution.py:426
  51.5 1.8 slices.3
  53.3 0.3 collective-permute-start
  53.6 5.4 %all-to-all-start.1 = ((f32[8,8,1536]{2,1,0:T(8,128)}), f32[8,8,1536]{2,1,0:T(8,128)S(1)}, u32[]{:S(2)}, u32[]{:S(2)}) async-start(f32[8,8,1536]{2,1,0:T(8,128)} %bitcast.8), calls=%async_computation.1 | async-start | bytes 786432 | tf_op jit(solution)/shard_map/lead/all_to_all | solution.py:439
  59.0 8.8 %all-to-all-done.1 = f32[8,8,1536]{2,1,0:T(8,128)S(1)} async-done(((f32[8,8,1536]{2,1,0:T(8,128)}), f32[8,8,1536]{2,1,0:T(8,128)S(1)}, u32[]{:S(2)}, u32[]{:S(2)}) %all-to-all-start.1) | async-done | bytes 393248 | tf_op jit(solution)/shard_map/lead/all_to_all | solution.py:439
  67.8 0.0 collective-permute-done
  67.9 0.9 pad_maximum_fusion
  68.8 7.2 %all-to-all-start.2 = ((f32[8,16,1536]{2,1,0:T(8,128)}), f32[8,16,1536]{2,1,0:T(8,128)S(1)}, u32[]{:S(2)}, u32[]{:S(2)}) async-start(f32[8,16,1536]{2,1,0:T(8,128)} %pad_maximum_fusion), calls=%async_computation.2 | async-start | bytes 1572864 | tf_op jit(solution)/shard_map/lead/all_to_all | solution.py:446
  76.0 0.0 all-gather.7.cloned.1.call-start
  76.0 1.1 select_bitcast_fusion.1
  77.1 1.0 pad_maximum_fusion.1
  78.0 0.0 all-gather.7.cloned.1.call-update
  78.0 0.0 all-gather.5.cloned.1.call-start
  78.1 9.7 %all-to-all-done.2 = f32[8,16,1536]{2,1,0:T(8,128)S(1)} async-done(((f32[8,16,1536]{2,1,0:T(8,128)}), f32[8,16,1536]{2,1,0:T(8,128)S(1)}, u32[]{:S(2)}, u32[]{:S(2)}) %all-to-all-start.2) | async-done | bytes 786464 | tf_op jit(solution)/shard_map/lead/all_to_all | solution.py:446
  87.8 0.8 slice_bitcast_fusion
  88.6 0.1 broadcast_in_dim.7
  88.7 17.6 %all_to_all.30 = f32[8,64,512]{2,1,0:T(8,128)S(1)} all-to-all(f32[8,64,512]{2,1,0:T(8,128)S(1)} %broadcast_in_dim.7), channel_id=1, replica_groups=mesh['x_hi'=2,'z'=4,'y'=4,'x_lo'=2,'core'=2] {'y','x_lo'}, dimensions={0} | all-to-all | bytes 2097152 | tf_op jit(solution)/shard_map/lead/all_to_all | solution.py:388
  106.3 0.0 copy-start.1
  106.3 2.5 collective-permute-start.1
  108.9 2.4 collective-permute-done.1.other_ref.other1_ref
  111.3 0.2 broadcast_in_dim.8
  111.5 0.0 copy-done.1
  111.5 19.8 %factor.3 = (f32[512,512]{1,0:T(8,128)}, f32[512,512]{1,0:T(8,128)}) custom-call(s32[1]{0:T(128)} %bitcast.2.odd_ref, f32[512,512]{1,0:T(8,128)} %bitcast.37, f32[512,512]{1,0:T(8,128)} %collective-permute-done.1.other_ref.other1_ref), custom_call_target="tpu_custom_call" | custom-call | flops 20000000000 | bytes 16777216 | tf_op jit(solution)/shard_map/factor/pallas_call | solution.py:213
  131.3 0.0 all-gather.5.cloned.1.call-update
  131.4 39.2 %all_to_all.31 = f32[8,64,1024]{2,1,0:T(8,128)} all-to-all(f32[8,64,1024]{2,1,0:T(8,128)S(1)} %broadcast_in_dim.8), channel_id=1, replica_groups=mesh['x_hi'=2,'z'=4,'y'=4,'x_lo'=2,'core'=2] {'y','x_lo'}, dimensions={0} | all-to-all | bytes 4194304 | tf_op jit(solution)/shard_map/lead/all_to_all | solution.py:453
  170.5 3.0 %collective-permute-start.2 = (f32[512,1024]{1,0:T(8,128)}, f32[512,1024]{1,0:T(8,128)}, u32[]{:S(2)}, u32[]{:S(2)}) collective-permute-start(f32[512,1024]{1,0:T(8,128)} %bitcast.15.mine2_ref.mine_ref), channel_id=1, source_target_pairs={{0,1},{1,0},{2,3},{3,2},{4,5},{5,4},{6,7},{7,6},{8,9},{9,8},{10,11... | collective-permute-start | bytes 6291464 | tf_op jit(solution)/shard_map/panel_rows/ppermute | solution.py:409
  173.6 0.6 pad_add_fusion.place_ref
  174.1 0.6 dynamic-slice_bitcast_fusion.row_hot_ref
  174.7 5.2 %all-to-all-start.5 = ((f32[8,256,256]{2,1,0:T(8,128)}), f32[8,256,256]{2,1,0:T(8,128)S(1)}, u32[]{:S(2)}, u32[]{:S(2)}) async-start(f32[8,256,256]{2,1,0:T(8,128)} %bitcast.16), calls=%async_computation.5 | async-start | bytes 4194304 | tf_op jit(solution)/shard_map/exchange/all_to_all | solution.py:472
  180.0 0.0 collective-permute-done.2.other2_ref.other_ref
  180.0 23.6 %factor.4 = (f32[512,512]{1,0:T(8,128)}, f32[512,512]{1,0:T(8,128)}, f32[512,512]{1,0:T(8,128)}) custom-call(s32[1]{0:T(128)} %bitcast.2.odd_ref, f32[512,512]{1,0:T(8,128)} %bitcast.38, f32[512,512]{1,0:T(8,128)} %collective-permute-done.1.other_ref.other1_ref, f32[512,1024]{1,0:T(8,128)} %bitcast.15.mine2_ref.mine_ref, ...), custom_call_target="tpu_custom_call" | custom-call | flops 20000000000 | bytes 16777216 | tf_op jit(solution)/shard_map/factor/pallas_call | solution.py:213
  203.6 0.0 all-gather.7.cloned.1.call-done
  203.6 32.1 %factor.5 = (f32[512,512]{1,0:T(8,128)}, f32[512,512]{1,0:T(8,128)}, f32[512,512]{1,0:T(8,128)}, f32[512,512]{1,0:T(8,128)}, f32[512,1536]{1,0:T(8,128)}) custom-call(s32[1]{0:T(128)} %bitcast.2.odd_ref, f32[512,1024]{1,0:T(8,128)} %bitcast.15.mine2_ref.mine_ref, f32[512,1024]{1,0:T(8,128)} %collective-permute-done.2.other2_ref.other_ref, ...), custom_call_target="tpu_custom_call" | custom-call | flops 20000000000 | bytes 16777216 | tf_op jit(solution)/shard_map/factor/pallas_call | solution.py:213
  235.7 0.0 all-to-all-done.5
  235.7 0.0 copy-start
  235.7 0.0 all-gather.5.cloned.1.call-done
  235.7 1.4 copy-done
  237.1 28.2 %finish.1 = f32[1024,512]{1,0:T(8,128)} custom-call(s32[2]{0:T(128)} %pad_add_fusion.place_ref, f32[8,2,64,1536]{3,2,1,0:T(8,128)} %bitcast.41, f32[1024,512]{1,0:T(8,128)} %front_ref.1, f32[4,2,256,256]{3,2,1,0:T(8,128)} %bitcast.35, s32[2,4,256]{2,1,0:T(4,128)} %dynamic-slice_bitcast_fusion.row_hot_ref, s32[4,256]{1,0:T(4,128)} %get-tuple-element.53.col_hot_ref, ...), custom_call_target="tpu_custom_call" | custom-call | flops 20000000000 | bytes 25165824 | tf_op jit(solution)/shard_map/finish/pallas_call | solution.py:347
  (8 shorter events, 0.1 us)
Async XLA Ops:
  12.1 7.9 %copy-start.2 = (s32[4,4096]{1,0:T(4,128)S(1)}, s32[4,4096]{1,0:T(4,128)}, u32[]{:S(2)}) copy-start(s32[4,4096]{1,0:T(4,128)} %param.5) | copy-start | bytes 196612
  12.1 39.3 %all-to-all-start = ((f32[8,64,1280]{2,1,0:T(8,128)}), f32[8,64,1280]{2,1,0:T(8,128)S(1)}, u32[]{:S(2)}, u32[]{:S(2)}) async-start(f32[8,64,1280]{2,1,0:T(8,128)} %bitcast.34), calls=%async_computation | async-start | bytes 5242880 | tf_op jit(solution)/shard_map/slices/all_to_all | solution.py:426
  53.3 14.5 %collective-permute-start = (f32[64,1536]{1,0:T(8,128)}, f32[64,1536]{1,0:T(8,128)S(1)}, u32[]{:S(2)}, u32[]{:S(2)}) collective-permute-start(f32[64,1536]{1,0:T(8,128)} %slices.3), channel_id=1, source_target_pairs={{0,64},{64,0},{1,65},{65,1},{2,66},{66,2},{3,67},{67,3},{4,68},{68... | collective-permute-start | bytes 1179656 | tf_op jit(solution)/shard_map/panel_cols/ppermute | solution.py:436
  53.6 14.2 %all-to-all-start.1 = ((f32[8,8,1536]{2,1,0:T(8,128)}), f32[8,8,1536]{2,1,0:T(8,128)S(1)}, u32[]{:S(2)}, u32[]{:S(2)}) async-start(f32[8,8,1536]{2,1,0:T(8,128)} %bitcast.8), calls=%async_computation.1 | async-start | bytes 786432 | tf_op jit(solution)/shard_map/lead/all_to_all | solution.py:439
  68.8 19.0 %all-to-all-start.2 = ((f32[8,16,1536]{2,1,0:T(8,128)}), f32[8,16,1536]{2,1,0:T(8,128)S(1)}, u32[]{:S(2)}, u32[]{:S(2)}) async-start(f32[8,16,1536]{2,1,0:T(8,128)} %pad_maximum_fusion), calls=%async_computation.2 | async-start | bytes 1572864 | tf_op jit(solution)/shard_map/lead/all_to_all | solution.py:446
  76.0 127.6 %all-gather.7.cloned.1.call-start = ((), (), s32[]{:S(2)}) async-start(), calls=%async_computation.7 | async-start | bytes 3932160 | tf_op jit(solution)/shard_map/panel_cols/all_gather | solution.py:458
  78.0 157.7 %all-gather.5.cloned.1.call-start = ((), (), s32[]{:S(2)}) async-start(), calls=%async_computation.6 | async-start | bytes 6684672 | tf_op jit(solution)/shard_map/panel_rows/all_gather | solution.py:466
  106.3 5.2 %copy-start.1 = (f32[8,64,512]{2,1,0:T(8,128)}, f32[8,64,512]{2,1,0:T(8,128)S(1)}, u32[]{:S(2)}) copy-start(f32[8,64,512]{2,1,0:T(8,128)S(1)} %all_to_all.30) | copy-start | bytes 3145732
  106.3 4.9 %collective-permute-start.1 = (f32[512,512]{1,0:T(8,128)S(1)}, f32[512,512]{1,0:T(8,128)}, u32[]{:S(2)}, u32[]{:S(2)}) collective-permute-start(f32[512,512]{1,0:T(8,128)S(1)} %bitcast.36), channel_id=1, source_target_pairs={{0,1},{1,0},{2,3},{3,2},{4,5},{5,4},{6,7},{7,6},{8,9},{9,8},{10,11... | collective-permute-start | bytes 3145736 | tf_op jit(solution)/shard_map/lead/ppermute | solution.py:409
  170.5 9.4 %collective-permute-start.2 = (f32[512,1024]{1,0:T(8,128)}, f32[512,1024]{1,0:T(8,128)}, u32[]{:S(2)}, u32[]{:S(2)}) collective-permute-start(f32[512,1024]{1,0:T(8,128)} %bitcast.15.mine2_ref.mine_ref), channel_id=1, source_target_pairs={{0,1},{1,0},{2,3},{3,2},{4,5},{5,4},{6,7},{7,6},{8,9},{9,8},{10,11... | collective-permute-start | bytes 6291464 | tf_op jit(solution)/shard_map/panel_rows/ppermute | solution.py:409
  174.7 61.0 %all-to-all-start.5 = ((f32[8,256,256]{2,1,0:T(8,128)}), f32[8,256,256]{2,1,0:T(8,128)S(1)}, u32[]{:S(2)}, u32[]{:S(2)}) async-start(f32[8,256,256]{2,1,0:T(8,128)} %bitcast.16), calls=%async_computation.5 | async-start | bytes 4194304 | tf_op jit(solution)/shard_map/exchange/all_to_all | solution.py:472
  235.7 1.4 copy-start
Sparse Core Ops, SparseCore 0:
  78.5 41.1 all-gather.6
  131.5 63.2 all-gather.4

commit v7 on v6

--- a/solution.py
+++ b/solution.py
@@ -462,11 +462,10 @@
         l00, w0 = factor_call(factor0, [SQUARE] * 2, [square], odd, mine1, other1)
 
     with jax.named_scope("panel_rows"):
-        w0, share = lax.optimization_barrier((w0, share))
+        w0, contrib, mine2, share = lax.optimization_barrier((w0, contrib, mine2, share))
+        other2 = swap(mine2)
         row_rows = lax.all_gather(share, COL, axis=0, tiled=False)
         row_rows = row_rows.reshape(nc // 2, 2, per, LEAD)
-        w0, contrib, mine2 = lax.optimization_barrier((w0, contrib, mine2))
-        other2 = swap(mine2)
 
     with jax.named_scope("exchange"):
         arrived = lax.all_to_all(contrib.reshape(nr, PICK, PICK), ROW, 0, 0, tiled=True)

time: 277 us -> 246 us (0.89)
  blocking collectives: 56.7 us -> 17.6 us
  waiting for transfers between devices: 51.8 us -> 57.4 us
  starting transfers between devices: 31.5 us -> 34.6 us
    all_to_all x1 -> x0, blocking collectives: 39.2 us -> none  [body(): mine2 = lax.all_to_all(fan, CHIP, 0, 0, tiled=True).reshape(-1, 2 * BLOCK)]
    all_to_all x0 -> x1, waiting for transfers between devices: none -> 5.56 us  [body(): mine2 = lax.all_to_all(fan, CHIP, 0, 0, tiled=True).reshape(-1, 2 * BLOCK)]
    all_to_all x0 -> x1, starting transfers between devices: none -> 4.39 us  [body(): mine2 = lax.all_to_all(fan, CHIP, 0, 0, tiled=True).reshape(-1, 2 * BLOCK)]
  transfers between devices with their start and end apart: 9 -> 10, of which waited for: 4 -> 5; matrix products, arithmetic and copies ran while one was open for 2% -> 3% of each run, Pallas kernels for 28% -> 31%
where the time goes in v7:
time: 246 us; the launch traced here: 242 us
  Pallas kernels  110 us (45%)
  waiting for transfers between devices  57.4 us (23%)
  starting transfers between devices  34.6 us (14%)
  blocking collectives  17.6 us (7%)
  between operations  13.7 us (6%)
  other arithmetic  4.95 us (2%)
  local copies, waits for them, and re-layouts  3.78 us (2%)
    pallas_call x3, Pallas kernels, factor_call(): pl.pallas_call(kernel, grid=(1,), in_specs=[SMEM] + specs, out_specs=[pl....  75.7 us
    all_to_all x1, waiting for transfers between devices, body(): got = lax.all_to_all(outgoing.reshape(nr, per, -1), ROW, 0, 0, tiled=True)  30.8 us
    pallas_call x1, Pallas kernels, finish_call(): pl.pallas_call(finish, grid=(2,), in_specs=[SMEM, pl.BlockSpec((8, 1, BLO...  28.3 us
    all_to_all x1, blocking collectives, spread(): return lax.all_to_all(copies_of(a, count), axis, 0, 0, tiled=True)  17.6 us
    all_to_all x1, waiting for transfers between devices, body(): both = lax.all_to_all(both, ROW, 0, 0, tiled=True)  9.76 us
    all_to_all x1, waiting for transfers between devices, body(): lax.all_to_all(own_slice.reshape(nc // 2, per // (nc // 2), LEAD), CHIP,...  8.81 us
    all_to_all x1, starting transfers between devices, body(): got = lax.all_to_all(outgoing.reshape(nr, per, -1), ROW, 0, 0, tiled=True)  7.85 us
    all_to_all x1, starting transfers between devices, body(): both = lax.all_to_all(both, ROW, 0, 0, tiled=True)  7.17 us
  transfers between devices with their start and end apart: 10, of which 5 were waited for; matrix products, arithmetic and copies ran while one was open for 3% of the time, Pallas kernels for 31%

profile of v7, /device:TPU:7, one launch (start us, length us, event | category | flops | bytes accessed | tf_op | source)
XLA Modules:
  0.0 242.2 jit_solution(2804588286600937510)
XLA Ops:
  6.5 1.3 subtract_bitcast_fusion
  7.8 4.3 %slices.2 = f32[512,1280]{1,0:T(8,128)} custom-call(s32[1]{0:T(128)} %bitcast.flag_ref, s32[1,256]{1,0:T(1,128)} %get-tuple-element.54.cols_ref, s32[1,256]{1,0:T(1,128)} %get-tuple-element.53.rows_ref, f32[2048,256]{1,0:T(8,128)} %contrib_ref.1, f32[1024,512]{1,0:T(8,128)} %front_ref.1), custom_call_target="tpu_custom_call" | custom-call | tf_op jit(solution)/shard_map/slices/pallas_call | solution.py:412
  12.2 0.0 copy-start.2
  12.2 7.8 %all-to-all-start = ((f32[8,64,1280]{2,1,0:T(8,128)}), f32[8,64,1280]{2,1,0:T(8,128)S(1)}, u32[]{:S(2)}, u32[]{:S(2)}) async-start(f32[8,64,1280]{2,1,0:T(8,128)} %bitcast.34), calls=%async_computation | async-start | bytes 5242880 | tf_op jit(solution)/shard_map/slices/all_to_all | solution.py:426
  20.0 0.0 copy-done.2
  20.0 0.1 broadcast_subtract_fusion
  20.1 0.6 dynamic-slice_bitcast_fusion.1
  20.7 30.8 %all-to-all-done.got_ref = f32[8,64,1280]{2,1,0:T(8,128)S(1)} async-done(((f32[8,64,1280]{2,1,0:T(8,128)}), f32[8,64,1280]{2,1,0:T(8,128)S(1)}, u32[]{:S(2)}, u32[]{:S(2)}) %all-to-all-start) | async-done | bytes 2621472 | tf_op jit(solution)/shard_map/slices/all_to_all | solution.py:426
  51.5 1.8 slices.3
  53.3 0.3 collective-permute-start
  53.6 5.4 %all-to-all-start.1 = ((f32[8,8,1536]{2,1,0:T(8,128)}), f32[8,8,1536]{2,1,0:T(8,128)S(1)}, u32[]{:S(2)}, u32[]{:S(2)}) async-start(f32[8,8,1536]{2,1,0:T(8,128)} %bitcast.8), calls=%async_computation.1 | async-start | bytes 786432 | tf_op jit(solution)/shard_map/lead/all_to_all | solution.py:439
  59.0 8.8 %all-to-all-done.1 = f32[8,8,1536]{2,1,0:T(8,128)S(1)} async-done(((f32[8,8,1536]{2,1,0:T(8,128)}), f32[8,8,1536]{2,1,0:T(8,128)S(1)}, u32[]{:S(2)}, u32[]{:S(2)}) %all-to-all-start.1) | async-done | bytes 393248 | tf_op jit(solution)/shard_map/lead/all_to_all | solution.py:439
  67.8 0.0 collective-permute-done
  67.9 0.9 pad_maximum_fusion
  68.8 7.2 %all-to-all-start.2 = ((f32[8,16,1536]{2,1,0:T(8,128)}), f32[8,16,1536]{2,1,0:T(8,128)S(1)}, u32[]{:S(2)}, u32[]{:S(2)}) async-start(f32[8,16,1536]{2,1,0:T(8,128)} %pad_maximum_fusion), calls=%async_computation.2 | async-start | bytes 1572864 | tf_op jit(solution)/shard_map/lead/all_to_all | solution.py:446
  76.0 0.0 all-gather.7.cloned.1.call-start
  76.0 1.1 select_bitcast_fusion.1
  77.1 1.0 pad_maximum_fusion.1
  78.0 0.0 all-gather.7.cloned.1.call-update
  78.1 9.8 %all-to-all-done.2 = f32[8,16,1536]{2,1,0:T(8,128)S(1)} async-done(((f32[8,16,1536]{2,1,0:T(8,128)}), f32[8,16,1536]{2,1,0:T(8,128)S(1)}, u32[]{:S(2)}, u32[]{:S(2)}) %all-to-all-start.2) | async-done | bytes 786464 | tf_op jit(solution)/shard_map/lead/all_to_all | solution.py:446
  87.8 0.8 slice_bitcast_fusion
  88.6 0.1 broadcast_in_dim.7
  88.8 17.6 %all_to_all.30 = f32[8,64,512]{2,1,0:T(8,128)S(1)} all-to-all(f32[8,64,512]{2,1,0:T(8,128)S(1)} %broadcast_in_dim.7), channel_id=1, replica_groups=mesh['x_hi'=2,'z'=4,'y'=4,'x_lo'=2,'core'=2] {'y','x_lo'}, dimensions={0} | all-to-all | bytes 2097152 | tf_op jit(solution)/shard_map/lead/all_to_all | solution.py:388
  106.3 0.0 copy-start.1
  106.3 2.1 collective-permute-start.1
  108.4 2.4 collective-permute-done.1.other_ref.other1_ref
  110.8 1.6 broadcast_in_dim.8
  112.4 0.0 copy-done.1
  112.4 4.4 %all-to-all-start.4 = ((f32[8,64,1024]{2,1,0:T(8,128)}), f32[8,64,1024]{2,1,0:T(8,128)S(1)}, u32[]{:S(2)}, u32[]{:S(2)}) async-start(f32[8,64,1024]{2,1,0:T(8,128)} %broadcast_in_dim.8), calls=%async_computation.4 | async-start | bytes 4194304 | tf_op jit(solution)/shard_map/lead/all_to_all | solution.py:453
  116.8 0.5 all-gather.5.cloned.1.call-start
  117.3 19.8 %factor.3 = (f32[512,512]{1,0:T(8,128)}, f32[512,512]{1,0:T(8,128)}) custom-call(s32[1]{0:T(128)} %bitcast.2.odd_ref, f32[512,512]{1,0:T(8,128)} %bitcast.39, f32[512,512]{1,0:T(8,128)} %collective-permute-done.1.other_ref.other1_ref), custom_call_target="tpu_custom_call" | custom-call | flops 20000000000 | bytes 16777216 | tf_op jit(solution)/shard_map/factor/pallas_call | solution.py:213
  137.1 5.6 %all-to-all-done.4 = f32[8,64,1024]{2,1,0:T(8,128)S(1)} async-done(((f32[8,64,1024]{2,1,0:T(8,128)}), f32[8,64,1024]{2,1,0:T(8,128)S(1)}, u32[]{:S(2)}, u32[]{:S(2)}) %all-to-all-start.4) | async-done | bytes 2097184 | tf_op jit(solution)/shard_map/lead/all_to_all | solution.py:453
  142.6 0.0 copy-start
  142.6 0.0 all-gather.5.cloned.1.call-update
  142.7 1.3 collective-permute-start.2
  144.0 0.6 pad_add_fusion.place_ref
  144.5 0.6 dynamic-slice_bitcast_fusion.row_hot_ref
  145.1 0.0 copy-done
  145.1 5.7 %all-to-all-start.5 = ((f32[8,256,256]{2,1,0:T(8,128)}), f32[8,256,256]{2,1,0:T(8,128)}, u32[]{:S(2)}, u32[]{:S(2)}) async-start(f32[8,256,256]{2,1,0:T(8,128)} %bitcast.16), calls=%async_computation.5 | async-start | bytes 4194304 | tf_op jit(solution)/shard_map/exchange/all_to_all | solution.py:471
  150.9 0.0 collective-permute-done.2.other2_ref.other_ref
  150.9 23.7 %factor.4 = (f32[512,512]{1,0:T(8,128)}, f32[512,512]{1,0:T(8,128)}, f32[512,512]{1,0:T(8,128)}) custom-call(s32[1]{0:T(128)} %bitcast.2.odd_ref, f32[512,512]{1,0:T(8,128)} %bitcast.40, f32[512,512]{1,0:T(8,128)} %collective-permute-done.1.other_ref.other1_ref, f32[512,1024]{1,0:T(8,128)} %bitcast.36, ...), custom_call_target="tpu_custom_call" | custom-call | flops 20000000000 | bytes 16777216 | tf_op jit(solution)/shard_map/factor/pallas_call | solution.py:213
  174.6 0.0 all-gather.7.cloned.1.call-done
  174.6 32.2 %factor.5 = (f32[512,512]{1,0:T(8,128)}, f32[512,512]{1,0:T(8,128)}, f32[512,512]{1,0:T(8,128)}, f32[512,512]{1,0:T(8,128)}, f32[512,1536]{1,0:T(8,128)}) custom-call(s32[1]{0:T(128)} %bitcast.2.odd_ref, f32[512,1024]{1,0:T(8,128)} %bitcast.37, f32[512,1024]{1,0:T(8,128)} %collective-permute-done.2.other2_ref.other_ref, ...), custom_call_target="tpu_custom_call" | custom-call | flops 20000000000 | bytes 16777216 | tf_op jit(solution)/shard_map/factor/pallas_call | solution.py:213
  206.8 0.0 all-to-all-done.5
  206.8 0.0 all-gather.5.cloned.1.call-done
  206.9 28.3 %finish.1 = f32[1024,512]{1,0:T(8,128)} custom-call(s32[2]{0:T(128)} %pad_add_fusion.place_ref, f32[8,2,64,1536]{3,2,1,0:T(8,128)} %bitcast.43, f32[1024,512]{1,0:T(8,128)} %front_ref.1, f32[4,2,256,256]{3,2,1,0:T(8,128)} %bitcast.17.arrived_ref, s32[2,4,256]{2,1,0:T(4,128)} %dynamic-slice_bitcast_fusion.row_hot_ref, ...), custom_call_target="tpu_custom_call" | custom-call | flops 20000000000 | bytes 25165824 | tf_op jit(solution)/shard_map/finish/pallas_call | solution.py:347
  (8 shorter events, 0.1 us)
Async XLA Ops:
  12.2 7.9 %copy-start.2 = (s32[4,4096]{1,0:T(4,128)S(1)}, s32[4,4096]{1,0:T(4,128)}, u32[]{:S(2)}) copy-start(s32[4,4096]{1,0:T(4,128)} %param.5) | copy-start | bytes 196612
  12.2 39.3 %all-to-all-start = ((f32[8,64,1280]{2,1,0:T(8,128)}), f32[8,64,1280]{2,1,0:T(8,128)S(1)}, u32[]{:S(2)}, u32[]{:S(2)}) async-start(f32[8,64,1280]{2,1,0:T(8,128)} %bitcast.34), calls=%async_computation | async-start | bytes 5242880 | tf_op jit(solution)/shard_map/slices/all_to_all | solution.py:426
  53.3 14.5 %collective-permute-start = (f32[64,1536]{1,0:T(8,128)}, f32[64,1536]{1,0:T(8,128)S(1)}, u32[]{:S(2)}, u32[]{:S(2)}) collective-permute-start(f32[64,1536]{1,0:T(8,128)} %slices.3), channel_id=1, source_target_pairs={{0,64},{64,0},{1,65},{65,1},{2,66},{66,2},{3,67},{67,3},{4,68},{68... | collective-permute-start | bytes 1179656 | tf_op jit(solution)/shard_map/panel_cols/ppermute | solution.py:436
  53.6 14.2 %all-to-all-start.1 = ((f32[8,8,1536]{2,1,0:T(8,128)}), f32[8,8,1536]{2,1,0:T(8,128)S(1)}, u32[]{:S(2)}, u32[]{:S(2)}) async-start(f32[8,8,1536]{2,1,0:T(8,128)} %bitcast.8), calls=%async_computation.1 | async-start | bytes 786432 | tf_op jit(solution)/shard_map/lead/all_to_all | solution.py:439
  68.8 19.0 %all-to-all-start.2 = ((f32[8,16,1536]{2,1,0:T(8,128)}), f32[8,16,1536]{2,1,0:T(8,128)S(1)}, u32[]{:S(2)}, u32[]{:S(2)}) async-start(f32[8,16,1536]{2,1,0:T(8,128)} %pad_maximum_fusion), calls=%async_computation.2 | async-start | bytes 1572864 | tf_op jit(solution)/shard_map/lead/all_to_all | solution.py:446
  76.0 98.6 %all-gather.7.cloned.1.call-start = ((), (), s32[]{:S(2)}) async-start(), calls=%async_computation.7 | async-start | bytes 3932160 | tf_op jit(solution)/shard_map/panel_cols/all_gather | solution.py:458
  106.3 6.1 %copy-start.1 = (f32[8,64,512]{2,1,0:T(8,128)}, f32[8,64,512]{2,1,0:T(8,128)S(1)}, u32[]{:S(2)}) copy-start(f32[8,64,512]{2,1,0:T(8,128)S(1)} %all_to_all.30) | copy-start | bytes 3145732
  106.3 4.5 %collective-permute-start.1 = (f32[512,512]{1,0:T(8,128)S(1)}, f32[512,512]{1,0:T(8,128)}, u32[]{:S(2)}, u32[]{:S(2)}) collective-permute-start(f32[512,512]{1,0:T(8,128)S(1)} %bitcast.38), channel_id=1, source_target_pairs={{0,1},{1,0},{2,3},{3,2},{4,5},{5,4},{6,7},{7,6},{8,9},{9,8},{10,11... | collective-permute-start | bytes 3145736 | tf_op jit(solution)/shard_map/lead/ppermute | solution.py:409
  112.4 30.2 %all-to-all-start.4 = ((f32[8,64,1024]{2,1,0:T(8,128)}), f32[8,64,1024]{2,1,0:T(8,128)S(1)}, u32[]{:S(2)}, u32[]{:S(2)}) async-start(f32[8,64,1024]{2,1,0:T(8,128)} %broadcast_in_dim.8), calls=%async_computation.4 | async-start | bytes 4194304 | tf_op jit(solution)/shard_map/lead/all_to_all | solution.py:453
  116.8 90.1 %all-gather.5.cloned.1.call-start = ((), (), s32[]{:S(2)}) async-start(), calls=%async_computation.6 | async-start | bytes 6684672 | tf_op jit(solution)/shard_map/panel_rows/all_gather | solution.py:467
  142.6 2.5 %copy-start = (f32[8,64,1024]{2,1,0:T(8,128)}, f32[8,64,1024]{2,1,0:T(8,128)S(1)}, u32[]{:S(2)}) copy-start(f32[8,64,1024]{2,1,0:T(8,128)S(1)} %all-to-all-done.4) | copy-start | bytes 6291460
  142.7 8.2 %collective-permute-start.2 = (f32[512,1024]{1,0:T(8,128)S(1)}, f32[512,1024]{1,0:T(8,128)}, u32[]{:S(2)}, u32[]{:S(2)}) collective-permute-start(f32[512,1024]{1,0:T(8,128)S(1)} %bitcast.35), channel_id=1, source_target_pairs={{0,1},{1,0},{2,3},{3,2},{4,5},{5,4},{6,7},{7,6},{8,9},{9,8},{10,11... | collective-permute-start | bytes 6291464 | tf_op jit(solution)/shard_map/panel_rows/ppermute | solution.py:409
  145.1 61.7 %all-to-all-start.5 = ((f32[8,256,256]{2,1,0:T(8,128)}), f32[8,256,256]{2,1,0:T(8,128)}, u32[]{:S(2)}, u32[]{:S(2)}) async-start(f32[8,256,256]{2,1,0:T(8,128)} %bitcast.16), calls=%async_computation.5 | async-start | bytes 4194304 | tf_op jit(solution)/shard_map/exchange/all_to_all | solution.py:471
Sparse Core Ops, SparseCore 0:
  78.5 41.1 all-gather.6
  142.8 63.8 all-gather.4
